TPU v7x, 32 devices: a whole 2x2x4 slice. The times are simulated.
32 devices in a mesh: dp: 8 (over z, y), mp: 4 (over x, core).
Axes of the slice: x: 2, y: 2, z: 4, core: 2. Of those that a mesh axis runs over, the one named last changes fastest.
Arguments:
- tokens: bfloat16 [8192, 2048], P(('dp', 'mp')), may hold values from -6 to 6
- layer_vectors: bfloat16 [8192, 256], P(('dp', 'mp')), may hold values from -6 to 6
- segment_ids: int32 [8192], P('dp'), may hold values from 0 to 23, as said below
- cotangent: bfloat16 [8192, 2048], P(('dp', 'mp')), may hold values from -6 to 6
- norm_gains: bfloat16 [6, 2048], P(None, ('dp', 'mp')), may hold values from 0.099609375 to 1.8984375
- head_gains: bfloat16 [512], P(('dp', 'mp')), may hold values from 1 to 2
- w_query: bfloat16 [2048, 2048], P('dp', 'mp'), may hold values from -0.125 to 0.125
- w_key: bfloat16 [2048, 512], P(('dp', 'mp')), may hold values from -0.125 to 0.125
- w_value: bfloat16 [2048, 512], P(('dp', 'mp')), may hold values from -0.125 to 0.125
- w_out: bfloat16 [2048, 2048], P('mp', 'dp'), may hold values from -0.125 to 0.125
- w_left: bfloat16 [2048, 64], P(('dp', 'mp')), may hold values from -0.125 to 0.125
- w_right: bfloat16 [64, 2048], P(None, ('dp', 'mp')), may hold values from -0.75 to 0.75
- w_gate: bfloat16 [2048, 8192], P('dp', 'mp'), may hold values from -0.125 to 0.125
- w_up: bfloat16 [2048, 8192], P('dp', 'mp'), may hold values from -0.125 to 0.125
- w_down: bfloat16 [8192, 2048], P('mp', 'dp'), may hold values from -0.0625 to 0.0625
- w_layer_gate: bfloat16 [2048, 256], P(('dp', 'mp')), may hold values from -0.125 to 0.125
- w_layer_proj: bfloat16 [256, 2048], P(None, ('dp', 'mp')), may hold values from -0.375 to 0.375
Outputs:
- output: bfloat16 [8192, 2048], P(('dp', 'mp'))
- grad_tokens: bfloat16 [8192, 2048], P(('dp', 'mp'))
- grad_layer_vectors: bfloat16 [8192, 256], P(('dp', 'mp'))
- grad_norm_gains: float32 [6, 2048], P(None, ('dp', 'mp'))
- grad_head_gains: float32 [512], P(('dp', 'mp'))
- grad_w_query: float32 [2048, 2048], P('dp', 'mp')
- grad_w_key: float32 [2048, 512], P(('dp', 'mp'))
- grad_w_value: float32 [2048, 512], P(('dp', 'mp'))
- grad_w_out: float32 [2048, 2048], P('mp', 'dp')
- grad_w_left: float32 [2048, 64], P(('dp', 'mp'))
- grad_w_right: float32 [64, 2048], P(None, ('dp', 'mp'))
- grad_w_gate: float32 [2048, 8192], P('dp', 'mp')
- grad_w_up: float32 [2048, 8192], P('dp', 'mp')
- grad_w_down: float32 [8192, 2048], P('mp', 'dp')
- grad_w_layer_gate: float32 [2048, 256], P(('dp', 'mp'))
- grad_w_layer_proj: float32 [256, 2048], P(None, ('dp', 'mp'))
Inputs may be any that keep to these rules, and one draw needn't show every extreme that they name: `segment_ids`: Sorted; the 1024 tokens of sequence s hold documents 3 s, 3 s + 1 and 3 s + 2 in that order; the first and the last document have 256 - 256 // 4 to 255 tokens each.
All inputs are finite; a program needn't handle non-finite values.
Results may differ from a plain program's by a relative error of at most 0.024.
Values may be sent and summed in bfloat16 or wider, within the bound.
No kernel may reach another device: no remote copies, remote signals or barrier semaphores. Data moves between devices by JAX's collectives and lax.ppermute only.
A program may use at most 192 MiB of HBM per device.

v0:
```python
import math

import jax
import jax.numpy as jnp
from jax import lax
from jax.sharding import PartitionSpec as P

KV_HEADS = 2
HEAD_DIM = 256
WINDOW = 512


epsilon = 1e-06
root_half = 1.0 / math.sqrt(2.0)
masked_score = -1e30


def rms_norm(values, scales):
    return values * lax.rsqrt(jnp.mean(values * values, axis=-1, keepdims=True) + epsilon) * scales


def plain_norm(values):
    return values * lax.rsqrt(jnp.mean(values * values, axis=-1, keepdims=True) + epsilon)


def norm_back(values, scales, upstream):
    _, pullback = jax.vjp(rms_norm, values, scales)
    return pullback(upstream)


def geglu(gate_pre, other):
    return jax.nn.gelu(gate_pre, approximate=True) * other


def product(left, right):
    return jnp.dot(left, right, preferred_element_type=jnp.float32)


def product_left(left, right):
    return lax.dot_general(
        left, right, (((0,), (0,)), ((), ())), preferred_element_type=jnp.float32
    )


def product_right(left, right):
    return lax.dot_general(
        left, right, (((1,), (1,)), ((), ())), preferred_element_type=jnp.float32
    )


def positions_of(segments):
    length = segments.shape[0]
    places = jnp.arange(length, dtype=jnp.int32)
    fresh = jnp.concatenate([jnp.ones((1,), dtype=bool), segments[1:] != segments[:-1]])
    starts = lax.cummax(jnp.where(fresh, places, 0), axis=0)
    return places - starts


def rotary_tables(positions, head_size):
    half = head_size // 2
    frequency = jnp.exp(
        jnp.arange(half, dtype=jnp.float32) * (-2.0 * math.log(10000.0) / head_size)
    )
    angle = positions.astype(jnp.float32)[:, None] * frequency[None, :]
    return (jnp.cos(angle)[:, None, :], jnp.sin(angle)[:, None, :])


def rotate(values, cosine, sine):
    half = values.shape[-1] // 2
    first = values[..., :half]
    second = values[..., half:]
    return jnp.concatenate(
        [first * cosine - second * sine, second * cosine + first * sine], axis=-1
    )


def gather_rows(piece):
    return lax.all_gather(piece, "mp", axis=0, tiled=True)


def gather_grads(piece):
    return lax.all_gather(piece, "mp", axis=0, tiled=True)


def spread_rows(left, right, rows):

    def term(start, count):
        return product(left, right)

    return lax.psum_scatter(
        term(jnp.int32(0), lax.axis_size("mp") * rows).astype(jnp.bfloat16),
        "mp",
        scatter_dimension=0,
        tiled=True,
    ).astype(jnp.float32)


def spread_grads(pairs, rows):

    def term(start, count):
        total = None
        for left, right in pairs:
            part_sum = product_right(left, right)
            total = part_sum if total is None else total + part_sum
        return total

    return lax.psum_scatter(
        term(jnp.int32(0), lax.axis_size("mp") * rows).astype(jnp.bfloat16),
        "mp",
        scatter_dimension=0,
        tiled=True,
    ).astype(jnp.float32)


def shards(
    tokens,
    layer_vectors,
    segment_ids,
    cotangent,
    norm_gains,
    head_gains,
    w_query,
    w_key,
    w_value,
    w_out,
    w_left,
    w_right,
    w_gate,
    w_up,
    w_down,
    w_layer_gate,
    w_layer_proj,
):
    small = (
        lax.all_gather(norm_gains, ("dp", "mp"), axis=1, tiled=True),
        lax.all_gather(head_gains, ("dp", "mp"), axis=0, tiled=True),
        lax.all_gather(w_key, ("dp", "mp"), axis=0, tiled=True),
        lax.all_gather(w_value, ("dp", "mp"), axis=0, tiled=True),
        lax.all_gather(w_left, ("dp", "mp"), axis=0, tiled=True),
        lax.all_gather(w_right, ("dp", "mp"), axis=1, tiled=True),
        lax.all_gather(w_layer_gate, ("dp", "mp"), axis=0, tiled=True),
        lax.all_gather(w_layer_proj, ("dp", "mp"), axis=1, tiled=True),
    )
    gains = small[0].astype(jnp.float32)
    head_scales = small[1].astype(jnp.float32)
    key_all, value_all, left_weight, right_weight, layer_gate_weight, layer_proj_weight = small[2:]
    query_weight, out_weight = (
        lax.all_gather(w_query, "dp", axis=0, tiled=True),
        lax.all_gather(w_out, "dp", axis=1, tiled=True),
    )
    gate_weight, up_weight, down_weight = (
        lax.all_gather(w_gate, "dp", axis=0, tiled=True),
        lax.all_gather(w_up, "dp", axis=0, tiled=True),
        lax.all_gather(w_down, "dp", axis=1, tiled=True),
    )
    group_size = lax.axis_size("mp")
    shared_head = lax.axis_index("mp") * KV_HEADS // group_size
    key_weight = lax.dynamic_slice_in_dim(key_all, shared_head * HEAD_DIM, HEAD_DIM, 1)
    value_weight = lax.dynamic_slice_in_dim(value_all, shared_head * HEAD_DIM, HEAD_DIM, 1)
    rows = tokens.shape[0]
    length = segment_ids.shape[0]
    blocks = length // WINDOW
    scale = HEAD_DIM ** (-0.5)
    inputs = tokens.astype(jnp.float32)
    vectors = layer_vectors.astype(jnp.float32)
    normed = rms_norm(inputs, gains[0])
    normed_low = normed.astype(jnp.bfloat16)
    normed_all = gather_rows(normed_low)
    query_raw = product(normed_all, query_weight)
    key_raw = product(normed_all, key_weight)
    value_raw = product(normed_all, value_weight)
    cosine, sine = rotary_tables(positions_of(segment_ids), HEAD_DIM)

    def query_side(raw, scales):
        return rotate(rms_norm(raw.reshape(length, -1, HEAD_DIM), scales), cosine, sine)

    def key_side(raw, scales):
        return query_side(raw, scales)[:, 0]

    query_scales = head_scales[:HEAD_DIM]
    key_scales = head_scales[HEAD_DIM:]
    query_low = query_side(query_raw, query_scales).astype(jnp.bfloat16).transpose(1, 0, 2)
    heads_here = query_low.shape[0]
    pad_rows = jnp.zeros((WINDOW, HEAD_DIM), jnp.bfloat16)
    key_pad = jnp.concatenate([pad_rows, key_side(key_raw, key_scales).astype(jnp.bfloat16)])
    value_pad = jnp.concatenate([pad_rows, plain_norm(value_raw).astype(jnp.bfloat16)])
    segment_pad = jnp.concatenate([jnp.full((WINDOW,), -1, jnp.int32), segment_ids])
    row_place = jnp.arange(WINDOW)[:, None]
    col_place = jnp.arange(2 * WINDOW)[None, :]
    near = (col_place > row_place) & (col_place <= row_place + WINDOW)

    def block_scores(block):
        start = block * WINDOW
        query_block = lax.dynamic_slice_in_dim(query_low, start, WINDOW, 1)
        key_block = lax.dynamic_slice_in_dim(key_pad, start, 2 * WINDOW, 0)
        row_segments = lax.dynamic_slice_in_dim(segment_pad, start + WINDOW, WINDOW, 0)
        col_segments = lax.dynamic_slice_in_dim(segment_pad, start, 2 * WINDOW, 0)
        allowed = near & (row_segments[:, None] == col_segments[None, :])
        scores = scale * jnp.einsum(
            "hqd,kd->hqk", query_block, key_block, preferred_element_type=jnp.float32
        )
        return (jnp.where(allowed[None], scores, masked_score), query_block, key_block)

    def forward_block(block):
        scores, query_block, key_block = block_scores(block)
        top = jnp.max(scores, axis=-1, keepdims=True)
        expo = jnp.exp(scores - top)
        total = jnp.sum(expo, axis=-1, keepdims=True)
        probs = (expo / total).astype(jnp.bfloat16)
        value_block = lax.dynamic_slice_in_dim(value_pad, block * WINDOW, 2 * WINDOW, 0)
        output = jnp.einsum("hqk,kd->hqd", probs, value_block, preferred_element_type=jnp.float32)
        return (output.astype(jnp.bfloat16), (top + jnp.log(total))[..., 0])

    attended, log_totals = lax.map(forward_block, jnp.arange(blocks))
    attended_low = attended.transpose(0, 2, 1, 3).reshape(length, heads_here * HEAD_DIM)
    attn = spread_rows(attended_low, out_weight, rows)
    after_attn = inputs + rms_norm(attn, gains[1])
    left_low = product(normed_low, left_weight).astype(jnp.bfloat16)
    laurel_pre = product(left_low, right_weight)
    mixed = (after_attn + normed + rms_norm(laurel_pre, gains[2])) * root_half
    ff_in_all = gather_rows(rms_norm(mixed, gains[3]).astype(jnp.bfloat16))
    gate_pre = product(ff_in_all, gate_weight)
    up_pre = product(ff_in_all, up_weight)
    hidden_low = geglu(gate_pre, up_pre).astype(jnp.bfloat16)
    ff_out = spread_rows(hidden_low, down_weight, rows)
    after_ff = mixed + rms_norm(ff_out, gains[4])
    after_ff_low = after_ff.astype(jnp.bfloat16)
    layer_pre = product(after_ff_low, layer_gate_weight)
    layer_mix_low = geglu(layer_pre, vectors).astype(jnp.bfloat16)
    layer_out = product(layer_mix_low, layer_proj_weight)
    result = after_ff + rms_norm(layer_out, gains[5])
    query_back, out_back = (
        lax.all_gather(w_query, "dp", axis=0, tiled=True),
        lax.all_gather(w_out, "dp", axis=1, tiled=True),
    )
    gate_back, up_back, down_back = (
        lax.all_gather(w_gate, "dp", axis=0, tiled=True),
        lax.all_gather(w_up, "dp", axis=0, tiled=True),
        lax.all_gather(w_down, "dp", axis=1, tiled=True),
    )
    upstream = cotangent.astype(jnp.float32)
    grad_layer_out, grad_gain_five = norm_back(layer_out, gains[5], upstream)
    grad_layer_out_low = grad_layer_out.astype(jnp.bfloat16)
    grad_layer_proj = product_left(layer_mix_low, grad_layer_out_low)
    grad_mix = product_right(grad_layer_out_low, layer_proj_weight)
    _, layer_pull = jax.vjp(geglu, layer_pre, vectors)
    grad_layer_pre, grad_vectors = layer_pull(grad_mix)
    grad_layer_pre_low = grad_layer_pre.astype(jnp.bfloat16)
    grad_layer_gate = product_left(after_ff_low, grad_layer_pre_low)
    grad_after_ff = upstream + product_right(grad_layer_pre_low, layer_gate_weight)
    grad_ff_out, grad_gain_four = norm_back(ff_out, gains[4], grad_after_ff)
    grad_ff_all = gather_grads(grad_ff_out.astype(jnp.bfloat16))
    grad_down = product_left(hidden_low, grad_ff_all)
    grad_hidden = product_right(grad_ff_all, down_back)
    _, ff_pull = jax.vjp(geglu, gate_pre, up_pre)
    grad_gate, grad_up = ff_pull(grad_hidden)
    grad_gate_low = grad_gate.astype(jnp.bfloat16)
    grad_up_low = grad_up.astype(jnp.bfloat16)
    grad_gate_weight = product_left(ff_in_all, grad_gate_low)
    grad_up_weight = product_left(ff_in_all, grad_up_low)
    grad_ff_in = spread_grads(((grad_gate_low, gate_back), (grad_up_low, up_back)), rows)
    grad_mixed_norm, grad_gain_three = norm_back(mixed, gains[3], grad_ff_in)
    grad_branch = (grad_after_ff + grad_mixed_norm) * root_half
    grad_laurel, grad_gain_two = norm_back(laurel_pre, gains[2], grad_branch)
    grad_laurel_low = grad_laurel.astype(jnp.bfloat16)
    grad_right = product_left(left_low, grad_laurel_low)
    grad_left_low = product_right(grad_laurel_low, right_weight).astype(jnp.bfloat16)
    grad_left = product_left(normed_low, grad_left_low)
    grad_attn, grad_gain_one = norm_back(attn, gains[1], grad_branch)
    grad_attn_all = gather_grads(grad_attn.astype(jnp.bfloat16))
    grad_out = product_left(attended_low, grad_attn_all)
    grad_attended_low = product_right(grad_attn_all, out_back).astype(jnp.bfloat16)
    grad_heads = grad_attended_low.reshape(length, heads_here, HEAD_DIM).transpose(1, 0, 2)

    def backward_block(carry, block):
        grad_key_pad, grad_value_pad = carry
        start = block * WINDOW
        scores, query_block, key_block = block_scores(block)
        probs = jnp.exp(scores - log_totals[block][..., None])
        value_block = lax.dynamic_slice_in_dim(value_pad, start, 2 * WINDOW, 0)
        grad_block = lax.dynamic_slice_in_dim(grad_heads, start, WINDOW, 1)
        grad_probs = jnp.einsum(
            "hqd,kd->hqk", grad_block, value_block, preferred_element_type=jnp.float32
        )
        inner = jnp.sum(probs * grad_probs, axis=-1, keepdims=True)
        grad_scores = (probs * (grad_probs - inner)).astype(jnp.bfloat16)
        grad_query_block = scale * jnp.einsum(
            "hqk,kd->hqd", grad_scores, key_block, preferred_element_type=jnp.float32
        )
        grad_key_block = scale * jnp.einsum(
            "hqk,hqd->kd", grad_scores, query_block, preferred_element_type=jnp.float32
        )
        grad_value_block = jnp.einsum(
            "hqk,hqd->kd",
            probs.astype(jnp.bfloat16),
            grad_block,
            preferred_element_type=jnp.float32,
        )
        grad_key_pad = lax.dynamic_update_slice_in_dim(
            grad_key_pad,
            lax.dynamic_slice_in_dim(grad_key_pad, start, 2 * WINDOW, 0) + grad_key_block,
            start,
            0,
        )
        grad_value_pad = lax.dynamic_update_slice_in_dim(
            grad_value_pad,
            lax.dynamic_slice_in_dim(grad_value_pad, start, 2 * WINDOW, 0) + grad_value_block,
            start,
            0,
        )
        return ((grad_key_pad, grad_value_pad), grad_query_block)

    zero_pad = jnp.zeros((length + WINDOW, HEAD_DIM), jnp.float32)
    (grad_key_pad, grad_value_pad), grad_query_blocks = lax.scan(
        backward_block, (zero_pad, zero_pad), jnp.arange(blocks)
    )
    grad_query = grad_query_blocks.transpose(0, 2, 1, 3).reshape(length, heads_here, HEAD_DIM)
    _, query_pull = jax.vjp(query_side, query_raw, query_scales)
    grad_query_raw, grad_query_scales = query_pull(grad_query)
    _, key_pull = jax.vjp(key_side, key_raw, key_scales)
    grad_key_raw, grad_key_scales = key_pull(grad_key_pad[WINDOW:])
    _, value_pull = jax.vjp(plain_norm, value_raw)
    (grad_value_raw,) = value_pull(grad_value_pad[WINDOW:])
    grad_query_low = grad_query_raw.astype(jnp.bfloat16)
    grad_key_low = grad_key_raw.astype(jnp.bfloat16)
    grad_value_low = grad_value_raw.astype(jnp.bfloat16)
    grad_query_weight = product_left(normed_all, grad_query_low)
    key_grad_full = lax.dynamic_update_slice_in_dim(
        jnp.zeros(key_all.shape, jnp.float32),
        product_left(normed_all, grad_key_low),
        shared_head * HEAD_DIM,
        1,
    )
    value_grad_full = lax.dynamic_update_slice_in_dim(
        jnp.zeros(value_all.shape, jnp.float32),
        product_left(normed_all, grad_value_low),
        shared_head * HEAD_DIM,
        1,
    )
    grad_normed_heads = spread_grads(
        ((grad_query_low, query_back), (grad_key_low, key_weight), (grad_value_low, value_weight)),
        rows,
    )
    grad_normed = grad_branch + product_right(grad_left_low, left_weight) + grad_normed_heads
    grad_inputs_norm, grad_gain_zero = norm_back(inputs, gains[0], grad_normed)
    grad_inputs = grad_branch + grad_inputs_norm
    gain_grads = jnp.stack(
        [
            grad_gain_zero,
            grad_gain_one,
            grad_gain_two,
            grad_gain_three,
            grad_gain_four,
            grad_gain_five,
        ]
    )
    head_grads = jnp.concatenate([grad_query_scales, grad_key_scales])
    attn_grads = (
        lax.psum_scatter(
            grad_query_weight.astype(jnp.bfloat16), "dp", scatter_dimension=0, tiled=True
        ).astype(jnp.float32),
        lax.psum_scatter(
            grad_out.astype(jnp.bfloat16), "dp", scatter_dimension=1, tiled=True
        ).astype(jnp.float32),
    )
    ff_grads = (
        lax.psum_scatter(
            grad_gate_weight.astype(jnp.bfloat16), "dp", scatter_dimension=0, tiled=True
        ).astype(jnp.float32),
        lax.psum_scatter(
            grad_up_weight.astype(jnp.bfloat16), "dp", scatter_dimension=0, tiled=True
        ).astype(jnp.float32),
        lax.psum_scatter(
            grad_down.astype(jnp.bfloat16), "dp", scatter_dimension=1, tiled=True
        ).astype(jnp.float32),
    )
    small_grads = (
        lax.psum_scatter(gain_grads, ("dp", "mp"), scatter_dimension=1, tiled=True),
        lax.psum_scatter(head_grads, ("dp", "mp"), scatter_dimension=0, tiled=True),
        lax.psum_scatter(key_grad_full, ("dp", "mp"), scatter_dimension=0, tiled=True),
        lax.psum_scatter(value_grad_full, ("dp", "mp"), scatter_dimension=0, tiled=True),
        lax.psum_scatter(grad_left, ("dp", "mp"), scatter_dimension=0, tiled=True),
        lax.psum_scatter(grad_right, ("dp", "mp"), scatter_dimension=1, tiled=True),
        lax.psum_scatter(grad_layer_gate, ("dp", "mp"), scatter_dimension=0, tiled=True),
        lax.psum_scatter(grad_layer_proj, ("dp", "mp"), scatter_dimension=1, tiled=True),
    )
    return (
        result.astype(jnp.bfloat16),
        grad_inputs.astype(jnp.bfloat16),
        grad_vectors.astype(jnp.bfloat16),
        small_grads[0],
        small_grads[1],
        attn_grads[0],
        small_grads[2],
        small_grads[3],
        attn_grads[1],
        small_grads[4],
        small_grads[5],
        ff_grads[0],
        ff_grads[1],
        ff_grads[2],
        small_grads[6],
        small_grads[7],
    )


def solution(mesh):
    in_specs = (
        P(("dp", "mp"), None),
        P(("dp", "mp"), None),
        P("dp"),
        P(("dp", "mp"), None),
        P(None, ("dp", "mp")),
        P(("dp", "mp")),
        P("dp", "mp"),
        P(("dp", "mp"), None),
        P(("dp", "mp"), None),
        P("mp", "dp"),
        P(("dp", "mp"), None),
        P(None, ("dp", "mp")),
        P("dp", "mp"),
        P("dp", "mp"),
        P("mp", "dp"),
        P(("dp", "mp"), None),
        P(None, ("dp", "mp")),
    )
    out_specs = (
        P(("dp", "mp"), None),
        P(("dp", "mp"), None),
        P(("dp", "mp"), None),
        P(None, ("dp", "mp")),
        P(("dp", "mp")),
        P("dp", "mp"),
        P(("dp", "mp"), None),
        P(("dp", "mp"), None),
        P("mp", "dp"),
        P(("dp", "mp"), None),
        P(None, ("dp", "mp")),
        P("dp", "mp"),
        P("dp", "mp"),
        P("mp", "dp"),
        P(("dp", "mp"), None),
        P(None, ("dp", "mp")),
    )
    return jax.shard_map(shards, mesh=mesh, in_specs=in_specs, out_specs=out_specs, check_vma=False)
```

profile of v0, /device:TPU:0, one launch (start us, length us, event | category | flops | bytes accessed | tf_op | source)
XLA Modules:
  0.0 2786.0 jit_solution(7657492606499107481)
XLA Ops:
  8.0 43.8 %all-gather = bf16[32,64,6]{1,2,0:T(8,128)(2,1)S(1)} all-gather(bf16[1,64,6]{1,2,0:T(8,128)(2,1)} %bitcast.237), channel_id=1, replica_groups=mesh['dp'=8,'mp'=4] {'dp','mp'}, dimensions={0}, use_global_device_ids=true | all-gather | bytes 25344 | tf_op jit(solution)/shard_map/all_gather | solution.py:135
  115.2 50.6 %all-gather.21.cloned.1.call-done = bf16[2048,512]{1,0:T(8,128)(2,1)} async-done(((bf16[64,512]{1,0:T(8,128)(2,1)}), bf16[2048,512]{1,0:T(8,128)(2,1)}) %all-gather.21.cloned.1.call-update) | async-done | bytes 2097168 | tf_op jit(solution)/shard_map/all_gather | solution.py:138
  171.9 44.1 %all-gather.17.cloned.1.call-done = bf16[2048,512]{1,0:T(8,128)(2,1)} async-done(((bf16[256,512]{1,0:T(8,128)(2,1)}), bf16[2048,512]{1,0:T(8,128)(2,1)}) %all-gather.17.cloned.1.call-update) | async-done | bytes 2097168 | tf_op jit(solution)/shard_map/all_gather | solution.py:148
  365.4 82.9 %all-gather.27.cloned.1.call-done = bf16[2048,2048]{1,0:T(8,128)(2,1)} async-done(((bf16[256,2048]{1,0:T(8,128)(2,1)}), bf16[2048,2048]{1,0:T(8,128)(2,1)}) %all-gather.27.cloned.1.call-update) | async-done | bytes 8388624 | tf_op jit(solution)/shard_map/all_gather | solution.py:152
  497.8 112.7 %all-gather.29.cloned.1.call-done = bf16[2048,2048]{1,0:T(8,128)(2,1)} async-done(((bf16[256,2048]{1,0:T(8,128)(2,1)}), bf16[2048,2048]{1,0:T(8,128)(2,1)}) %all-gather.29.cloned.1.call-update) | async-done | bytes 8388624 | tf_op jit(solution)/shard_map/all_gather | solution.py:153
  628.2 107.9 %all-gather.31.cloned.1.call-done = bf16[2048,2048]{1,0:T(8,128)(2,1)} async-done(((bf16[2048,256]{1,0:T(8,128)(2,1)}), bf16[2048,2048]{1,0:T(8,128)(2,1)}) %all-gather.31.cloned.1.call-update) | async-done | bytes 8388624 | tf_op jit(solution)/shard_map/all_gather | solution.py:154
  751.6 41.3 %reduce-scatter.23.cloned.1.call-done = bf16[256,2048]{1,0:T(8,128)(2,1)} async-done(((bf16[1024,2048]{1,0:T(8,128)(2,1)}), bf16[256,2048]{1,0:T(8,128)(2,1)}) %reduce-scatter.23.cloned.1.call-update) | async-done | bytes 1048592 | tf_op jit(solution)/shard_map/reduce_scatter | solution.py:90
  796.2 53.1 %all-gather.33.cloned.1.call-done = bf16[2048,256]{1,0:T(8,128)(2,1)} async-done(((bf16[64,256]{1,0:T(8,128)(2,1)}), bf16[2048,256]{1,0:T(8,128)(2,1)}) %all-gather.33.cloned.1.call-update) | async-done | bytes 1048592 | tf_op jit(solution)/shard_map/all_gather | solution.py:141
  851.0 53.8 %all-gather.35.cloned.1.call-done = bf16[256,2048]{0,1:T(8,128)(2,1)} async-done(((bf16[256,64]{0,1:T(8,128)(2,1)}), bf16[256,2048]{0,1:T(8,128)(2,1)}) %all-gather.35.cloned.1.call-update) | async-done | bytes 1048592 | tf_op jit(solution)/shard_map/all_gather | solution.py:142
  1000.2 44.0 %reduce-scatter.25.cloned.1.call-done = bf16[256,2048]{1,0:T(8,128)(2,1)} async-done(((bf16[1024,2048]{1,0:T(8,128)(2,1)}), bf16[256,2048]{1,0:T(8,128)(2,1)}) %reduce-scatter.25.cloned.1.call-update) | async-done | bytes 1048592 | tf_op jit(solution)/shard_map/reduce_scatter | solution.py:107
  1096.0 66.2 %while.33 = (s32[]{:T(128)}, f32[1536,256]{0,1:T(8,128)S(1)}, f32[1536,256]{0,1:T(8,128)}, f32[2,2,512,256]{3,2,0,1:T(8,128)}, s32[2]{0:T(128)S(1)}, /*index=5*/...) while((s32[]{:T(128)}, f32[1536,256]{0,1:T(8,128)S(1)}, ...), condition=%wide.region_25.26_spmd.clone, body=%wide.region_23.25_spmd.clone.sunk | while | flops 2703752192 | bytes 108577864 | solution.py:314
  1274.9 89.4 %reduce-scatter.51.cloned.1.call-done = f32[64,64]{1,0:T(8,128)} async-done(((f32[2048,64]{1,0:T(8,128)}), f32[64,64]{1,0:T(8,128)}) %reduce-scatter.51.cloned.1.call-update) | async-done | bytes 16400
  1365.7 40.6 %all-reduce.8 = f32[512]{0:T(512)S(1)} all-reduce(f32[512]{0:T(512)S(1)} %pad_maximum_fusion), channel_id=7, replica_groups=mesh['dp'=8,'mp'=4] {'dp','mp'}, use_global_device_ids=true, to_apply=%region_40.41.clone | all-reduce | flops 512 | bytes 4096
  1406.9 107.7 %reduce-scatter.43.cloned.1.call-done = bf16[2048,256]{1,0:T(8,128)(2,1)} async-done(((bf16[2048,2048]{1,0:T(8,128)(2,1)}), bf16[2048,256]{1,0:T(8,128)(2,1)}) %reduce-scatter.43.cloned.1.call-update) | async-done | bytes 1048592 | tf_op jit(solution)/shard_map/reduce_scatter | solution.py:373
  1517.3 148.8 %reduce-scatter.39.cloned.1.call-done = bf16[256,2048]{1,0:T(8,128)(2,1)} async-done(((bf16[2048,2048]{1,0:T(8,128)(2,1)}), bf16[256,2048]{1,0:T(8,128)(2,1)}) %reduce-scatter.39.cloned.1.call-update) | async-done | bytes 1048592 | tf_op jit(solution)/shard_map/reduce_scatter | solution.py:367
  1668.9 149.3 %reduce-scatter.41.cloned.1.call-done = bf16[256,2048]{1,0:T(8,128)(2,1)} async-done(((bf16[2048,2048]{1,0:T(8,128)(2,1)}), bf16[256,2048]{1,0:T(8,128)(2,1)}) %reduce-scatter.41.cloned.1.call-update) | async-done | bytes 1048592 | tf_op jit(solution)/shard_map/reduce_scatter | solution.py:370
  1821.0 67.8 %reduce-scatter.35.cloned.1.call-done = bf16[512,256]{1,0:T(8,128)(2,1)} async-done(((bf16[512,2048]{1,0:T(8,128)(2,1)}), bf16[512,256]{1,0:T(8,128)(2,1)}) %reduce-scatter.35.cloned.1.call-update) | async-done | bytes 262160 | tf_op jit(solution)/shard_map/reduce_scatter | solution.py:362
  1890.6 68.4 %reduce-scatter.29.cloned.1.call-done = bf16[256,512]{1,0:T(8,128)(2,1)} async-done(((bf16[2048,512]{1,0:T(8,128)(2,1)}), bf16[256,512]{1,0:T(8,128)(2,1)}) %reduce-scatter.29.cloned.1.call-update) | async-done | bytes 262160 | tf_op jit(solution)/shard_map/reduce_scatter | solution.py:359
  1964.2 130.8 %reduce-scatter.49.cloned.1.call-done = f32[64,6]{1,0:T(8,128)} async-done(((f32[2048,6]{1,0:T(8,128)}), f32[64,6]{1,0:T(8,128)}) %reduce-scatter.49.cloned.1.call-update) | async-done | bytes 1552
  2096.4 134.2 %reduce-scatter.45.cloned.1.call-done = f32[64,256]{1,0:T(8,128)} async-done(((f32[2048,256]{1,0:T(8,128)}), f32[64,256]{1,0:T(8,128)}) %reduce-scatter.45.cloned.1.call-update) | async-done | bytes 65552 | tf_op jit(solution)/shard_map/reduce_scatter | solution.py:384
  2230.6 135.4 %reduce-scatter.47.cloned.1.call-done = f32[256,64]{0,1:T(8,128)} async-done(((f32[256,2048]{0,1:T(8,128)}), f32[256,64]{0,1:T(8,128)}) %reduce-scatter.47.cloned.1.call-update) | async-done | bytes 65552 | tf_op jit(solution)/shard_map/reduce_scatter | solution.py:385
  2366.0 133.5 %reduce-scatter.37.cloned.1.call-done = f32[64,64]{1,0:T(8,128)} async-done(((f32[2048,64]{1,0:T(8,128)}), f32[64,64]{1,0:T(8,128)}) %reduce-scatter.37.cloned.1.call-update) | async-done | bytes 16400 | tf_op jit(solution)/shard_map/reduce_scatter | solution.py:382
  2499.5 139.9 %reduce-scatter.33.cloned.1.call-done = f32[64,512]{1,0:T(8,128)} async-done(((f32[2048,512]{1,0:T(8,128)}), f32[64,512]{1,0:T(8,128)}) %reduce-scatter.33.cloned.1.call-update) | async-done | bytes 131088 | tf_op jit(solution)/shard_map/reduce_scatter | solution.py:381
  2639.4 139.9 %reduce-scatter.31.cloned.1.call-done = f32[64,512]{1,0:T(8,128)} async-done(((f32[2048,512]{1,0:T(8,128)}), f32[64,512]{1,0:T(8,128)}) %reduce-scatter.31.cloned.1.call-update) | async-done | bytes 131088 | tf_op jit(solution)/shard_map/reduce_scatter | solution.py:380
  (507 shorter events, 658.8 us)
Async XLA Ops:
  56.1 159.9 %all-gather.17.cloned.1.call-start = ((), (), s32[]{:S(2)}) async-start(), calls=%async_computation.17 | async-start | bytes 2359296 | tf_op jit(solution)/shard_map/all_gather | solution.py:148
  56.7 210.8 %all-gather.23.cloned.1.call-start = ((), (), s32[]{:S(2)}) async-start(), calls=%async_computation.20 | async-start | bytes 2359296 | tf_op jit(solution)/shard_map/all_gather | solution.py:149
  57.3 299.7 %reduce-scatter.21.cloned.1.call-start = ((), (), s32[]{:S(2)}) async-start(), calls=%async_computation.21 | async-start | bytes 5242880 | tf_op jit(solution)/shard_map/reduce_scatter | solution.py:90
  273.6 174.7 %all-gather.27.cloned.1.call-start = ((), (), s32[]{:S(2)}) async-start(), calls=%async_computation.23 | async-start | bytes 9437184 | tf_op jit(solution)/shard_map/all_gather | solution.py:152
  274.3 208.8 %all-gather.25.cloned.1.call-start = ((), (), s32[]{:S(2)}) async-start(), calls=%async_computation.22 | async-start | bytes 5242880 | tf_op jit(solution)/shard_map/all_gather | solution.py:78
  364.0 246.5 %all-gather.29.cloned.1.call-start = ((), (), s32[]{:S(2)}) async-start(), calls=%async_computation.24 | async-start | bytes 9437184 | tf_op jit(solution)/shard_map/all_gather | solution.py:153
  364.8 371.4 %all-gather.31.cloned.1.call-start = ((), (), s32[]{:S(2)}) async-start(), calls=%async_computation.25 | async-start | bytes 9437184 | tf_op jit(solution)/shard_map/all_gather | solution.py:154
  365.3 427.6 %reduce-scatter.23.cloned.1.call-start = ((), (), s32[]{:S(2)}) async-start(), calls=%async_computation.26 | async-start | bytes 5242880 | tf_op jit(solution)/shard_map/reduce_scatter | solution.py:90
  750.6 154.2 %all-gather.35.cloned.1.call-start = ((), (), s32[]{:S(2)}) async-start(), calls=%async_computation.28 | async-start | bytes 1081344 | tf_op jit(solution)/shard_map/all_gather | solution.py:142
  751.4 198.6 %all-gather.37.cloned.1.call-start = ((), (), s32[]{:S(2)}) async-start(), calls=%async_computation.29 | async-start | bytes 5242880 | tf_op jit(solution)/shard_map/all_gather | solution.py:82
  916.4 127.8 %reduce-scatter.25.cloned.1.call-start = ((), (), s32[]{:S(2)}) async-start(), calls=%async_computation.30 | async-start | bytes 5242880 | tf_op jit(solution)/shard_map/reduce_scatter | solution.py:107
  1053.9 189.9 %reduce-scatter.27.cloned.1.call-start = ((), (), s32[]{:S(2)}) async-start(), calls=%async_computation.32 | async-start | bytes 5242880 | tf_op jit(solution)/shard_map/reduce_scatter | solution.py:107
  1182.0 182.2 %reduce-scatter.51.cloned.1.call-start = ((), (), s32[]{:S(2)}) async-start(), calls=%async_computation.44 | async-start | bytes 1081344
  1184.8 329.8 %reduce-scatter.43.cloned.1.call-start = ((), (), s32[]{:S(2)}) async-start(), calls=%async_computation.40 | async-start | bytes 9437184 | tf_op jit(solution)/shard_map/reduce_scatter | solution.py:373
  1199.0 467.1 %reduce-scatter.39.cloned.1.call-start = ((), (), s32[]{:S(2)}) async-start(), calls=%async_computation.38 | async-start | bytes 9437184 | tf_op jit(solution)/shard_map/reduce_scatter | solution.py:367
  1214.3 604.0 %reduce-scatter.41.cloned.1.call-start = ((), (), s32[]{:S(2)}) async-start(), calls=%async_computation.39 | async-start | bytes 9437184 | tf_op jit(solution)/shard_map/reduce_scatter | solution.py:370
  1228.5 660.4 %reduce-scatter.35.cloned.1.call-start = ((), (), s32[]{:S(2)}) async-start(), calls=%async_computation.36 | async-start | bytes 2359296 | tf_op jit(solution)/shard_map/reduce_scatter | solution.py:362
  1235.6 723.5 %reduce-scatter.29.cloned.1.call-start = ((), (), s32[]{:S(2)}) async-start(), calls=%async_computation.33 | async-start | bytes 2359296 | tf_op jit(solution)/shard_map/reduce_scatter | solution.py:359
  1241.7 853.2 %reduce-scatter.49.cloned.1.call-start = ((), (), s32[]{:S(2)}) async-start(), calls=%async_computation.43 | async-start | bytes 1081344
  1249.9 980.7 %reduce-scatter.45.cloned.1.call-start = ((), (), s32[]{:S(2)}) async-start(), calls=%async_computation.41 | async-start | bytes 2162688 | tf_op jit(solution)/shard_map/reduce_scatter | solution.py:384
  1253.1 1112.9 %reduce-scatter.47.cloned.1.call-start = ((), (), s32[]{:S(2)}) async-start(), calls=%async_computation.42 | async-start | bytes 2162688 | tf_op jit(solution)/shard_map/reduce_scatter | solution.py:385
  1256.3 1243.2 %reduce-scatter.37.cloned.1.call-start = ((), (), s32[]{:S(2)}) async-start(), calls=%async_computation.37 | async-start | bytes 1081344 | tf_op jit(solution)/shard_map/reduce_scatter | solution.py:382
  1259.8 1379.6 %reduce-scatter.33.cloned.1.call-start = ((), (), s32[]{:S(2)}) async-start(), calls=%async_computation.35 | async-start | bytes 4325376 | tf_op jit(solution)/shard_map/reduce_scatter | solution.py:381
  1267.3 1512.0 %reduce-scatter.31.cloned.1.call-start = ((), (), s32[]{:S(2)}) async-start(), calls=%async_computation.34 | async-start | bytes 4325376 | tf_op jit(solution)/shard_map/reduce_scatter | solution.py:380
  (133 other events, 3799.4 us)
Sparse Core Ops, SparseCore 0:
  10.9 59.2 all-gather.18
  109.5 56.2 all-gather.20
  167.8 48.1 all-gather.16
  217.9 49.5 all-gather.22
  273.7 44.9 reduce-scatter.20
  321.0 127.1 all-gather.26
  485.5 124.9 all-gather.28
  612.6 123.5 all-gather.30
  795.6 53.6 all-gather.32
  852.1 52.6 all-gather.34
  999.6 44.4 reduce-scatter.24
  1182.2 44.5 reduce-scatter.26
  1229.4 134.7 reduce-scatter.50
  1368.3 146.2 reduce-scatter.42
  1518.1 147.9 reduce-scatter.38
  1670.2 147.9 reduce-scatter.40
  1821.8 67.0 reduce-scatter.34
  1892.4 66.6 reduce-scatter.28
  1961.1 133.7 reduce-scatter.48
  2097.9 132.6 reduce-scatter.44
  2233.3 132.6 reduce-scatter.46
  2368.8 130.6 reduce-scatter.36
  2502.3 137.0 reduce-scatter.32
  2642.3 136.9 reduce-scatter.30
  (5 shorter events, 177.3 us)
where the time goes:
time: 2800 us; the launch traced here: 2790 us
  waiting for transfers between devices  2170 us (78%)
  matrix products  265 us (9%)
  blocking collectives  202 us (7%)
  other arithmetic  67.3 us (2%)
  local copies, waits for them, and re-layouts  54.6 us (2%)
    unnamed x31, waiting for transfers between devices  226 us
    reduce_scatter x1, waiting for transfers between devices, shards(): lax.psum_scatter(grad_up_weight.astype(jnp.bfloat16), 'dp', scatter_dimen...  149 us
    reduce_scatter x1, waiting for transfers between devices, shards(): lax.psum_scatter(grad_gate_weight.astype(jnp.bfloat16), 'dp', scatter_dim...  149 us
    reduce_scatter x1, waiting for transfers between devices, shards(): lax.psum_scatter(value_grad_full, ('dp', 'mp'), scatter_dimension=0, tile...  140 us
    reduce_scatter x1, waiting for transfers between devices, shards(): lax.psum_scatter(key_grad_full, ('dp', 'mp'), scatter_dimension=0, tiled=...  140 us
    reduce_scatter x1, waiting for transfers between devices, shards(): lax.psum_scatter(grad_layer_proj, ('dp', 'mp'), scatter_dimension=1, tile...  135 us
    reduce_scatter x1, waiting for transfers between devices, shards(): lax.psum_scatter(grad_layer_gate, ('dp', 'mp'), scatter_dimension=0, tile...  134 us
    reduce_scatter x1, waiting for transfers between devices, shards(): lax.psum_scatter(grad_left, ('dp', 'mp'), scatter_dimension=0, tiled=True)  133 us
  transfers between devices with their start and end apart: 29, of which 26 were waited for; matrix products, arithmetic and copies ran while one was open for 7% of the time, Pallas kernels for 0%

commit v1 on v0

v1 whole, which is shorter than its diff:
```python
import math

import jax
import jax.numpy as jnp
from jax import lax
from jax.experimental import pallas as pl
from jax.experimental.pallas import tpu as pltpu
from jax.sharding import PartitionSpec as P

HEAD_DIM = 256
WINDOW = 512

epsilon = 1e-06
root_half = 1.0 / math.sqrt(2.0)
masked_score = -1e30
bf16 = jnp.bfloat16
f32 = jnp.float32


def rms_norm(values, scales):
    return values * lax.rsqrt(jnp.mean(values * values, axis=-1, keepdims=True) + epsilon) * scales


def norm_back(values, scales, upstream):
    _, pullback = jax.vjp(rms_norm, values, scales)
    return pullback(upstream)


def geglu(gate_pre, other):
    return jax.nn.gelu(gate_pre, approximate=True) * other


def product(left, right):
    return jnp.dot(left, right, preferred_element_type=f32)


def product_left(left, right):
    return lax.dot_general(left, right, (((0,), (0,)), ((), ())), preferred_element_type=f32)


def product_right(left, right):
    return lax.dot_general(left, right, (((1,), (1,)), ((), ())), preferred_element_type=f32)


def rotary_tables(segments):
    length = segments.shape[0]
    half = HEAD_DIM // 2
    places = jnp.arange(length, dtype=jnp.int32)
    starts = jnp.sum((segments[None, :] < segments[:, None]).astype(jnp.int32), axis=1)
    frequency = jnp.exp(jnp.arange(half, dtype=f32) * (-2.0 * math.log(10000.0) / HEAD_DIM))
    angle = (places - starts).astype(f32)[:, None] * frequency[None, :]
    return jnp.cos(angle), jnp.sin(angle)


def after(value, *others):
    return lax.optimization_barrier((value, *others))[0]


def core_swap(value):
    return lax.ppermute(value, "mp", [(0, 1), (1, 0), (2, 3), (3, 2)])


def chip_swap(value):
    return lax.ppermute(value, "mp", [(0, 2), (2, 0), (1, 3), (3, 1)])


class Ring:
    def __init__(self):
        self.count = count = lax.axis_size("dp")
        order = [*range(0, count, 2), *reversed(range(1, count, 2))]
        self.ahead = [(order[i], order[(i + 1) % count]) for i in range(count)]
        self.behind = [(b, a) for a, b in self.ahead]
        me = lax.axis_index("dp")
        self.place = jnp.where(me % 2 == 0, me // 2, count - 1 - me // 2)
        self.unrolled = count <= 8

    def member(self, offset):
        place = (self.place + offset) % self.count
        return jnp.where(place < self.count // 2, 2 * place, 2 * (self.count - 1 - place) + 1)

    def up(self, value):
        return lax.ppermute(value, "dp", self.ahead)

    def down(self, value):
        return lax.ppermute(value, "dp", self.behind)

    def gather(self, block, wait=()):
        size, width = block.shape
        if wait:
            block = after(block, *wait)
        if not self.unrolled:
            return lax.all_gather(block, "dp", axis=0, tiled=True), [()] * self.count
        whole = jnp.zeros((size * self.count, width), block.dtype)

        def put(whole, piece, offset, inner=0):
            return lax.dynamic_update_slice(whole, piece, (self.member(offset) * size + inner, 0))

        whole = put(whole, block, 0)
        left = right = block
        hops = []
        for hop in range(1, self.count // 2):
            left, right = self.up(left), self.down(right)
            whole = put(whole, left, -hop)
            whole = put(whole, right, hop)
            hops.append((left, right))
        half = size // 32 * 16
        far = self.count // 2
        left, right = self.up(left[:half]), self.down(right[half:])
        whole = put(whole, left, -far)
        whole = put(whole, right, far, half)
        hops.append((left, right))
        return whole, hops

    def reduce(self, whole, wait=()):
        size = whole.shape[0] // self.count
        if wait:
            whole = after(whole, *wait)
        if not self.unrolled:
            own = lax.psum_scatter(whole, "dp", scatter_dimension=0, tiled=True)
            return own.astype(f32), [()] * self.count

        def take(offset, start=0, stop=size):
            return lax.dynamic_slice_in_dim(
                whole, self.member(offset) * size + start, stop - start, 0
            )

        half = size // 32 * 16
        far = self.count // 2
        left, right = self.up(take(far, 0, half)), self.down(take(far, half, size))
        left = jnp.pad(left, [(0, size - half), (0, 0)])
        right = jnp.pad(right, [(half, 0), (0, 0)])
        hops = [(left, right)]
        for hop in reversed(range(1, far)):
            left = self.up((take(hop).astype(f32) + left).astype(bf16))
            right = self.down((take(-hop).astype(f32) + right).astype(bf16))
            hops.append((left, right))
        return take(0).astype(f32) + left + right, hops


def join(mine, other, swapped, axis):
    return jnp.where(
        swapped,
        jnp.concatenate([other, mine], axis=axis),
        jnp.concatenate([mine, other], axis=axis),
    )


def gather_small(piece, axis):
    me = lax.axis_index("mp")
    piece = join(piece, core_swap(piece), me % 2 == 1, axis)
    piece = join(piece, chip_swap(piece), me // 2 == 1, axis)
    count = lax.axis_size("dp")
    me = lax.axis_index("dp")
    step = 1
    while step < count:
        other = lax.ppermute(piece, "dp", [(i, i ^ step) for i in range(count)])
        piece = join(piece, other, (me // step) % 2 == 1, axis)
        step *= 2
    return piece


def sum_small(value):
    value = value + core_swap(value)
    value = value + chip_swap(value)
    count = lax.axis_size("dp")
    step = 1
    while step < count:
        value = value + lax.ppermute(value, "dp", [(i, i ^ step) for i in range(count)])
        step *= 2
    return value


def gather_slots(piece):
    near = core_swap(piece)
    across = chip_swap(piece)
    return piece, near, across, core_swap(across)


def reduce_slots(partial, pieces=2):
    parts = []
    for i in range(pieces):
        inner = core_swap(partial(3, i, pieces).astype(bf16))
        outer = chip_swap((partial(2, i, pieces) + inner).astype(bf16))
        near = core_swap(partial(1, i, pieces).astype(bf16))
        parts.append((i, near, outer))
    return jnp.concatenate(
        [partial(0, i, pieces) + near + outer for i, near, outer in parts], axis=1
    )


def columns(value, i, pieces):
    width = value.shape[1] // pieces
    return value[:, i * width : (i + 1) * width]


def rows_of(value, i, pieces):
    width = value.shape[0] // pieces
    return value[i * width : (i + 1) * width]


def normalize(raw):
    return raw * lax.rsqrt(jnp.mean(raw * raw, axis=-1, keepdims=True) + epsilon)


def turn(values, cosine, sine):
    half = HEAD_DIM // 2
    first, second = values[:, :half], values[:, half:]
    return jnp.concatenate(
        [first * cosine - second * sine, second * cosine + first * sine], axis=1
    )


def dot(left, right, dims):
    return lax.dot_general(left, right, ((dims[:1], dims[1:]), ((), ())), preferred_element_type=f32)


TILE = 256


def tiles(length):
    return [(i, max(0, i - WINDOW)) for i in range(0, length, TILE)]


def tile_probs(query, key, start, first, rows_ref, cols_ref):
    stop = start + TILE
    scores = dot(query, key, (1, 1)) * HEAD_DIM**-0.5
    row = start + lax.broadcasted_iota(jnp.int32, scores.shape, 0)
    col = first + lax.broadcasted_iota(jnp.int32, scores.shape, 1)
    kept = (col <= row) & (row - col < WINDOW)
    kept &= rows_ref[start:stop, :] == cols_ref[:, first:stop]
    scores = jnp.where(kept, scores, masked_score)
    expo = jnp.exp(scores - jnp.max(scores, axis=-1, keepdims=True))
    return expo / jnp.sum(expo, axis=-1, keepdims=True)


def forward_kernel(raw_ref, cos_ref, sin_ref, rows_ref, cols_ref, gain_ref, out_ref, low_ref):
    length, across = raw_ref.shape
    heads = across // HEAD_DIM - 2
    key_at, value_at = heads * HEAD_DIM, (heads + 1) * HEAD_DIM
    for start in range(0, length, TILE):
        at = slice(start, start + TILE)
        for head in range(heads + 1):
            cols = slice(head * HEAD_DIM, (head + 1) * HEAD_DIM)
            gain = gain_ref[int(head == heads) : int(head == heads) + 1, :]
            turned = turn(normalize(raw_ref[at, cols]) * gain, cos_ref[at, :], sin_ref[at, :])
            low_ref[at, cols] = turned.astype(bf16)
        low_ref[at, value_at:] = normalize(raw_ref[at, value_at:]).astype(bf16)
    for start, first in tiles(length):
        stop = start + TILE
        key = low_ref[first:stop, key_at:value_at]
        value = low_ref[first:stop, value_at:]
        for head in range(heads):
            cols = slice(head * HEAD_DIM, (head + 1) * HEAD_DIM)
            probs = tile_probs(low_ref[start:stop, cols], key, start, first, rows_ref, cols_ref)
            out_ref[start:stop, cols] = dot(probs.astype(bf16), value, (1, 0)).astype(bf16)


def norm_grad(raw, gain, upstream):
    scale = lax.rsqrt(jnp.mean(raw * raw, axis=-1, keepdims=True) + epsilon)
    unit = raw * scale
    inner = upstream * gain
    grad = scale * (inner - unit * jnp.mean(inner * unit, axis=-1, keepdims=True))
    return grad, jnp.sum(upstream * unit, axis=0, keepdims=True)


def backward_kernel(
    raw_ref, low_ref, up_ref, cos_ref, sin_ref, rows_ref, cols_ref, gain_ref, out_ref, gain_out_ref,
    key_sum, value_sum,
):
    length, across = raw_ref.shape
    heads = across // HEAD_DIM - 2
    key_at, value_at = heads * HEAD_DIM, (heads + 1) * HEAD_DIM
    scale = HEAD_DIM**-0.5
    key_sum[...] = jnp.zeros_like(key_sum)
    value_sum[...] = jnp.zeros_like(value_sum)
    query_gain = jnp.zeros((1, HEAD_DIM), f32)
    key_gain = jnp.zeros((1, HEAD_DIM), f32)
    for start, first in tiles(length):
        stop = start + TILE
        at = slice(start, stop)
        key = low_ref[first:stop, key_at:value_at]
        value = low_ref[first:stop, value_at:]
        for head in range(heads):
            cols = slice(head * HEAD_DIM, (head + 1) * HEAD_DIM)
            query = low_ref[at, cols]
            upstream = up_ref[at, cols]
            probs = tile_probs(query, key, start, first, rows_ref, cols_ref)
            grad_probs = dot(upstream, value, (1, 1))
            inner = jnp.sum(probs * grad_probs, axis=-1, keepdims=True)
            grad_scores = (probs * (grad_probs - inner)).astype(bf16)
            value_sum[first:stop, :] += dot(probs.astype(bf16), upstream, (0, 0))
            key_sum[first:stop, :] += dot(grad_scores, query, (0, 0)) * scale
            grad_query = dot(grad_scores, key, (1, 0)) * scale
            grad_query = turn(grad_query, cos_ref[at, :], -sin_ref[at, :])
            grad, gain = norm_grad(raw_ref[at, cols], gain_ref[0:1, :], grad_query)
            out_ref[at, cols] = grad.astype(bf16)
            query_gain += gain
    for start in range(0, length, TILE):
        at = slice(start, start + TILE)
        grad_key = turn(key_sum[at, :], cos_ref[at, :], -sin_ref[at, :])
        grad, gain = norm_grad(raw_ref[at, key_at:value_at], gain_ref[1:2, :], grad_key)
        out_ref[at, key_at:value_at] = grad.astype(bf16)
        key_gain += gain
        grad, _ = norm_grad(raw_ref[at, value_at:], 1.0, value_sum[at, :])
        out_ref[at, value_at:] = grad.astype(bf16)
    gain_out_ref[...] = jnp.concatenate([query_gain, key_gain])


def local_call(kernel, out_shape, flops, inputs, scratch=()):
    size = sum(math.prod(v.shape) * v.dtype.itemsize for v in [*inputs, *jax.tree.leaves(out_shape)])
    vmem = pl.BlockSpec(memory_space=pltpu.VMEM)
    return pl.pallas_call(
        kernel,
        out_shape=out_shape,
        in_specs=[vmem] * len(inputs),
        out_specs=[vmem] * len(out_shape),
        scratch_shapes=list(scratch),
        compiler_params=pltpu.CompilerParams(vmem_limit_bytes=40 * 2**20),
        cost_estimate=pl.CostEstimate(flops=flops, bytes_accessed=size, transcendentals=0),
    )(*inputs)


def attention(raw, cosine, sine, segments, head_scales):
    length, across = raw.shape
    tables = (cosine, sine, segments[:, None], segments[None, :], head_scales)
    heads = across // HEAD_DIM - 2
    return local_call(
        forward_kernel,
        [
            jax.ShapeDtypeStruct((length, heads * HEAD_DIM), bf16),
            jax.ShapeDtypeStruct((length, across), bf16),
        ],
        4 * heads * length * 2 * WINDOW * HEAD_DIM,
        (raw, *tables),
    )


def attention_back(raw, low, upstream, cosine, sine, segments, head_scales):
    length, across = raw.shape
    tables = (cosine, sine, segments[:, None], segments[None, :], head_scales)
    return local_call(
        backward_kernel,
        [jax.ShapeDtypeStruct((length, across), bf16), jax.ShapeDtypeStruct((2, HEAD_DIM), f32)],
        10 * upstream.shape[1] * length * 2 * WINDOW,
        (raw, low, upstream, *tables),
        [pltpu.VMEM((length, HEAD_DIM), f32)] * 2,
    )


def shards(
    tokens,
    layer_vectors,
    segment_ids,
    cotangent,
    norm_gains,
    head_gains,
    w_query,
    w_key,
    w_value,
    w_out,
    w_left,
    w_right,
    w_gate,
    w_up,
    w_down,
    w_layer_gate,
    w_layer_proj,
):
    ring = Ring()
    count = ring.count
    mine = lax.axis_index("mp")
    chip, core = mine // 2, mine % 2
    rows, width = tokens.shape
    length = segment_ids.shape[0]
    share = w_key.shape[0]
    rank = w_left.shape[1]
    layer_dim = w_layer_gate.shape[1]

    heads_part = head_gains.shape[0]
    packed = jnp.concatenate(
        [norm_gains, jnp.pad(head_gains, (0, norm_gains.shape[1] - heads_part))[None]]
    )
    packed = gather_small(packed, 1).astype(f32)
    gains = packed[:6]
    head_scales = packed[6].reshape(-1, norm_gains.shape[1])[:, :heads_part].reshape(2, HEAD_DIM)

    def in_order(slots):
        whole = jnp.zeros((4 * slots[0].shape[0], *slots[0].shape[1:]), slots[0].dtype)
        for slot, piece in enumerate(slots):
            whole = lax.dynamic_update_slice(whole, piece, ((mine ^ slot) * piece.shape[0], 0))
        return whole

    side = HEAD_DIM
    line = w_query.shape[1]
    fold = 2 * rank * share // line
    parts = [
        w_query,
        w_out.T,
        w_key,
        w_value,
        jnp.concatenate([w_layer_gate, w_layer_proj.T], axis=1),
        jnp.concatenate([w_left, w_right.T], axis=1).reshape(fold, line),
    ]
    first, hops = ring.gather(jnp.concatenate(parts))
    gate_up, hops = ring.gather(jnp.concatenate([w_gate, w_up], axis=1), hops[-3])
    down_t, _ = ring.gather(w_down.T, hops[-2])
    first = first.reshape(count, -1, line)
    starts = [sum(p.shape[0] for p in parts[:i]) for i in range(len(parts) + 1)]
    query_weight, out_t, key_part, value_part, layer_part, rank_part = (
        first[:, a:b] for a, b in zip(starts[:-1], starts[1:])
    )
    out_t = out_t.reshape(-1, line)

    def head_columns(value, head):
        return lax.dynamic_slice_in_dim(value, head * side, side, 2)

    def kv_of(head):
        return jnp.concatenate(
            [head_columns(key_part, head), head_columns(value_part, head)], axis=2
        )

    small_part = jnp.concatenate(
        [layer_part, rank_part.reshape(count, share, 2 * rank)], axis=2
    )

    def interleave(own, across):
        both = join(own[:, None], across[:, None], chip == 1, 1)[:, :, None]
        other = core_swap(both)
        return join(both, other, core == 1, 2).reshape(count * 4 * share, -1)

    mixture = interleave(
        jnp.concatenate([kv_of(chip), small_part], axis=2),
        chip_swap(jnp.concatenate([kv_of(1 - chip), small_part], axis=2)),
    )
    qkv_weight = jnp.concatenate(
        [query_weight.reshape(-1, line), mixture[:, : 2 * side]], axis=1
    )
    layer_gate_weight, layer_proj_weight, left_weight, right_weight = jnp.split(
        mixture[:, 2 * side :],
        [layer_dim, 2 * layer_dim, 2 * layer_dim + rank],
        axis=1,
    )

    token_all = in_order(gather_slots(tokens))
    inputs = tokens.astype(f32)
    vectors = layer_vectors.astype(f32)
    normed = rms_norm(inputs, gains[0])
    normed_low = normed.astype(bf16)
    normed_all = rms_norm(token_all.astype(f32), gains[0]).astype(bf16)
    qkv_raw = product(normed_all, qkv_weight)
    cosine, sine = rotary_tables(segment_ids)
    attended_low, qkv_low = attention(qkv_raw, cosine, sine, segment_ids, head_scales)

    def slot_rows(value, slot):
        return lax.dynamic_slice_in_dim(value, (mine ^ slot) * rows, rows, 0)

    attn = reduce_slots(
        lambda slot, i, pieces: product_right(
            slot_rows(attended_low, slot), rows_of(out_t, i, pieces)
        )
    )
    after_attn = inputs + rms_norm(attn, gains[1])
    left_low = product(normed_low, left_weight).astype(bf16)
    laurel_pre = product_right(left_low, right_weight)
    mixed = (after_attn + normed + rms_norm(laurel_pre, gains[2])) * root_half
    ff_in_all = jnp.concatenate(gather_slots(rms_norm(mixed, gains[3]).astype(bf16)))
    hidden_units = w_gate.shape[1]
    gate_pre = product(ff_in_all, gate_up[:, :hidden_units])
    up_pre = product(ff_in_all, gate_up[:, hidden_units:])
    hidden_low = geglu(gate_pre, up_pre).astype(bf16)
    ff_out = reduce_slots(
        lambda slot, i, pieces: product_right(
            rows_of(hidden_low, slot, 4), rows_of(down_t, i, pieces)
        )
    )
    after_ff = mixed + rms_norm(ff_out, gains[4])
    after_ff_low = after_ff.astype(bf16)
    layer_pre = product(after_ff_low, layer_gate_weight)
    layer_mix_low = geglu(layer_pre, vectors).astype(bf16)
    layer_out = product_right(layer_mix_low, layer_proj_weight)
    result = after_ff + rms_norm(layer_out, gains[5])

    upstream = cotangent.astype(f32)
    grad_layer_out, grad_gain_five = norm_back(layer_out, gains[5], upstream)
    grad_layer_out_low = grad_layer_out.astype(bf16)
    grad_layer_proj = product_left(grad_layer_out_low, layer_mix_low)
    grad_mix = product(grad_layer_out_low, layer_proj_weight)
    _, layer_pull = jax.vjp(geglu, layer_pre, vectors)
    grad_layer_pre, grad_vectors = layer_pull(grad_mix)
    grad_layer_pre_low = grad_layer_pre.astype(bf16)
    grad_layer_gate = product_left(after_ff_low, grad_layer_pre_low)
    grad_after_ff = upstream + product_right(grad_layer_pre_low, layer_gate_weight)
    grad_ff_out, grad_gain_four = norm_back(ff_out, gains[4], grad_after_ff)
    grad_ff_all = jnp.concatenate(gather_slots(grad_ff_out.astype(bf16)))
    grad_down_t, hops = ring.reduce(product_left(grad_ff_all, hidden_low).astype(bf16))
    grad_hidden = product(grad_ff_all, down_t)
    _, ff_pull = jax.vjp(geglu, gate_pre, up_pre)
    grad_gate, grad_up = ff_pull(grad_hidden)
    grad_gate_low = grad_gate.astype(bf16)
    grad_up_low = grad_up.astype(bf16)
    grad_gate_weight, gate_hops = ring.reduce(
        product_left(ff_in_all, grad_gate_low).astype(bf16), hops[-2]
    )
    grad_up_weight, up_hops = ring.reduce(
        product_left(ff_in_all, grad_up_low).astype(bf16), hops[-2]
    )
    grad_ff_in = reduce_slots(
        lambda slot, i, pieces: product_right(
            rows_of(grad_gate_low, slot, 4), rows_of(gate_up, i, pieces)[:, :hidden_units]
        )
        + product_right(
            rows_of(grad_up_low, slot, 4), rows_of(gate_up, i, pieces)[:, hidden_units:]
        )
    )
    grad_mixed_norm, grad_gain_three = norm_back(mixed, gains[3], grad_ff_in)
    grad_branch = (grad_after_ff + grad_mixed_norm) * root_half
    grad_laurel, grad_gain_two = norm_back(laurel_pre, gains[2], grad_branch)
    grad_laurel_low = grad_laurel.astype(bf16)
    grad_right = product_left(grad_laurel_low, left_low)
    grad_left_low = product(grad_laurel_low, right_weight).astype(bf16)
    grad_left = product_left(normed_low, grad_left_low)
    grad_attn, grad_gain_one = norm_back(attn, gains[1], grad_branch)
    grad_attn_all = in_order(gather_slots(grad_attn.astype(bf16)))
    grad_attended_low = product(grad_attn_all, out_t).astype(bf16)
    grad_qkv_low, head_grads = attention_back(
        qkv_raw, qkv_low, grad_attended_low, cosine, sine, segment_ids, head_scales
    )

    def pick(value, index, axis):
        return lax.dynamic_index_in_dim(value, index, axis, keepdims=False)

    small_partial = jnp.concatenate(
        [grad_layer_gate, grad_layer_proj, grad_left, grad_right], axis=1
    ).astype(bf16)
    small_partial = small_partial.reshape(count, 2, 2, share, -1)
    small_sum = pick(small_partial, core, 2).astype(f32) + core_swap(
        pick(small_partial, 1 - core, 2)
    )
    small_sum = pick(small_sum, chip, 1) + chip_swap(pick(small_sum, 1 - chip, 1).astype(bf16))
    small_sum = small_sum.astype(bf16)
    out_grad = product_left(grad_attn_all, attended_low).astype(bf16)
    second = jnp.concatenate(
        [
            out_grad.reshape(count, -1, line),
            small_sum[:, :, : 2 * layer_dim],
            small_sum[:, :, 2 * layer_dim :].reshape(count, fold, line),
        ],
        axis=1,
    )
    second, hops = ring.reduce(second.reshape(-1, line), gate_hops[-2] + up_hops[-2])
    out_rows = width // count
    grad_out = second[:out_rows].T
    grad_layer_gate_weight = second[out_rows : out_rows + share, :layer_dim]
    grad_layer_proj_weight = second[out_rows : out_rows + share, layer_dim:].T
    grad_rank = second[out_rows + share :].reshape(share, 2 * rank)
    grad_left_weight = grad_rank[:, :rank]
    grad_right_weight = grad_rank[:, rank:].T

    qkv_grad = product_left(normed_all, grad_qkv_low).astype(bf16)
    kv_partial = qkv_grad[:, line:].reshape(count, 2, 2, share, 2 * side)
    kv_sum = pick(kv_partial, core, 2).astype(f32) + core_swap(pick(kv_partial, 1 - core, 2))
    third = jnp.concatenate(
        [
            qkv_grad[:, :line].reshape(count, -1, line),
            kv_sum.astype(bf16).reshape(count, 2 * share, 2 * side),
        ],
        axis=1,
    )
    third, _ = ring.reduce(third.reshape(-1, line), hops[-2])
    grad_query_weight = third[:out_rows]
    kv_sum = third[out_rows:].reshape(2, share, 2 * side)
    kv_mine = pick(kv_sum, chip, 0)
    kv_other = chip_swap(pick(kv_sum, 1 - chip, 0).astype(bf16)).astype(f32)
    grad_key_weight = join(kv_mine[:, :side], kv_other[:, :side], chip == 1, 1)
    grad_value_weight = join(kv_mine[:, side:], kv_other[:, side:], chip == 1, 1)

    grad_normed_heads = reduce_slots(
        lambda slot, i, pieces: product_right(
            slot_rows(grad_qkv_low, slot), rows_of(qkv_weight, i, pieces)
        )
    )
    grad_normed = grad_branch + product_right(grad_left_low, left_weight) + grad_normed_heads
    grad_inputs_norm, grad_gain_zero = norm_back(inputs, gains[0], grad_normed)
    grad_inputs = grad_branch + grad_inputs_norm
    head_grads = head_grads.reshape(-1)
    gain_grads = jnp.stack(
        [
            grad_gain_zero,
            grad_gain_one,
            grad_gain_two,
            grad_gain_three,
            grad_gain_four,
            grad_gain_five,
            jnp.pad(head_grads, (0, width - head_grads.shape[0])),
        ]
    )
    gain_grads = sum_small(gain_grads)
    device = lax.axis_index("dp") * 4 + mine
    part = norm_gains.shape[1]
    grad_norm_gains = lax.dynamic_slice_in_dim(gain_grads[:6], device * part, part, 1)
    grad_head_gains = lax.dynamic_slice_in_dim(gain_grads[6], device * heads_part, heads_part, 0)
    return (
        result.astype(bf16),
        grad_inputs.astype(bf16),
        grad_vectors.astype(bf16),
        grad_norm_gains,
        grad_head_gains,
        grad_query_weight,
        grad_key_weight,
        grad_value_weight,
        grad_out,
        grad_left_weight,
        grad_right_weight,
        grad_gate_weight,
        grad_up_weight,
        grad_down_t.T,
        grad_layer_gate_weight,
        grad_layer_proj_weight,
    )


def solution(mesh):
    both = ("dp", "mp")
    in_specs = (
        P(both, None),
        P(both, None),
        P("dp"),
        P(both, None),
        P(None, both),
        P(both),
        P("dp", "mp"),
        P(both, None),
        P(both, None),
        P("mp", "dp"),
        P(both, None),
        P(None, both),
        P("dp", "mp"),
        P("dp", "mp"),
        P("mp", "dp"),
        P(both, None),
        P(None, both),
    )
    out_specs = (
        P(both, None),
        P(both, None),
        P(both, None),
        P(None, both),
        P(both),
        P("dp", "mp"),
        P(both, None),
        P(both, None),
        P("mp", "dp"),
        P(both, None),
        P(None, both),
        P("dp", "mp"),
        P("dp", "mp"),
        P("mp", "dp"),
        P(both, None),
        P(None, both),
    )
    return jax.shard_map(shards, mesh=mesh, in_specs=in_specs, out_specs=out_specs, check_vma=False)
```

time: 2800 us -> 1030 us (0.37)
  waiting for transfers between devices: 2170 us -> 424 us
  blocking collectives: 202 us -> 0 us
  starting transfers between devices: 1.56 us -> 114 us
  local copies, waits for them, and re-layouts: 54.6 us -> 139 us
    reduce_scatter x14 -> x0, waiting for transfers between devices: 1310 us -> none  [the longest x1 149 us: shards(): lax.psum_scatter(grad_up_weight.astype(jnp.bfloat16), 'dp', scatter_dimen...]
    all_gather x13 -> x0, waiting for transfers between devices: 637 us -> none  [the longest x1 113 us: shards(): lax.all_gather(w_up, 'dp', axis=0, tiled=True)]
    ppermute x0 -> x116, waiting for transfers between devices: none -> 424 us  [the longest x32 214 us: up(): return lax.ppermute(value, 'dp', self.ahead)]
    unnamed x31 -> x0, waiting for transfers between devices: 226 us -> none
    all_gather x3 -> x0, blocking collectives: 124 us -> none  [the longest x1 43.8 us: shards(): lax.all_gather(norm_gains, ('dp', 'mp'), axis=1, tiled=True)]
    ppermute x0 -> x116, starting transfers between devices: none -> 114 us  [the longest x32 54.8 us: up(): return lax.ppermute(value, 'dp', self.ahead)]
    unnamed x2 -> x0, blocking collectives: 77.8 us -> none
    dynamic_update_slice x6 -> x34, local copies, waits for them, and re-layouts: 9.19 us -> 64.7 us  [the longest x27 49.6 us: put(): lax.dynamic_update_slice(whole, piece, (self.member(offset) * size + inne...]
  transfers between devices with their start and end apart: 29 -> 116, of which waited for: 26 -> 50; matrix products, arithmetic and copies ran while one was open for 7% -> 36% of each run, Pallas kernels for 0% -> 1%
where the time goes in v1:
time: 1030 us; the launch traced here: 1020 us
  waiting for transfers between devices  424 us (41%)
  matrix products  241 us (23%)
  local copies, waits for them, and re-layouts  139 us (13%)
  starting transfers between devices  114 us (11%)
  other arithmetic  85.8 us (8%)
  Pallas kernels  12.4 us (1%)
    ppermute x32, waiting for transfers between devices, up(): return lax.ppermute(value, 'dp', self.ahead)  214 us
    dot_general x44, matrix products, product_right(): lax.dot_general(left, right, (((1,), (1,)), ((), ())), preferred_element_...  116 us
    ppermute x17, waiting for transfers between devices, chip_swap(): return lax.ppermute(value, 'mp', [(0, 2), (2, 0), (1, 3), (3, 1)])  105 us
    ppermute x32, waiting for transfers between devices, down(): return lax.ppermute(value, 'dp', self.behind)  75.8 us
    dot_general x9, matrix products, product(): return jnp.dot(left, right, preferred_element_type=f32)  71.8 us
    ppermute x32, starting transfers between devices, up(): return lax.ppermute(value, 'dp', self.ahead)  54.8 us
    dot_general x9, matrix products, product_left(): lax.dot_general(left, right, (((0,), (0,)), ((), ())), preferred_element_...  53.9 us
    dynamic_update_slice x27, local copies, waits for them, and re-layouts, put(): lax.dynamic_update_slice(whole, piece, (self.member(offset) * size + inne...  49.6 us
  transfers between devices with their start and end apart: 116, of which 50 were waited for; matrix products, arithmetic and copies ran while one was open for 36% of the time, Pallas kernels for 1%

profile of v1, /device:TPU:0, one launch (start us, length us, event | category | flops | bytes accessed | tf_op | source)
XLA Modules:
  0.0 1020.1 jit_solution(16055330903833134902)
XLA Ops:
  23.9 12.2 %collective-permute-done.4 = bf16[7,128]{1,0:T(8,128)(2,1)S(1)} collective-permute-done((bf16[7,128]{1,0:T(8,128)(2,1)S(1)}, bf16[7,128]{1,0:T(8,128)(2,1)S(1)}, u32[]{:S(2)}, u32[]{:S(2)}) %collective-permute-start.4) | collective-permute-done | bytes 1824 | tf_op jit(solution)/shard_map/ppermute | solution.py:64
  87.5 43.0 %collective-permute-done.14 = bf16[352,512]{1,0:T(8,128)(2,1)S(1)} collective-permute-done((bf16[352,512]{1,0:T(8,128)(2,1)S(1)}, bf16[352,512]{1,0:T(8,128)(2,1)S(1)}, u32[]{:S(2)}, u32[]{:S(2)}) %collective-permute-start.14) | collective-permute-done | bytes 360480 | tf_op jit(solution)/shard_map/ppermute | solution.py:82
  182.2 24.5 %collective-permute-done.29 = bf16[256,4096]{1,0:T(8,128)(2,1)} collective-permute-done((bf16[256,4096]{1,0:T(8,128)(2,1)}, bf16[256,4096]{1,0:T(8,128)(2,1)}, u32[]{:S(2)}, u32[]{:S(2)}) %collective-permute-start.29) | collective-permute-done | bytes 2097184 | tf_op jit(solution)/shard_map/ppermute | solution.py:82
  217.3 9.0 fusion.14.raw_ref
  238.0 11.6 %collective-permute-done.20 = bf16[256,1024]{1,0:T(8,128)(2,1)S(1)} collective-permute-done((bf16[256,1024]{1,0:T(8,128)(2,1)S(1)}, bf16[256,1024]{1,0:T(8,128)(2,1)S(1)}, u32[]{:S(2)}, u32[]{:S(2)}) %collective-permute-start.20) | collective-permute-done | bytes 524320 | tf_op jit(solution)/shard_map/ppermute | solution.py:64
  250.1 9.9 collective-permute-done.23
  294.5 17.8 %collective-permute-done.33 = bf16[128,4096]{1,0:T(8,128)(2,1)S(1)} collective-permute-done((bf16[128,4096]{1,0:T(8,128)(2,1)S(1)}, bf16[128,4096]{1,0:T(8,128)(2,1)S(1)}, u32[]{:S(2)}, u32[]{:S(2)}) %collective-permute-start.33) | collective-permute-done | bytes 1048608 | tf_op jit(solution)/shard_map/ppermute | solution.py:82
  315.7 14.0 %fusion.12 = f32[1024,2048]{1,0:T(8,128)} fusion(bf16[2048,4096]{1,0:T(8,128)(2,1)} %constant_dynamic-update-slice_fusion.13, bf16[256,2048]{1,0:T(8,128)(2,1)S(1)} %collective-permute-done.26, bf16[256,2048]{1,0:T(8,128)(2,1)S(1)} %collective-permute-done.25, bf16[256,2048]{1,0:T(8,128)(2,1)S(1)} %collective-permute-done.24, ...), kind=kOutput, calls=%fused_computation.16 | convolution fusion | flops 8606711808 | bytes 20971520 | tf_op jit(solution)/shard_map/dot_general | solution.py:34
  334.9 19.3 %multiply_convert_fusion.1 = (bf16[1024,2048]{1,0:T(8,128)(2,1)}, f32[1024,2048]{1,0:T(8,128)}) fusion(f32[1024,2048]{1,0:T(8,128)} %fusion.12, bf16[2048,4096]{1,0:T(8,128)(2,1)} %constant_dynamic-update-slice_fusion.13, bf16[256,2048]{1,0:T(8,128)(2,1)} %copy-done.91, bf16[256,2048]{1,0:T(8,128)(2,1)} %copy-done.85, bf16[256,2048]{1,0:T(8,128)(2,1)} %copy-done.88, ...), kind=kOutput, calls=%fused_computation.19 | convolution fusion | flops 8627683328 | bytes 33554432 | tf_op jit(solution)/shard_map/dot_general | solution.py:34
  429.0 23.4 %collective-permute-done.50 = bf16[256,2048]{1,0:T(8,128)(2,1)} collective-permute-done((bf16[256,2048]{1,0:T(8,128)(2,1)S(1)}, bf16[256,2048]{1,0:T(8,128)(2,1)}, u32[]{:S(2)}, u32[]{:S(2)}) %collective-permute-start.50) | collective-permute-done | bytes 1048608 | tf_op jit(solution)/shard_map/ppermute | solution.py:64
  461.3 23.4 %fusion.9 = (bf16[1024,2048]{1,0:T(8,128)(2,1)}, bf16[1024,2048]{1,0:T(8,128)(2,1)}) fusion(f32[1024,2048]{1,0:T(8,128)} %fusion.12, f32[1024,2048]{1,0:T(8,128)} %get-tuple-element.174, bf16[2048,2048]{0,1:T(8,128)(2,1)} %constant_dynamic-update-slice_fusion.4, bf16[256,2048]{1,0:T(8,128)(2,1)} %copy-done.96, ...), kind=kOutput, calls=%fused_computation.13 | convolution fusion | flops 8657043456 | bytes 37748736 | tf_op jit(solution)/shard_map/dot_general | solution.py:34
  516.5 10.9 %convolution_convert_fusion.1 = bf16[2048,2048]{1,0:T(8,128)(2,1)S(1)} fusion(bf16[1024,2048]{1,0:T(8,128)(2,1)S(1)} %copy-done.102, bf16[256,2048]{1,0:T(8,128)(2,1)S(1)} %copy-done.97, bf16[256,2048]{1,0:T(8,128)(2,1)} %collective-permute-done.50, bf16[256,2048]{1,0:T(8,128)(2,1)S(1)} %copy-done.95, bf16[256,2048]{1,0:T(8,128)(2,1)S(1)} %fusion.75), kind=kOutput, calls=%fused_computation.22 | convolution fusion | flops 8610906112 | bytes 16777216 | tf_op jit(solution)/shard_map/dot_general | solution.py:38
  542.7 13.6 %convolution_convert_fusion = bf16[2048,2048]{1,0:T(8,128)(2,1)} fusion(bf16[1024,2048]{1,0:T(8,128)(2,1)} %get-tuple-element.104, bf16[256,2048]{1,0:T(8,128)(2,1)S(1)} %copy-done.92, bf16[256,2048]{1,0:T(8,128)(2,1)S(1)} %copy-done.86, bf16[256,2048]{1,0:T(8,128)(2,1)S(1)} %copy-done.89, bf16[256,2048]{1,0:T(8,128)(2,1)S(1)} %copy-done.49), kind=kOutput, calls=%fused_computation.21 | convolution fusion | flops 8610906112 | bytes 16777216 | tf_op jit(solution)/shard_map/dot_general | solution.py:38
  574.9 9.2 collective-permute-done.54
  624.9 11.4 %convolution_convert_fusion.2 = bf16[2048,2048]{1,0:T(8,128)(2,1)} fusion(bf16[1024,2048]{1,0:T(8,128)(2,1)S(1)} %copy-done.100, bf16[256,2048]{1,0:T(8,128)(2,1)S(1)} %copy-done.93, bf16[256,2048]{1,0:T(8,128)(2,1)S(1)} %copy-done.87, bf16[256,2048]{1,0:T(8,128)(2,1)S(1)} %copy-done.90, bf16[256,2048]{1,0:T(8,128)(2,1)S(1)} %copy-done.50), kind=kOutput, calls=%fused_computation.23 | convolution fusion | flops 8610906112 | bytes 16777216 | tf_op jit(solution)/shard_map/dot_general | solution.py:38
  701.7 9.4 collective-permute-done.90
  749.7 17.0 %collective-permute-done.85 = bf16[256,2048]{1,0:T(8,128)(2,1)S(1)} collective-permute-done((bf16[256,2048]{1,0:T(8,128)(2,1)S(1)}, bf16[256,2048]{1,0:T(8,128)(2,1)S(1)}, u32[]{:S(2)}, u32[]{:S(2)}) %collective-permute-start.85) | collective-permute-done | bytes 1048608 | tf_op jit(solution)/shard_map/ppermute | solution.py:85
  774.1 18.7 %collective-permute-done.88 = bf16[256,2048]{1,0:T(8,128)(2,1)S(1)} collective-permute-done((bf16[256,2048]{1,0:T(8,128)(2,1)S(1)}, bf16[256,2048]{1,0:T(8,128)(2,1)S(1)}, u32[]{:S(2)}, u32[]{:S(2)}) %collective-permute-start.88) | collective-permute-done | bytes 1048608 | tf_op jit(solution)/shard_map/ppermute | solution.py:82
  795.8 19.4 %collective-permute-done.82 = bf16[256,2048]{1,0:T(8,128)(2,1)S(1)} collective-permute-done((bf16[256,2048]{1,0:T(8,128)(2,1)S(1)}, bf16[256,2048]{1,0:T(8,128)(2,1)S(1)}, u32[]{:S(2)}, u32[]{:S(2)}) %collective-permute-start.82) | collective-permute-done | bytes 1048608 | tf_op jit(solution)/shard_map/ppermute | solution.py:82
  839.0 21.3 %collective-permute-done.83 = bf16[256,2048]{1,0:T(8,128)(2,1)} collective-permute-done((bf16[256,2048]{1,0:T(8,128)(2,1)}, bf16[256,2048]{1,0:T(8,128)(2,1)}, u32[]{:S(2)}, u32[]{:S(2)}) %collective-permute-start.83) | collective-permute-done | bytes 1048608 | tf_op jit(solution)/shard_map/ppermute | solution.py:82
  863.4 19.2 %collective-permute-done.69 = f32[7,2048]{1,0:T(8,128)S(1)} collective-permute-done((f32[7,2048]{1,0:T(8,128)S(1)}, f32[7,2048]{1,0:T(8,128)S(1)}, u32[]{:S(2)}, u32[]{:S(2)}) %collective-permute-start.69) | collective-permute-done | bytes 57376 | tf_op jit(solution)/shard_map/ppermute | solution.py:168
  922.8 13.6 %collective-permute-done.99 = bf16[192,512]{1,0:T(8,128)(2,1)} collective-permute-done((bf16[192,512]{1,0:T(8,128)(2,1)}, bf16[192,512]{1,0:T(8,128)(2,1)}, u32[]{:S(2)}, u32[]{:S(2)}) %collective-permute-start.99) | collective-permute-done | bytes 196640 | tf_op jit(solution)/shard_map/ppermute | solution.py:82
  959.2 10.3 %collective-permute-done.103 = bf16[192,512]{1,0:T(8,128)(2,1)S(1)} collective-permute-done((bf16[192,512]{1,0:T(8,128)(2,1)S(1)}, bf16[192,512]{1,0:T(8,128)(2,1)S(1)}, u32[]{:S(2)}, u32[]{:S(2)}) %collective-permute-start.103) | collective-permute-done | bytes 196640 | tf_op jit(solution)/shard_map/ppermute | solution.py:85
  969.7 8.5 collective-permute-done.101
  (700 shorter events, 626.5 us)
Async XLA Ops:
  10.0 55.8 %collective-permute-start = (bf16[256,2048]{1,0:T(8,128)(2,1)}, bf16[256,2048]{1,0:T(8,128)(2,1)}, u32[]{:S(2)}, u32[]{:S(2)}) collective-permute-start(bf16[256,2048]{1,0:T(8,128)(2,1)} %param.17), channel_id=1, source_target_pairs={{0,1},{1,0},{2,3},{3,2},{4,5},{5,4},{6,7},{7,6},{8,9},{9,8},{10,11... | collective-permute-start | bytes 3145736 | tf_op jit(solution)/shard_map/ppermute | solution.py:60
  10.0 54.3 %collective-permute-start.1 = (bf16[256,2048]{1,0:T(8,128)(2,1)}, bf16[256,2048]{1,0:T(8,128)(2,1)}, u32[]{:S(2)}, u32[]{:S(2)}) collective-permute-start(bf16[256,2048]{1,0:T(8,128)(2,1)} %param.17), channel_id=1, source_target_pairs={{0,2},{2,0},{1,3},{3,1},{4,6},{6,4},{5,7},{7,5},{8,10},{10,8},{9,1... | collective-permute-start | bytes 3145736 | tf_op jit(solution)/shard_map/ppermute | solution.py:64
  64.3 89.7 %collective-permute-start.2 = (bf16[256,2048]{1,0:T(8,128)(2,1)}, bf16[256,2048]{1,0:T(8,128)(2,1)}, u32[]{:S(2)}, u32[]{:S(2)}) collective-permute-start(bf16[256,2048]{1,0:T(8,128)(2,1)} %collective-permute-done.1), channel_id=1, source_target_pairs={{0,1},{1,0},{2,3},{3,2},{4,5},{5,4},{6,7},{7,6},{8,9},{9,8},{10,11... | collective-permute-start | bytes 3145736 | tf_op jit(solution)/shard_map/ppermute | solution.py:60
  70.5 88.9 %collective-permute-start.27 = (bf16[256,4096]{1,0:T(8,128)(2,1)}, bf16[256,4096]{1,0:T(8,128)(2,1)}, u32[]{:S(2)}, u32[]{:S(2)}) collective-permute-start(bf16[256,4096]{1,0:T(8,128)(2,1)} %pad_maximum_fusion.8), channel_id=1, source_target_pairs={{0,8},{8,16},{16,24},{24,28},{28,20},{20,12},{12,4},{4,0},{1,9},{9... | collective-permute-start | bytes 6291464 | tf_op jit(solution)/shard_map/ppermute | solution.py:82
  71.0 90.7 %collective-permute-start.28 = (bf16[256,4096]{1,0:T(8,128)(2,1)}, bf16[256,4096]{1,0:T(8,128)(2,1)}, u32[]{:S(2)}, u32[]{:S(2)}) collective-permute-start(bf16[256,4096]{1,0:T(8,128)(2,1)} %pad_maximum_fusion.8), channel_id=1, source_target_pairs={{8,0},{16,8},{24,16},{28,24},{20,28},{12,20},{4,12},{0,4},{9,1},{1... | collective-permute-start | bytes 6291464 | tf_op jit(solution)/shard_map/ppermute | solution.py:85
  81.4 49.1 %collective-permute-start.14 = (bf16[352,512]{1,0:T(8,128)(2,1)S(1)}, bf16[352,512]{1,0:T(8,128)(2,1)S(1)}, u32[]{:S(2)}, u32[]{:S(2)}) collective-permute-start(bf16[352,512]{1,0:T(8,128)(2,1)S(1)} %slice.344), channel_id=1, source_target_pairs={{0,8},{8,16},{16,24},{24,28},{28,20},{20,12},{12,4},{4,0},{1,9},{9... | collective-permute-start | bytes 1081352 | tf_op jit(solution)/shard_map/ppermute | solution.py:82
  84.0 52.4 %collective-permute-start.15 = (bf16[368,512]{1,0:T(8,128)(2,1)S(1)}, bf16[368,512]{1,0:T(8,128)(2,1)S(1)}, u32[]{:S(2)}, u32[]{:S(2)}) collective-permute-start(bf16[368,512]{1,0:T(8,128)(2,1)S(1)} %slice.345), channel_id=1, source_target_pairs={{8,0},{16,8},{24,16},{28,24},{20,28},{12,20},{4,12},{0,4},{9,1},{1... | collective-permute-start | bytes 1130504 | tf_op jit(solution)/shard_map/ppermute | solution.py:85
  159.4 47.3 %collective-permute-start.29 = (bf16[256,4096]{1,0:T(8,128)(2,1)}, bf16[256,4096]{1,0:T(8,128)(2,1)}, u32[]{:S(2)}, u32[]{:S(2)}) collective-permute-start(bf16[256,4096]{1,0:T(8,128)(2,1)} %collective-permute-done.27), channel_id=1, source_target_pairs={{0,8},{8,16},{16,24},{24,28},{28,20},{20,12},{12,4},{4,0},{1,9},{9... | collective-permute-start | bytes 6291464 | tf_op jit(solution)/shard_map/ppermute | solution.py:82
  161.7 47.5 %collective-permute-start.30 = (bf16[256,4096]{1,0:T(8,128)(2,1)}, bf16[256,4096]{1,0:T(8,128)(2,1)}, u32[]{:S(2)}, u32[]{:S(2)}) collective-permute-start(bf16[256,4096]{1,0:T(8,128)(2,1)} %collective-permute-done.28), channel_id=1, source_target_pairs={{8,0},{16,8},{24,16},{28,24},{20,28},{12,20},{4,12},{0,4},{9,1},{1... | collective-permute-start | bytes 6291464 | tf_op jit(solution)/shard_map/ppermute | solution.py:85
  206.7 57.0 %collective-permute-start.31 = (bf16[256,4096]{1,0:T(8,128)(2,1)}, bf16[256,4096]{1,0:T(8,128)(2,1)}, u32[]{:S(2)}, u32[]{:S(2)}) collective-permute-start(bf16[256,4096]{1,0:T(8,128)(2,1)} %collective-permute-done.29), channel_id=1, source_target_pairs={{0,8},{8,16},{16,24},{24,28},{28,20},{20,12},{12,4},{4,0},{1,9},{9... | collective-permute-start | bytes 6291464 | tf_op jit(solution)/shard_map/ppermute | solution.py:82
  209.2 54.5 %collective-permute-start.32 = (bf16[256,4096]{1,0:T(8,128)(2,1)}, bf16[256,4096]{1,0:T(8,128)(2,1)}, u32[]{:S(2)}, u32[]{:S(2)}) collective-permute-start(bf16[256,4096]{1,0:T(8,128)(2,1)} %collective-permute-done.30), channel_id=1, source_target_pairs={{8,0},{16,8},{24,16},{28,24},{20,28},{12,20},{4,12},{0,4},{9,1},{1... | collective-permute-start | bytes 6291464 | tf_op jit(solution)/shard_map/ppermute | solution.py:85
  267.1 45.2 %collective-permute-start.33 = (bf16[128,4096]{1,0:T(8,128)(2,1)S(1)}, bf16[128,4096]{1,0:T(8,128)(2,1)S(1)}, u32[]{:S(2)}, u32[]{:S(2)}) collective-permute-start(bf16[128,4096]{1,0:T(8,128)(2,1)S(1)} %slice.359), channel_id=1, source_target_pairs={{0,8},{8,16},{16,24},{24,28},{28,20},{20,12},{12,4},{4,0},{1,9},{9... | collective-permute-start | bytes 3145736 | tf_op jit(solution)/shard_map/ppermute | solution.py:82
  528.8 90.6 %collective-permute-start.75 = (bf16[128,2048]{1,0:T(8,128)(2,1)}, bf16[128,2048]{1,0:T(8,128)(2,1)}, u32[]{:S(2)}, u32[]{:S(2)}) collective-permute-start(bf16[128,2048]{1,0:T(8,128)(2,1)} %get-tuple-element.122), channel_id=1, source_target_pairs={{0,8},{8,16},{16,24},{24,28},{28,20},{20,12},{12,4},{4,0},{1,9},{9... | collective-permute-start | bytes 1572872 | tf_op jit(solution)/shard_map/ppermute | solution.py:82
  542.3 45.5 %collective-permute-start.55 = (bf16[256,1024]{1,0:T(8,128)(2,1)S(1)}, bf16[256,1024]{1,0:T(8,128)(2,1)S(1)}, u32[]{:S(2)}, u32[]{:S(2)}) collective-permute-start(bf16[256,1024]{1,0:T(8,128)(2,1)S(1)} %fusion.158), channel_id=1, source_target_pairs={{0,1},{1,0},{2,3},{3,2},{4,5},{5,4},{6,7},{7,6},{8,9},{9,8},{10,11... | collective-permute-start | bytes 1572872 | tf_op jit(solution)/shard_map/ppermute | solution.py:60
  565.4 54.0 %collective-permute-start.79 = (bf16[256,2048]{1,0:T(8,128)(2,1)}, bf16[256,2048]{1,0:T(8,128)(2,1)}, u32[]{:S(2)}, u32[]{:S(2)}) collective-permute-start(bf16[256,2048]{1,0:T(8,128)(2,1)} %add_convert_fusion.15), channel_id=1, source_target_pairs={{8,0},{16,8},{24,16},{28,24},{20,28},{12,20},{4,12},{0,4},{9,1},{1... | collective-permute-start | bytes 3145736 | tf_op jit(solution)/shard_map/ppermute | solution.py:85
  636.4 57.7 %collective-permute-start.80 = (bf16[256,2048]{1,0:T(8,128)(2,1)}, bf16[256,2048]{1,0:T(8,128)(2,1)}, u32[]{:S(2)}, u32[]{:S(2)}) collective-permute-start(bf16[256,2048]{1,0:T(8,128)(2,1)} %get-tuple-element.119), channel_id=1, source_target_pairs={{8,0},{16,8},{24,16},{28,24},{20,28},{12,20},{4,12},{0,4},{9,1},{1... | collective-permute-start | bytes 3145736 | tf_op jit(solution)/shard_map/ppermute | solution.py:85
  714.1 55.9 %collective-permute-start.61 = (bf16[256,1024]{1,0:T(8,128)(2,1)}, bf16[256,1024]{1,0:T(8,128)(2,1)}, u32[]{:S(2)}, u32[]{:S(2)}) collective-permute-start(bf16[256,1024]{1,0:T(8,128)(2,1)} %convolution_convert_fusion.17), channel_id=1, source_target_pairs={{0,1},{1,0},{2,3},{3,2},{4,5},{5,4},{6,7},{7,6},{8,9},{9,8},{10,11... | collective-permute-start | bytes 1572872 | tf_op jit(solution)/shard_map/ppermute | solution.py:60
  770.0 45.2 %collective-permute-start.82 = (bf16[256,2048]{1,0:T(8,128)(2,1)S(1)}, bf16[256,2048]{1,0:T(8,128)(2,1)S(1)}, u32[]{:S(2)}, u32[]{:S(2)}) collective-permute-start(bf16[256,2048]{1,0:T(8,128)(2,1)S(1)} %get-tuple-element.116), channel_id=1, source_target_pairs={{0,8},{8,16},{16,24},{24,28},{28,20},{20,12},{12,4},{4,0},{1,9},{9... | collective-permute-start | bytes 3145736 | tf_op jit(solution)/shard_map/ppermute | solution.py:82
  773.1 54.8 %collective-permute-start.92 = (bf16[256,2048]{1,0:T(8,128)(2,1)}, bf16[256,2048]{1,0:T(8,128)(2,1)}, u32[]{:S(2)}, u32[]{:S(2)}) collective-permute-start(bf16[256,2048]{1,0:T(8,128)(2,1)} %get-tuple-element.111), channel_id=1, source_target_pairs={{8,0},{16,8},{24,16},{28,24},{20,28},{12,20},{4,12},{0,4},{9,1},{1... | collective-permute-start | bytes 3145736 | tf_op jit(solution)/shard_map/ppermute | solution.py:85
  773.6 56.0 %collective-permute-start.86 = (bf16[256,2048]{1,0:T(8,128)(2,1)}, bf16[256,2048]{1,0:T(8,128)(2,1)}, u32[]{:S(2)}, u32[]{:S(2)}) collective-permute-start(bf16[256,2048]{1,0:T(8,128)(2,1)} %get-tuple-element.115), channel_id=1, source_target_pairs={{8,0},{16,8},{24,16},{28,24},{20,28},{12,20},{4,12},{0,4},{9,1},{1... | collective-permute-start | bytes 3145736 | tf_op jit(solution)/shard_map/ppermute | solution.py:85
  827.9 54.9 %collective-permute-start.72 = (bf16[8,2,64,512]{3,2,1,0:T(8,128)(2,1)S(1)}, bf16[8,2,64,512]{3,2,1,0:T(8,128)(2,1)S(1)}, u32[]{:S(2)}, u32[]{:S(2)}) collective-permute-start(bf16[8,2,64,512]{3,2,1,0:T(8,128)(2,1)S(1)} %dynamic-slice_bitcast_fusion.1), channel_id=1, source_target_pairs={{0,1},{1,0},{2,3},{3,2},{4,5},{5,4},{6,7},{7,6},{8,9},{9,8},{10,11... | collective-permute-start | bytes 3145736 | tf_op jit(solution)/shard_map/ppermute | solution.py:60
  827.9 88.9 %collective-permute-start.114 = (bf16[256,2048]{1,0:T(8,128)(2,1)S(1)}, bf16[256,2048]{1,0:T(8,128)(2,1)S(1)}, u32[]{:S(2)}, u32[]{:S(2)}) collective-permute-start(bf16[256,2048]{1,0:T(8,128)(2,1)S(1)} %get-tuple-element.105), channel_id=1, source_target_pairs={{0,8},{8,16},{16,24},{24,28},{28,20},{20,12},{12,4},{4,0},{1,9},{9... | collective-permute-start | bytes 3145736 | tf_op jit(solution)/shard_map/ppermute | solution.py:82
  829.6 87.3 %collective-permute-start.115 = (bf16[256,2048]{1,0:T(8,128)(2,1)S(1)}, bf16[256,2048]{1,0:T(8,128)(2,1)S(1)}, u32[]{:S(2)}, u32[]{:S(2)}) collective-permute-start(bf16[256,2048]{1,0:T(8,128)(2,1)S(1)} %get-tuple-element.106), channel_id=1, source_target_pairs={{8,0},{16,8},{24,16},{28,24},{20,28},{12,20},{4,12},{0,4},{9,1},{1... | collective-permute-start | bytes 3145736 | tf_op jit(solution)/shard_map/ppermute | solution.py:85
  837.8 44.8 %collective-permute-start.69 = (f32[7,2048]{1,0:T(8,128)S(1)}, f32[7,2048]{1,0:T(8,128)S(1)}, u32[]{:S(2)}, u32[]{:S(2)}) collective-permute-start(f32[7,2048]{1,0:T(8,128)S(1)} %add.1020), channel_id=1, source_target_pairs={{0,4},{4,0},{8,12},{12,8},{16,20},{20,16},{24,28},{28,24},{1,5},{5... | collective-permute-start | bytes 172040 | tf_op jit(solution)/shard_map/ppermute | solution.py:168
  (209 other events, 4119.0 us)

commit v2 on v1

v2 whole, which is shorter than its diff:
```python
import math

import jax
import jax.numpy as jnp
from jax import lax
from jax.experimental import pallas as pl
from jax.experimental.pallas import tpu as pltpu
from jax.sharding import PartitionSpec as P

HEAD_DIM = 256
WINDOW = 512

epsilon = 1e-06
root_half = 1.0 / math.sqrt(2.0)
masked_score = -1e30
bf16 = jnp.bfloat16
f32 = jnp.float32


light = pl.CostEstimate(flops=1, bytes_accessed=1, transcendentals=0)


def rms_norm(values, scales):
    return values * lax.rsqrt(jnp.mean(values * values, axis=-1, keepdims=True) + epsilon) * scales


def norm_back(values, scales, upstream):
    _, pullback = jax.vjp(rms_norm, values, scales)
    return pullback(upstream)


def geglu(gate_pre, other):
    return jax.nn.gelu(gate_pre, approximate=True) * other


def product(left, right):
    return jnp.dot(left, right, preferred_element_type=f32)


def product_left(left, right):
    return lax.dot_general(left, right, (((0,), (0,)), ((), ())), preferred_element_type=f32)


def product_right(left, right):
    return lax.dot_general(left, right, (((1,), (1,)), ((), ())), preferred_element_type=f32)


def rotary_tables(segments):
    length = segments.shape[0]
    half = HEAD_DIM // 2
    places = jnp.arange(length, dtype=jnp.int32)
    starts = jnp.sum((segments[None, :] < segments[:, None]).astype(jnp.int32), axis=1)
    frequency = jnp.exp(jnp.arange(half, dtype=f32) * (-2.0 * math.log(10000.0) / HEAD_DIM))
    angle = (places - starts).astype(f32)[:, None] * frequency[None, :]
    return jnp.cos(angle), jnp.sin(angle)


def sync(value):
    return lax.optimization_barrier(value)


def core_swap(value):
    return lax.ppermute(value, "mp", [(0, 1), (1, 0), (2, 3), (3, 2)])


def chip_swap(value):
    return lax.ppermute(value, "mp", [(0, 2), (2, 0), (1, 3), (3, 1)])


class Ring:
    def __init__(self):
        self.count = count = lax.axis_size("dp")
        order = [*range(0, count, 2), *reversed(range(1, count, 2))]
        self.ahead = [(order[i], order[(i + 1) % count]) for i in range(count)]
        self.behind = [(b, a) for a, b in self.ahead]
        me = lax.axis_index("dp")
        self.place = jnp.where(me % 2 == 0, me // 2, count - 1 - me // 2)
        self.unrolled = count <= 8

    def member(self, offset):
        place = (self.place + offset) % self.count
        return jnp.where(place < self.count // 2, 2 * place, 2 * (self.count - 1 - place) + 1)

    def up(self, value):
        return lax.ppermute(value, "dp", self.ahead)

    def down(self, value):
        return lax.ppermute(value, "dp", self.behind)

    def gather(self, block):
        return Gather(self, block)

    def reduce(self, whole=None, far=None):
        return Reduce(self, whole, far)


class Gather:
    def __init__(self, ring, block):
        self.ring, self.size, self.hop = ring, block.shape[0], 0
        self.left = self.right = block
        self.came = [(block,)]
        self.hops = ring.count // 2 if ring.unrolled else 1
        if ring.unrolled:
            whole = jnp.zeros((self.size * ring.count, block.shape[1]), block.dtype)
            self.whole = self.put(whole, block, 0)

    def put(self, whole, piece, offset, inner=0):
        start = self.ring.member(offset) * self.size + inner
        return lax.dynamic_update_slice(whole, piece, (start, 0))

    def ended(self):
        return self.hop == self.hops

    def step(self):
        if not self.ring.unrolled:
            self.hop += 1
            return lax.all_gather(self.left, "dp", axis=0, tiled=True)
        self.hop += 1
        left, right = self.left, self.right
        if self.hop == self.hops:
            half = self.size // 32 * 16
            left, right = left[:half], right[half:]
        return self.ring.up(left), self.ring.down(right)

    def upcoming(self):
        return ()

    def accept(self, pieces, later=()):
        if not self.ring.unrolled:
            self.whole = pieces
            return
        self.left, self.right = pieces
        self.came.append(pieces)
        inner = self.left.shape[0] if self.hop == self.hops else 0
        self.whole = self.put(self.whole, self.left, -self.hop)
        self.whole = self.put(self.whole, self.right, self.hop, inner)


def hop_kernel(ahead_ref, behind_ref, left_ref, right_ref, up_ref, down_ref):
    size, some = ahead_ref.shape[0], left_ref.shape[0]
    up_ref[:some] = (ahead_ref[:some].astype(f32) + left_ref[...].astype(f32)).astype(bf16)
    if some < size:
        up_ref[some:] = ahead_ref[some:]
    rest = size - right_ref.shape[0]
    down_ref[rest:] = (behind_ref[rest:].astype(f32) + right_ref[...].astype(f32)).astype(bf16)
    if rest:
        down_ref[:rest] = behind_ref[:rest]


class Reduce:
    def __init__(self, ring, whole=None, far=None):
        self.ring, self.next, self.far = ring, (), far
        self.hop = self.hops = ring.count // 2 if ring.unrolled else 1
        if whole is not None:
            self.give(sync(whole))

    def give(self, whole):
        self.whole, self.size = whole, whole.shape[0] // self.ring.count
        if not self.ring.unrolled:
            return
        if self.far is None:
            self.far = self.share(self.hops)
        elif self.hop < self.hops:
            self.next = (self.share(self.hop), self.share(-self.hop))

    def share(self, offset):
        at = self.ring.member(offset) * self.size
        return lax.dynamic_slice_in_dim(self.whole, at, self.size, 0)

    def ended(self):
        return self.hop == 0

    def step(self):
        if not self.ring.unrolled:
            return lax.psum_scatter(self.whole, "dp", scatter_dimension=0, tiled=True)
        if self.hop == self.hops:
            half = self.far.shape[0] // 32 * 16
            left, right = self.far[:half], self.far[half:]
        else:
            block = jax.ShapeDtypeStruct(self.next[0].shape, bf16)
            left, right = tiled_call(
                hop_kernel,
                [block] * 2,
                (*self.next, self.left, self.right),
                [pl.BlockSpec(p.shape, lambda i: (0, 0)) for p in (*self.next, self.left, self.right)],
                [pl.BlockSpec(block.shape, lambda i: (0, 0))] * 2,
                1,
            )
        return self.ring.up(left), self.ring.down(right)

    def upcoming(self):
        if not self.ring.unrolled or self.hop - 1 < 0 or not hasattr(self, "whole"):
            return ()
        later = self.hop - 1
        return tuple(self.share(o) for o in ((later, -later) if later else (0,)))

    def accept(self, pieces, later=()):
        self.hop -= 1
        self.next = later
        if not self.ring.unrolled:
            self.left = pieces
        else:
            self.left, self.right = pieces

    def total(self):
        while self.hop > 0:
            pieces = self.step()
            self.accept(pieces, self.upcoming())
        if not self.ring.unrolled:
            return self.left.astype(f32)
        return self.next[0].astype(f32) + self.left.astype(f32) + self.right.astype(f32)


def phase(rings, *values):
    rings = [r for r in rings if not r.ended()]
    pieces, later, values = sync(([r.step() for r in rings], [r.upcoming() for r in rings], values))
    for r, p, n in zip(rings, pieces, later):
        r.accept(p, n)
    return values[0] if len(values) == 1 else values


def join(mine, other, swapped, axis):
    return jnp.where(
        swapped,
        jnp.concatenate([other, mine], axis=axis),
        jnp.concatenate([mine, other], axis=axis),
    )


def gather_chip(piece, axis):
    me = lax.axis_index("mp")
    piece = join(piece, core_swap(piece), me % 2 == 1, axis)
    return join(piece, chip_swap(piece), me // 2 == 1, axis)


def gather_small(piece, axis):
    count = lax.axis_size("dp")
    me = lax.axis_index("dp")
    step = 1
    while step < count:
        other = lax.ppermute(piece, "dp", [(i, i ^ step) for i in range(count)])
        piece = join(piece, other, (me // step) % 2 == 1, axis)
        step *= 2
    return piece


def sum_chip(value):
    value = value + core_swap(value)
    return value + chip_swap(value)


def sum_step(value, step):
    count = lax.axis_size("dp")
    if step >= count:
        return value
    return value + lax.ppermute(value, "dp", [(i, i ^ step) for i in range(count)])


def stack_kernel(*refs):
    *pieces, out_ref = refs
    rows = pieces[0].shape[0]
    for i, piece in enumerate(pieces):
        out_ref[i * rows : (i + 1) * rows] = piece[...]


def stack(*pieces):
    rows, width = pieces[0].shape
    step = width // 4
    return pl.pallas_call(
        stack_kernel,
        out_shape=jax.ShapeDtypeStruct((rows * len(pieces), width), pieces[0].dtype),
        grid=(4,),
        in_specs=[pl.BlockSpec((rows, step), lambda i: (0, i))] * len(pieces),
        out_specs=pl.BlockSpec((rows * len(pieces), step), lambda i: (0, i)),
        compiler_params=pltpu.CompilerParams(vmem_limit_bytes=24 * 2**20),
        cost_estimate=light,
    )(*pieces)


def gather_slots(piece):
    near = core_swap(piece)
    across = chip_swap(piece)
    return stack(piece, near, across, core_swap(across))


def top(value):
    return value[: value.shape[0] // 2]


def bottom(value):
    return value[value.shape[0] // 2 :]


def add_core(value):
    return top(value) + core_swap(bottom(value).astype(bf16))


def cross(far):
    return chip_swap(add_core(far).astype(bf16))


def rows_of(value, i, pieces):
    width = value.shape[0] // pieces
    return value[i * width : (i + 1) * width]


def normalize(raw):
    return raw * lax.rsqrt(jnp.mean(raw * raw, axis=-1, keepdims=True) + epsilon)


def turn(values, cosine, sine):
    half = HEAD_DIM // 2
    first, second = values[:, :half], values[:, half:]
    return jnp.concatenate(
        [first * cosine - second * sine, second * cosine + first * sine], axis=1
    )


def dot(left, right, dims):
    return lax.dot_general(left, right, ((dims[:1], dims[1:]), ((), ())), preferred_element_type=f32)


TILE = 256


def tiles(length):
    return [(i, max(0, i - WINDOW)) for i in range(0, length, TILE)]


def tile_probs(query, key, start, first, rows_ref, cols_ref):
    stop = start + TILE
    scores = dot(query, key, (1, 1)) * HEAD_DIM**-0.5
    row = start + lax.broadcasted_iota(jnp.int32, scores.shape, 0)
    col = first + lax.broadcasted_iota(jnp.int32, scores.shape, 1)
    kept = (col <= row) & (row - col < WINDOW)
    kept &= rows_ref[start:stop, :] == cols_ref[:, first:stop]
    scores = jnp.where(kept, scores, masked_score)
    expo = jnp.exp(scores - jnp.max(scores, axis=-1, keepdims=True))
    return expo / jnp.sum(expo, axis=-1, keepdims=True)


def slot_at(mine_ref, start):
    return pl.ds(pl.multiple_of((mine_ref[0] ^ (start // TILE)) * TILE, TILE), TILE)


def forward_kernel(
    mine_ref, raw_ref, cos_ref, sin_ref, rows_ref, cols_ref, gain_ref, out_ref, low_ref
):
    length, across = raw_ref.shape
    heads = across // HEAD_DIM - 2
    key_at, value_at = heads * HEAD_DIM, (heads + 1) * HEAD_DIM
    for start in range(0, length, TILE):
        at, here = slice(start, start + TILE), slot_at(mine_ref, start)
        for head in range(heads + 1):
            cols = slice(head * HEAD_DIM, (head + 1) * HEAD_DIM)
            gain = gain_ref[int(head == heads) : int(head == heads) + 1, :]
            turned = turn(normalize(raw_ref[here, cols]) * gain, cos_ref[at, :], sin_ref[at, :])
            low_ref[at, cols] = turned.astype(bf16)
        low_ref[at, value_at:] = normalize(raw_ref[here, value_at:]).astype(bf16)
    for start, first in tiles(length):
        stop = start + TILE
        key = low_ref[first:stop, key_at:value_at]
        value = low_ref[first:stop, value_at:]
        for head in range(heads):
            cols = slice(head * HEAD_DIM, (head + 1) * HEAD_DIM)
            probs = tile_probs(low_ref[start:stop, cols], key, start, first, rows_ref, cols_ref)
            attended = dot(probs.astype(bf16), value, (1, 0))
            out_ref[slot_at(mine_ref, start), cols] = attended.astype(bf16)


def norm_grad(raw, gain, upstream):
    scale = lax.rsqrt(jnp.mean(raw * raw, axis=-1, keepdims=True) + epsilon)
    unit = raw * scale
    inner = upstream * gain
    grad = scale * (inner - unit * jnp.mean(inner * unit, axis=-1, keepdims=True))
    return grad, jnp.sum(upstream * unit, axis=0, keepdims=True)


def backward_kernel(
    mine_ref, raw_ref, low_ref, up_ref, cos_ref, sin_ref, rows_ref, cols_ref, gain_ref, out_ref,
    gain_out_ref, key_sum, value_sum,
):
    length, across = raw_ref.shape
    heads = across // HEAD_DIM - 2
    key_at, value_at = heads * HEAD_DIM, (heads + 1) * HEAD_DIM
    scale = HEAD_DIM**-0.5
    key_sum[...] = jnp.zeros_like(key_sum)
    value_sum[...] = jnp.zeros_like(value_sum)
    query_gain = jnp.zeros((1, HEAD_DIM), f32)
    key_gain = jnp.zeros((1, HEAD_DIM), f32)
    for start, first in tiles(length):
        stop = start + TILE
        at, here = slice(start, stop), slot_at(mine_ref, start)
        key = low_ref[first:stop, key_at:value_at]
        value = low_ref[first:stop, value_at:]
        for head in range(heads):
            cols = slice(head * HEAD_DIM, (head + 1) * HEAD_DIM)
            query = low_ref[at, cols]
            upstream = up_ref[here, cols]
            probs = tile_probs(query, key, start, first, rows_ref, cols_ref)
            grad_probs = dot(upstream, value, (1, 1))
            inner = jnp.sum(probs * grad_probs, axis=-1, keepdims=True)
            grad_scores = (probs * (grad_probs - inner)).astype(bf16)
            value_sum[first:stop, :] += dot(probs.astype(bf16), upstream, (0, 0))
            key_sum[first:stop, :] += dot(grad_scores, query, (0, 0)) * scale
            grad_query = dot(grad_scores, key, (1, 0)) * scale
            grad_query = turn(grad_query, cos_ref[at, :], -sin_ref[at, :])
            grad, gain = norm_grad(raw_ref[here, cols], gain_ref[0:1, :], grad_query)
            out_ref[here, cols] = grad.astype(bf16)
            query_gain += gain
    for start in range(0, length, TILE):
        at, here = slice(start, start + TILE), slot_at(mine_ref, start)
        grad_key = turn(key_sum[at, :], cos_ref[at, :], -sin_ref[at, :])
        grad, gain = norm_grad(raw_ref[here, key_at:value_at], gain_ref[1:2, :], grad_key)
        out_ref[here, key_at:value_at] = grad.astype(bf16)
        key_gain += gain
        grad, _ = norm_grad(raw_ref[here, value_at:], 1.0, value_sum[at, :])
        out_ref[here, value_at:] = grad.astype(bf16)
    gain_out_ref[...] = jnp.concatenate([query_gain, key_gain])


def local_call(kernel, out_shape, inputs, scratch=()):
    vmem = pl.BlockSpec(memory_space=pltpu.VMEM)
    return pl.pallas_call(
        kernel,
        out_shape=out_shape,
        in_specs=[pl.BlockSpec(memory_space=pltpu.SMEM)] + [vmem] * (len(inputs) - 1),
        out_specs=[vmem] * len(out_shape),
        scratch_shapes=list(scratch),
        compiler_params=pltpu.CompilerParams(vmem_limit_bytes=40 * 2**20),
        cost_estimate=light,
    )(*inputs)


def attention(mine, raw, cosine, sine, segments, head_scales):
    length, across = raw.shape
    tables = (cosine, sine, segments[:, None], segments[None, :], head_scales)
    heads = across // HEAD_DIM - 2
    return local_call(
        forward_kernel,
        [
            jax.ShapeDtypeStruct((length, heads * HEAD_DIM), bf16),
            jax.ShapeDtypeStruct((length, across), bf16),
        ],
        (mine, raw, *tables),
    )


def attention_back(mine, raw, low, upstream, cosine, sine, segments, head_scales):
    length, across = raw.shape
    tables = (cosine, sine, segments[:, None], segments[None, :], head_scales)
    return local_call(
        backward_kernel,
        [jax.ShapeDtypeStruct((length, across), bf16), jax.ShapeDtypeStruct((2, HEAD_DIM), f32)],
        (mine, raw, low, upstream, *tables),
        [pltpu.VMEM((length, HEAD_DIM), f32)] * 2,
    )


gelu_scale = math.sqrt(2.0 / math.pi)


def feed_forward_kernel(x_ref, gate_ref, up_ref, gate_pre_ref, up_pre_ref, hidden_ref):
    gate_pre = dot(x_ref[...], gate_ref[...], (1, 0))
    up_pre = dot(x_ref[...], up_ref[...], (1, 0))
    gate_pre_ref[...] = gate_pre
    up_pre_ref[...] = up_pre
    bend = jnp.tanh(gelu_scale * (gate_pre + 0.044715 * gate_pre**3))
    hidden_ref[...] = (0.5 * gate_pre * (1.0 + bend) * up_pre).astype(bf16)


def feed_forward_back_kernel(grad_ref, down_ref, gate_ref, up_ref, grad_gate_ref, grad_up_ref):
    grad = dot(grad_ref[...], down_ref[...], (1, 0))
    gate = gate_ref[...]
    bend = jnp.tanh(gelu_scale * (gate + 0.044715 * gate**3))
    slope = gelu_scale * (1.0 + 3.0 * 0.044715 * gate * gate)
    grad_up_ref[...] = (grad * (0.5 * gate * (1.0 + bend))).astype(bf16)
    slope = 0.5 * (1.0 + bend) + 0.5 * gate * (1.0 - bend * bend) * slope
    grad_gate_ref[...] = (grad * up_ref[...] * slope).astype(bf16)


def grad_in_kernel(grad_gate_ref, grad_up_ref, gate_ref, up_ref, out_ref):
    out_ref[...] = dot(grad_gate_ref[...], gate_ref[...], (1, 1)) + dot(
        grad_up_ref[...], up_ref[...], (1, 1)
    )


def tiled_call(kernel, outs, inputs, specs, out_specs, steps):
    return pl.pallas_call(
        kernel,
        out_shape=outs,
        grid=(steps,),
        in_specs=specs,
        out_specs=out_specs,
        compiler_params=pltpu.CompilerParams(vmem_limit_bytes=48 * 2**20),
        cost_estimate=light,
    )(*inputs)


def column_tile(rows):
    return pl.BlockSpec((rows, TILE), lambda i: (0, i))


def feed_forward(x, gate, up, part, before=()):
    tokens, width = x.shape
    units = gate.shape[1]
    steps = units // TILE // 2
    wide = jax.ShapeDtypeStruct((tokens, units), f32)

    def tile(rows):
        return pl.BlockSpec((rows, TILE), lambda i: (0, i + part * steps))

    def kernel(*refs):
        feed_forward_kernel(*refs[:3], *refs[-3:])

    return pl.pallas_call(
        kernel,
        out_shape=[wide, wide, jax.ShapeDtypeStruct((tokens, units), bf16)],
        grid=(steps,),
        in_specs=[
            pl.BlockSpec((tokens, width), lambda i: (0, 0)),
            tile(width),
            tile(width),
            *[pl.BlockSpec(memory_space=pl.ANY)] * len(before),
        ],
        out_specs=[tile(tokens)] * 3,
        input_output_aliases={3 + i: i for i in range(len(before))},
        compiler_params=pltpu.CompilerParams(vmem_limit_bytes=48 * 2**20),
        cost_estimate=light,
    )(x, gate, up, *before)


def pair_grad_kernel(left_ref, gate_ref, up_ref, out_ref):
    left = left_ref[...]
    rows = left.shape[1]
    out_ref[:rows] = dot(left, gate_ref[...], (0, 0)).astype(bf16)
    out_ref[rows:] = dot(left, up_ref[...], (0, 0)).astype(bf16)


def pair_grad(left, grad_gate, grad_up):
    tokens, width = left.shape
    units = grad_gate.shape[1]
    size = width // lax.axis_size("dp")
    tile = max(size, 128)
    whole = pl.BlockSpec((tokens, units), lambda i: (0, 0))
    out = tiled_call(
        pair_grad_kernel,
        [jax.ShapeDtypeStruct((2 * width, units), bf16)],
        (left, grad_gate, grad_up),
        [pl.BlockSpec((tokens, tile), lambda i: (0, i)), whole, whole],
        [pl.BlockSpec((2 * tile, units), lambda i: (i, 0))],
        width // tile,
    )[0]
    if tile == size:
        return out
    out = out.reshape(width // tile, 2, tile // size, size, units)
    return out.transpose(0, 2, 1, 3, 4).reshape(2 * width, units)


def feed_forward_back(grad, down_t, gate_pre, up_pre, far, before=()):
    half, width = grad.shape
    units = down_t.shape[1]

    def kernel(*refs):
        feed_forward_back_kernel(*refs[:4], *refs[-2:])

    return pl.pallas_call(
        kernel,
        out_shape=[jax.ShapeDtypeStruct((2 * half, units), bf16)] * 2,
        grid=(units // TILE,),
        in_specs=[
            pl.BlockSpec((half, width), lambda i: (0, 0)),
            column_tile(width),
            *[pl.BlockSpec((half, TILE), lambda i: (far, i))] * 2,
            *[pl.BlockSpec(memory_space=pl.ANY)] * len(before),
        ],
        out_specs=[pl.BlockSpec((half, TILE), lambda i: (far, i))] * 2,
        input_output_aliases={4 + i: i for i in range(len(before))},
        compiler_params=pltpu.CompilerParams(vmem_limit_bytes=48 * 2**20),
        cost_estimate=light,
    )(grad, down_t, gate_pre, up_pre, *before)


def grad_in(grad_gate, grad_up, gate, up, far):
    tokens, units = grad_gate.shape
    half, width = tokens // 2, gate.shape[0]
    rows = pl.BlockSpec((half, units), lambda i: (far, 0))
    weights = pl.BlockSpec((TILE, units), lambda i: (i, 0))
    return tiled_call(
        grad_in_kernel,
        [jax.ShapeDtypeStruct((half, width), f32)],
        (grad_gate, grad_up, gate, up),
        [rows, rows, weights, weights],
        [column_tile(half)],
        width // TILE,
    )[0]


def place_kernel(members_ref, *refs):
    *inputs, out_ref = refs
    place = 0
    for near, far in zip(inputs[::2], inputs[1::2]):
        for start in range(0, near.shape[1], TILE):
            cols = slice(start, start + TILE)
            at = pl.ds(pl.multiple_of(members_ref[place] * TILE, TILE), TILE)
            out_ref[:, at] = near[:, cols] + far[:, cols].astype(f32)
            place += 1


def place(members, sums, rows, width):
    return local_call(
        place_kernel, [jax.ShapeDtypeStruct((rows, width), f32)], (members, *sums)
    )[0]


def shards(
    tokens,
    layer_vectors,
    segment_ids,
    cotangent,
    norm_gains,
    head_gains,
    w_query,
    w_key,
    w_value,
    w_out,
    w_left,
    w_right,
    w_gate,
    w_up,
    w_down,
    w_layer_gate,
    w_layer_proj,
):
    ring = Ring()
    count = ring.count
    mine = lax.axis_index("mp")
    chip, core = mine // 2, mine % 2
    rows, width = tokens.shape
    length = segment_ids.shape[0]
    share = w_key.shape[0]
    rank = w_left.shape[1]
    layer_dim = w_layer_gate.shape[1]

    heads_part = head_gains.shape[0]
    def pick(value, index, axis):
        return lax.dynamic_index_in_dim(value, index, axis, keepdims=False)

    def small_core(value):
        value = value.reshape(count, 2, 2, share, -1)
        mine_too = core_swap(pick(value, 1 - core, 2))
        return (pick(value, core, 2).astype(f32) + mine_too).astype(bf16)

    def small_chip(value):
        other = chip_swap(pick(value, 1 - chip, 1))
        return (pick(value, chip, 1).astype(f32) + other).astype(bf16)

    side = HEAD_DIM
    line = w_query.shape[1]
    fold = 2 * rank * share // line
    extra = jnp.concatenate(
        [norm_gains, jnp.pad(head_gains, (0, norm_gains.shape[1] - heads_part))[None]]
    )
    extra = gather_chip(jnp.pad(extra, ((0, 8 - extra.shape[0]), (0, 0))), 1)
    gain_columns = extra.shape[1]
    extra = extra.reshape(-1, line)
    gain_rows = extra.shape[0]
    parts = [
        w_query,
        w_out.T,
        w_key,
        w_value,
        jnp.concatenate([w_layer_gate, w_layer_proj.T], axis=1),
        jnp.concatenate([w_left, w_right.T], axis=1).reshape(fold, line),
        jnp.pad(extra, ((0, 16 - gain_rows), (0, 0))),
    ]
    first = ring.gather(jnp.concatenate(parts))
    gate, up, last = (ring.gather(w) for w in (w_gate, w_up, w_down.T))
    inputs = tokens.astype(f32)
    vectors = layer_vectors.astype(f32)
    tokens_near = phase([first], core_swap(tokens))
    tables = phase([first], *rotary_tables(segment_ids))
    cosine, sine = tables
    tokens_far = phase([first], chip_swap(tokens))
    tokens_last = phase([first, gate], core_swap(tokens_far))

    whole = first.whole.reshape(count, -1, line)
    starts = [sum(p.shape[0] for p in parts[:i]) for i in range(len(parts) + 1)]
    query_weight, out_t, key_part, value_part, layer_part, rank_part, extra = (
        whole[:, a:b] for a, b in zip(starts[:-1], starts[1:])
    )
    out_t = out_t.reshape(-1, line)

    def head_columns(value, head):
        return lax.dynamic_slice_in_dim(value, head * side, side, 2)

    def kv_of(head):
        return jnp.concatenate(
            [head_columns(key_part, head), head_columns(value_part, head)], axis=2
        )

    small_part = jnp.concatenate(
        [layer_part, rank_part.reshape(count, share, 2 * rank)], axis=2
    )

    def interleave(own, across):
        both = join(own[:, None], across[:, None], chip == 1, 1)[:, :, None]
        other = core_swap(both)
        return join(both, other, core == 1, 2).reshape(count * 4 * share, -1)

    gains = extra[:, :gain_rows].reshape(count, 8, gain_columns).transpose(1, 0, 2)
    gains = gains.reshape(8, width).astype(f32)
    head_scales = gains[6].reshape(-1, norm_gains.shape[1])[:, :heads_part].reshape(2, HEAD_DIM)
    normed = rms_norm(inputs, gains[0])
    normed_low = normed.astype(bf16)
    normed_all = stack(
        normed_low,
        *(
            rms_norm(t.astype(f32), gains[0]).astype(bf16)
            for t in (tokens_near, tokens_far, tokens_last)
        ),
    )
    normed_all, kv_weight = phase([up], normed_all, chip_swap(kv_of(1 - chip)))
    qkv_weight = jnp.concatenate(
        [query_weight.reshape(-1, line), interleave(kv_of(chip), kv_weight)], axis=1
    )
    qkv_raw = product(normed_all, qkv_weight)
    here = mine.reshape(1)
    attended_low, qkv_low = attention(
        here, qkv_raw, cosine, sine, segment_ids, head_scales
    )
    half = length // 2
    attn_far = product_right(attended_low[half:], out_t)
    attn_far, attended_low, small_part, normed_low, small_all = phase(
        [gate], attn_far, attended_low, small_part, normed_low, chip_swap(small_part)
    )
    attn_near = product_right(attended_low[:half], out_t)
    attn_far, attn_near = phase([up], cross(attn_far), attn_near)
    attn = add_core(attn_near) + attn_far
    small_all = interleave(small_part, small_all)
    layer_gate_weight, layer_proj_weight, left_weight, right_weight = jnp.split(
        small_all, [layer_dim, 2 * layer_dim, 2 * layer_dim + rank], axis=1
    )
    left_low = product(normed_low, left_weight).astype(bf16)
    laurel_pre = product_right(left_low, right_weight)
    after_attn = inputs + rms_norm(attn, gains[1])
    mixed = (after_attn + normed + rms_norm(laurel_pre, gains[2])) * root_half
    ff_in_low = rms_norm(mixed, gains[3]).astype(bf16)
    ff_in_low, mixed, attn, laurel_pre = phase([gate], ff_in_low, mixed, attn, laurel_pre)
    ff_in_near, ff_in_far = phase([up], core_swap(ff_in_low), chip_swap(ff_in_low))
    ff_in_all = stack(ff_in_low, ff_in_near, ff_in_far, core_swap(ff_in_far))
    ff_in_all = phase([gate, up], ff_in_all)
    gate_weight, up_weight = gate.whole, up.whole
    forward, ff_in_all = phase(
        [last], feed_forward(ff_in_all, gate_weight, up_weight, 0), ff_in_all
    )
    forward, ff_in_all = phase(
        [last], feed_forward(ff_in_all, gate_weight, up_weight, 1, forward), ff_in_all
    )
    gate_pre, up_pre, hidden_low = forward
    hidden_near, hidden_far = hidden_low[:half], hidden_low[half:]

    if ring.unrolled:
        early = jnp.concatenate([p for hop in last.came for p in hop])
        early_far, early_near = phase(
            [last], product_right(hidden_far, early), product_right(hidden_near, early)
        )
        early_far, early_near = phase([last], cross(early_far), early_near)
        late = jnp.concatenate([p for hop in last.came[-2:] for p in hop])
        late_far, late_near = sync(
            (cross(product_right(hidden_far, late)), product_right(hidden_near, late))
        )
        offsets = [0]
        for hop in range(1, count // 2):
            offsets += [-hop, hop]
        members = jnp.stack([ring.member(o) for o in [*offsets, count // 2]]).astype(jnp.int32)
        sums = (add_core(early_near), early_far, add_core(late_near), late_far)
        ff_out = place(members, sums, rows, width)
    else:
        late_far = cross(product_right(hidden_far, last.whole))
        ff_out = add_core(product_right(hidden_near, last.whole)) + late_far
    down_t = last.whole
    after_ff = mixed + rms_norm(ff_out, gains[4])
    after_ff_low = after_ff.astype(bf16)
    layer_pre = product(after_ff_low, layer_gate_weight)
    layer_mix_low = geglu(layer_pre, vectors).astype(bf16)
    layer_out = product_right(layer_mix_low, layer_proj_weight)
    result = after_ff + rms_norm(layer_out, gains[5])

    upstream = cotangent.astype(f32)
    grad_layer_out, grad_gain_five = norm_back(layer_out, gains[5], upstream)
    grad_layer_out_low = grad_layer_out.astype(bf16)
    grad_mix = product(grad_layer_out_low, layer_proj_weight)
    _, layer_pull = jax.vjp(geglu, layer_pre, vectors)
    grad_layer_pre, grad_vectors = layer_pull(grad_mix)
    grad_layer_pre_low = grad_layer_pre.astype(bf16)
    grad_after_ff = upstream + product_right(grad_layer_pre_low, layer_gate_weight)
    grad_ff_out, grad_gain_four = norm_back(ff_out, gains[4], grad_after_ff)
    grad_ff_low, layer_mix_low, after_ff_low = sync(
        (grad_ff_out.astype(bf16), layer_mix_low, after_ff_low)
    )
    grad_layer_proj = product_left(grad_layer_out_low, layer_mix_low)
    grad_layer_gate = product_left(after_ff_low, grad_layer_pre_low)
    grad_ff_near = core_swap(grad_ff_low)
    grads_low = feed_forward_back(stack(grad_ff_low, grad_ff_near), down_t, gate_pre, up_pre, 0)
    grad_ff_far, grads_low, grad_ff_near = sync((chip_swap(grad_ff_low), grads_low, grad_ff_near))
    grad_ff_last = core_swap(grad_ff_far)
    grad_ff_all = stack(grad_ff_low, grad_ff_near, grad_ff_far, grad_ff_last)
    block = width // count
    far_columns = lax.dynamic_slice_in_dim(
        grad_ff_all, ring.member(count // 2) * block, block, 1
    )
    far_grad, grad_ff_all = sync(
        (product_left(far_columns, hidden_low).astype(bf16), grad_ff_all)
    )
    down_back = ring.reduce(far=far_grad)
    down_grad = product_left(grad_ff_all, hidden_low).astype(bf16)
    if ring.unrolled:
        down_grad, grad_ff_all = phase([down_back], down_grad, grad_ff_all)
    down_back.give(down_grad)
    grads_low = feed_forward_back(grad_ff_all[half:], down_t, gate_pre, up_pre, 1, grads_low)
    ff_in_far, *grads_low = phase([down_back], grad_in(*grads_low, gate_weight, up_weight, 1), *grads_low)
    ff_in_far, ff_in_near, *grads_low = phase(
        [down_back], cross(ff_in_far), grad_in(*grads_low, gate_weight, up_weight, 0), *grads_low
    )
    grad_ff_in = add_core(ff_in_near) + ff_in_far
    grad_mixed_norm, grad_gain_three = norm_back(mixed, gains[3], grad_ff_in)
    grad_branch = (grad_after_ff + grad_mixed_norm) * root_half
    grad_attn, grad_gain_one = norm_back(attn, gains[1], grad_branch)
    grad_attn_low, grad_branch = sync((grad_attn.astype(bf16), grad_branch))
    grad_attn_far, grad_attn_near, grad_attn_low, grad_branch, both_grad = phase(
        [down_back],
        chip_swap(grad_attn_low),
        core_swap(grad_attn_low),
        grad_attn_low,
        grad_branch,
        pair_grad(ff_in_all, *grads_low),
    )
    both_back = ring.reduce(both_grad)
    grad_attn_all = stack(grad_attn_low, grad_attn_near, grad_attn_far, core_swap(grad_attn_far))
    grad_attended_low = product(grad_attn_all, out_t).astype(bf16)
    grad_qkv_low, head_grads = attention_back(
        here, qkv_raw, qkv_low, grad_attended_low, cosine, sine, segment_ids, head_scales
    )
    normed_far = product_right(grad_qkv_low[half:], qkv_weight)
    normed_far, grad_qkv_low, grad_attn_all, grad_branch = phase(
        [both_back], normed_far, grad_qkv_low, grad_attn_all, grad_branch
    )

    normed_far, grad_qkv_low = sync((add_core(normed_far).astype(bf16), grad_qkv_low))
    normed_far = chip_swap(normed_far)
    qkv_grad = product_left(normed_all, grad_qkv_low).astype(bf16)
    out_grad = product_left(grad_attn_all, attended_low).astype(bf16)
    normed_near = product_right(grad_qkv_low[:half], qkv_weight)
    normed_far, normed_near, qkv_grad, out_grad, kv_grad, grad_branch = phase(
        [both_back],
        normed_far,
        normed_near,
        qkv_grad,
        out_grad,
        small_core(qkv_grad[:, line:]),
        grad_branch,
    )
    grad_laurel, grad_gain_two = norm_back(laurel_pre, gains[2], grad_branch)
    grad_laurel_low = grad_laurel.astype(bf16)
    grad_right = product_left(grad_laurel_low, left_low)
    grad_left_low = product(grad_laurel_low, right_weight).astype(bf16)
    grad_left = product_left(normed_low, grad_left_low)
    small_grad = jnp.concatenate(
        [grad_layer_gate, grad_layer_proj, grad_left, grad_right], axis=1
    ).astype(bf16)
    small_grad = small_chip(small_core(small_grad))
    second = jnp.concatenate(
        [
            qkv_grad[:, :line].reshape(count, -1, line),
            kv_grad.reshape(count, 2 * share, 2 * side),
            out_grad.reshape(count, -1, line),
            small_grad[:, :, : 2 * layer_dim],
            small_grad[:, :, 2 * layer_dim :].reshape(count, fold, line),
        ],
        axis=1,
    )
    second, grad_left_low = phase([both_back], second, grad_left_low)
    second = ring.reduce(second.reshape(-1, line))
    grad_normed_heads = add_core(normed_near) + normed_far
    grad_normed = grad_branch + product_right(grad_left_low, left_weight) + grad_normed_heads
    grad_inputs_norm, grad_gain_zero = norm_back(inputs, gains[0], grad_normed)
    grad_inputs = grad_branch + grad_inputs_norm
    head_grads = head_grads.reshape(-1)
    gain_grads = jnp.stack(
        [
            grad_gain_zero,
            grad_gain_one,
            grad_gain_two,
            grad_gain_three,
            grad_gain_four,
            grad_gain_five,
            jnp.pad(head_grads, (0, width - head_grads.shape[0])),
        ]
    )
    gain_grads, grad_inputs = phase(
        [both_back, second], sum_step(sum_chip(gain_grads), 1), grad_inputs
    )
    both_grad, down_grad, gain_grads = phase(
        [second], both_back.total(), down_back.total().T, sum_step(gain_grads, 2)
    )
    gate_grad, up_grad = jnp.split(both_grad, 2)
    gain_grads = phase([second], sum_step(gain_grads, 4))
    step = 8
    while step < count:
        gain_grads = sum_step(gain_grads, step)
        step *= 2
    device = lax.axis_index("dp") * 4 + mine
    part = norm_gains.shape[1]
    grad_norm_gains = lax.dynamic_slice_in_dim(gain_grads[:6], device * part, part, 1)
    grad_head_gains = lax.dynamic_slice_in_dim(gain_grads[6], device * heads_part, heads_part, 0)

    second = second.total()
    out_rows = width // count
    grad_query_weight, kv_sum, grad_out, grad_layer, grad_rank = jnp.split(
        second,
        [out_rows, out_rows + 2 * share, 2 * out_rows + 2 * share, 2 * out_rows + 3 * share],
    )
    grad_out = grad_out.T
    grad_layer_gate_weight = grad_layer[:, :layer_dim]
    grad_layer_proj_weight = grad_layer[:, layer_dim:].T
    grad_rank = grad_rank.reshape(share, 2 * rank)
    grad_left_weight = grad_rank[:, :rank]
    grad_right_weight = grad_rank[:, rank:].T
    kv_sum = kv_sum.reshape(2, share, 2 * side)
    kv_mine = pick(kv_sum, chip, 0)
    kv_other = chip_swap(pick(kv_sum, 1 - chip, 0).astype(bf16)).astype(f32)
    grad_key_weight = join(kv_mine[:, :side], kv_other[:, :side], chip == 1, 1)
    grad_value_weight = join(kv_mine[:, side:], kv_other[:, side:], chip == 1, 1)
    return (
        result.astype(bf16),
        grad_inputs.astype(bf16),
        grad_vectors.astype(bf16),
        grad_norm_gains,
        grad_head_gains,
        grad_query_weight,
        grad_key_weight,
        grad_value_weight,
        grad_out,
        grad_left_weight,
        grad_right_weight,
        gate_grad,
        up_grad,
        down_grad,
        grad_layer_gate_weight,
        grad_layer_proj_weight,
    )


def solution(mesh):
    both = ("dp", "mp")
    in_specs = (
        P(both, None),
        P(both, None),
        P("dp"),
        P(both, None),
        P(None, both),
        P(both),
        P("dp", "mp"),
        P(both, None),
        P(both, None),
        P("mp", "dp"),
        P(both, None),
        P(None, both),
        P("dp", "mp"),
        P("dp", "mp"),
        P("mp", "dp"),
        P(both, None),
        P(None, both),
    )
    out_specs = (
        P(both, None),
        P(both, None),
        P(both, None),
        P(None, both),
        P(both),
        P("dp", "mp"),
        P(both, None),
        P(both, None),
        P("mp", "dp"),
        P(both, None),
        P(None, both),
        P("dp", "mp"),
        P("dp", "mp"),
        P("mp", "dp"),
        P(both, None),
        P(None, both),
    )
    return jax.shard_map(shards, mesh=mesh, in_specs=in_specs, out_specs=out_specs, check_vma=False)
```

time: 1030 us -> 852 us (0.83)
  matrix products: 241 us -> 67.3 us
  Pallas kernels: 12.4 us -> 150 us
  waiting for transfers between devices: 424 us -> 327 us
  starting transfers between devices: 114 us -> 81.5 us
  other arithmetic: 85.8 us -> 70.7 us
    pallas_call x2 -> x24, Pallas kernels: 12.4 us -> 150 us  [the longest x12 74.4 us: tiled_call(): pl.pallas_call(kernel, out_shape=outs, grid=(steps,), in_specs=specs, out...]
    dot_general x44 -> x12, matrix products: 116 us -> 34 us  [product_right(): lax.dot_general(left, right, (((1,), (1,)), ((), ())), preferred_element_...]
    dot_general x9 -> x6, matrix products: 71.8 us -> 10.8 us  [product(): return jnp.dot(left, right, preferred_element_type=f32)]
    ppermute x32 -> x28, waiting for transfers between devices: 75.8 us -> 20.5 us  [down(): return lax.ppermute(value, 'dp', self.behind)]
    ppermute x17 -> x15, waiting for transfers between devices: 105 us -> 52.7 us  [chip_swap(): return lax.ppermute(value, 'mp', [(0, 2), (2, 0), (1, 3), (3, 1)])]
    dot_general x9 -> x8, matrix products: 53.9 us -> 22.5 us  [product_left(): lax.dot_general(left, right, (((0,), (0,)), ((), ())), preferred_element_...]
    unnamed x242 -> x250, local copies, waits for them, and re-layouts: 21.3 us -> 52.1 us
    dynamic_update_slice x34 -> x36, local copies, waits for them, and re-layouts: 64.7 us -> 34.8 us  [put(): return lax.dynamic_update_slice(whole, piece, (start, 0))]
  transfers between devices with their start and end apart: 116 -> 98, of which waited for: 50 -> 56; matrix products, arithmetic and copies ran while one was open for 36% -> 25% of each run, Pallas kernels for 1% -> 17%
where the time goes in v2:
time: 852 us; the launch traced here: 842 us
  waiting for transfers between devices  327 us (38%)
  Pallas kernels  150 us (18%)
  local copies, waits for them, and re-layouts  143 us (17%)
  starting transfers between devices  81.5 us (10%)
  other arithmetic  70.7 us (8%)
  matrix products  67.3 us (8%)
    ppermute x28, waiting for transfers between devices, up(): return lax.ppermute(value, 'dp', self.ahead)  186 us
    pallas_call x12, Pallas kernels, tiled_call(): pl.pallas_call(kernel, out_shape=outs, grid=(steps,), in_specs=specs, out...  74.4 us
    ppermute x3, waiting for transfers between devices, sum_step(): lax.ppermute(value, 'dp', [(i, i ^ step) for i in range(count)])  58.4 us
    ppermute x15, waiting for transfers between devices, chip_swap(): return lax.ppermute(value, 'mp', [(0, 2), (2, 0), (1, 3), (3, 1)])  52.7 us
    unnamed x250, local copies, waits for them, and re-layouts  52.1 us
    dynamic_update_slice x36, local copies, waits for them, and re-layouts, put(): return lax.dynamic_update_slice(whole, piece, (start, 0))  34.8 us
    dot_general x12, matrix products, product_right(): lax.dot_general(left, right, (((1,), (1,)), ((), ())), preferred_element_...  34 us
    ppermute x28, starting transfers between devices, up(): return lax.ppermute(value, 'dp', self.ahead)  32.3 us
  transfers between devices with their start and end apart: 98, of which 56 were waited for; matrix products, arithmetic and copies ran while one was open for 25% of the time, Pallas kernels for 17%

profile of v2, /device:TPU:0, one launch (start us, length us, event | category | flops | bytes accessed | tf_op | source)
XLA Modules:
  0.0 842.2 jit_solution(10390352797236512305)
XLA Ops:
  19.7 13.6 %collective-permute-done.2 = bf16[736,512]{1,0:T(8,128)(2,1)S(1)} collective-permute-done((bf16[736,512]{1,0:T(8,128)(2,1)S(1)}, bf16[736,512]{1,0:T(8,128)(2,1)S(1)}, u32[]{:S(2)}, u32[]{:S(2)}) %collective-permute-start.2) | collective-permute-done | bytes 753696 | tf_op jit(solution)/shard_map/ppermute | solution.py:85
  39.7 30.6 %collective-permute-done.5 = bf16[736,512]{1,0:T(8,128)(2,1)} collective-permute-done((bf16[736,512]{1,0:T(8,128)(2,1)S(1)}, bf16[736,512]{1,0:T(8,128)(2,1)}, u32[]{:S(2)}, u32[]{:S(2)}) %collective-permute-start.5) | collective-permute-done | bytes 753696 | tf_op jit(solution)/shard_map/ppermute | solution.py:85
  76.5 11.0 %collective-permute-done.7 = bf16[736,512]{1,0:T(8,128)(2,1)S(1)} collective-permute-done((bf16[736,512]{1,0:T(8,128)(2,1)}, bf16[736,512]{1,0:T(8,128)(2,1)S(1)}, u32[]{:S(2)}, u32[]{:S(2)}) %collective-permute-start.7) | collective-permute-done | bytes 753696 | tf_op jit(solution)/shard_map/ppermute | solution.py:85
  208.2 12.3 %collective-permute-done.22 = bf16[256,2048]{1,0:T(8,128)(2,1)S(1)} collective-permute-done((bf16[256,2048]{1,0:T(8,128)(2,1)S(1)}, bf16[256,2048]{1,0:T(8,128)(2,1)S(1)}, u32[]{:S(2)}, u32[]{:S(2)}) %collective-permute-start.22) | collective-permute-done | bytes 1048608 | tf_op jit(solution)/shard_map/ppermute | solution.py:85
  229.8 12.8 %collective-permute-done.34 = bf16[256,2048]{1,0:T(8,128)(2,1)S(1)} collective-permute-done((bf16[256,2048]{1,0:T(8,128)(2,1)}, bf16[256,2048]{1,0:T(8,128)(2,1)S(1)}, u32[]{:S(2)}, u32[]{:S(2)}) %collective-permute-start.34) | collective-permute-done | bytes 1048608 | tf_op jit(solution)/shard_map/ppermute | solution.py:85
  257.0 8.2 collective-permute-done.32
  281.4 14.2 %shard_map.291 = (f32[1024,2048]{1,0:T(8,128)}, f32[1024,2048]{1,0:T(8,128)}, bf16[1024,2048]{1,0:T(8,128)(2,1)S(1)}) custom-call(bf16[1024,2048]{1,0:T(8,128)(2,1)} %copy-done, bf16[2048,2048]{1,0:T(8,128)(2,1)} %constant_dynamic-update-slice_fusion.36.refs_1_.gate_ref, bf16[2048,2048]{1,0:T(8,128)(2,1)} %copy-done.32), custom_call_target="tpu_custom_call" | custom-call | flops 1 | bytes 1 | tf_op jit(solution)/shard_map/pallas_call | solution.py:516
  303.5 14.3 %shard_map.292 = (f32[1024,2048]{1,0:T(8,128)}, f32[1024,2048]{1,0:T(8,128)}, bf16[1024,2048]{1,0:T(8,128)(2,1)S(1)}) custom-call(bf16[1024,2048]{1,0:T(8,128)(2,1)} %copy-done, bf16[2048,2048]{1,0:T(8,128)(2,1)} %constant_dynamic-update-slice_fusion.36.refs_1_.gate_ref, ...), custom_call_target="tpu_custom_call", output_to_operand_aliasing={{0}: (3, {}), {1}: (4, {}), {2}: (5, {})} | custom-call | flops 1 | bytes 1 | tf_op jit(solution)/shard_map/pallas_call | solution.py:516
  353.7 11.0 %collective-permute-done.45 = bf16[128,2048]{1,0:T(8,128)(2,1)S(1)} collective-permute-done((bf16[128,2048]{1,0:T(8,128)(2,1)S(1)}, bf16[128,2048]{1,0:T(8,128)(2,1)S(1)}, u32[]{:S(2)}, u32[]{:S(2)}) %collective-permute-start.45) | collective-permute-done | bytes 524320 | tf_op jit(solution)/shard_map/ppermute | solution.py:85
  405.3 12.7 %shard_map.295 = (bf16[1024,2048]{1,0:T(8,128)(2,1)}, bf16[1024,2048]{1,0:T(8,128)(2,1)}) custom-call(bf16[512,2048]{1,0:T(8,128)(2,1)S(1)} %shard_map.294.refs_0_, bf16[2048,2048]{1,0:T(8,128)(2,1)} %copy-done.33, f32[1024,2048]{1,0:T(8,128)} %get-tuple-element.270.refs_2_, f32[1024,2048]{1,0:T(8,128)} %get-tuple-element.271.refs_3_), custom_call_target="tpu_custom_call" | custom-call | flops 1 | bytes 1 | tf_op jit(solution)/shard_map/pallas_call | solution.py:567
  418.1 9.3 %collective-permute-done.53.refs_2_ = bf16[256,2048]{1,0:T(8,128)(2,1)} collective-permute-done((bf16[256,2048]{1,0:T(8,128)(2,1)S(1)}, bf16[256,2048]{1,0:T(8,128)(2,1)}, u32[]{:S(2)}, u32[]{:S(2)}) %collective-permute-start.53) | collective-permute-done | bytes 1048608 | tf_op jit(solution)/shard_map/ppermute | solution.py:67
  437.8 9.6 %convolution_convert_fusion = bf16[2048,2048]{1,0:T(8,128)(2,1)S(1)} fusion(bf16[1024,2048]{1,0:T(8,128)(2,1)S(1)} %shard_map.296, bf16[1024,2048]{1,0:T(8,128)(2,1)S(1)} %copy-done.7), kind=kOutput, calls=%fused_computation | convolution fusion | flops 8594128896 | bytes 16777216 | tf_op jit(solution)/shard_map/dot_general | solution.py:41
  454.5 12.7 %shard_map.298 = (bf16[1024,2048]{1,0:T(8,128)(2,1)}, bf16[1024,2048]{1,0:T(8,128)(2,1)}) custom-call(bf16[512,2048]{1,0:T(8,128)(2,1)S(1)} %slice.281.refs_0_, bf16[2048,2048]{1,0:T(8,128)(2,1)} %copy-done.33, f32[1024,2048]{1,0:T(8,128)} %get-tuple-element.270.refs_2_, ...), custom_call_target="tpu_custom_call", output_to_operand_aliasing={{0}: (4, {}), {1}: (5, {})} | custom-call | flops 1 | bytes 1 | tf_op jit(solution)/shard_map/pallas_call | solution.py:567
  467.2 14.2 %shard_map.299 = f32[512,2048]{1,0:T(8,128)S(1)} custom-call(bf16[1024,2048]{1,0:T(8,128)(2,1)} %get-tuple-element.309.grad_gate_ref.gate_ref, bf16[1024,2048]{1,0:T(8,128)(2,1)} %get-tuple-element.310.grad_up_ref.up_ref, bf16[2048,2048]{1,0:T(8,128)(2,1)} %constant_dynamic-update-slice_fusion.36.refs_1_.gate_ref, bf16[2048,2048]{1,0:T(8,128)(2,1)} %copy-done.32), custom_call_target="tpu_custom_call" | custom-call | flops 1 | bytes 1 | tf_op jit(solution)/shard_map/pallas_call | solution.py:489
  487.3 14.2 %shard_map.301 = f32[512,2048]{1,0:T(8,128)S(1)} custom-call(bf16[1024,2048]{1,0:T(8,128)(2,1)} %get-tuple-element.309.grad_gate_ref.gate_ref, bf16[1024,2048]{1,0:T(8,128)(2,1)} %get-tuple-element.310.grad_up_ref.up_ref, bf16[2048,2048]{1,0:T(8,128)(2,1)} %constant_dynamic-update-slice_fusion.36.refs_1_.gate_ref, bf16[2048,2048]{1,0:T(8,128)(2,1)} %copy-done.32), custom_call_target="tpu_custom_call" | custom-call | flops 1 | bytes 1 | tf_op jit(solution)/shard_map/pallas_call | solution.py:489
  527.3 24.3 %shard_map.303 = bf16[4096,2048]{1,0:T(8,128)(2,1)} custom-call(bf16[1024,2048]{1,0:T(8,128)(2,1)S(1)} %copy-done.1, bf16[1024,2048]{1,0:T(8,128)(2,1)} %get-tuple-element.309.grad_gate_ref.gate_ref, bf16[1024,2048]{1,0:T(8,128)(2,1)} %get-tuple-element.310.grad_up_ref.up_ref), custom_call_target="tpu_custom_call" | custom-call | flops 1 | bytes 1 | tf_op jit(solution)/shard_map/pallas_call | solution.py:489
  558.4 10.8 %constant_dynamic-slice_fusion.10 = (bf16[512,2048]{1,0:T(8,128)(2,1)}, bf16[512,2048]{1,0:T(8,128)(2,1)}, bf16[512,2048]{1,0:T(8,128)(2,1)}, bf16[512,2048]{1,0...) fusion(bf16[4096,2048]{1,0:T(8,128)(2,1)} %shard_map.303, ...), kind=kLoop, calls=%fused_computation.210 | loop fusion | bytes 29360156 | tf_op jit(solution)/shard_map/dynamic_slice | solution.py:168
  576.5 8.1 shard_map.305
  621.6 14.2 %collective-permute-done.75 = bf16[256,2048]{1,0:T(8,128)(2,1)S(1)} collective-permute-done((bf16[256,2048]{1,0:T(8,128)(2,1)S(1)}, bf16[256,2048]{1,0:T(8,128)(2,1)S(1)}, u32[]{:S(2)}, u32[]{:S(2)}) %collective-permute-start.75) | collective-permute-done | bytes 1048608 | tf_op jit(solution)/shard_map/ppermute | solution.py:67
  635.8 11.3 %collective-permute-done.72.left_ref = bf16[512,2048]{1,0:T(8,128)(2,1)S(1)} collective-permute-done((bf16[512,2048]{1,0:T(8,128)(2,1)S(1)}, bf16[512,2048]{1,0:T(8,128)(2,1)S(1)}, u32[]{:S(2)}, u32[]{:S(2)}) %collective-permute-start.72) | collective-permute-done | bytes 2097184 | tf_op jit(solution)/shard_map/ppermute | solution.py:85
  680.4 7.8 collective-permute-done.80
  690.1 24.6 %collective-permute-done.77.left_ref = bf16[512,2048]{1,0:T(8,128)(2,1)} collective-permute-done((bf16[512,2048]{1,0:T(8,128)(2,1)}, bf16[512,2048]{1,0:T(8,128)(2,1)}, u32[]{:S(2)}, u32[]{:S(2)}) %collective-permute-start.77) | collective-permute-done | bytes 2097184 | tf_op jit(solution)/shard_map/ppermute | solution.py:85
  741.7 36.7 %collective-permute-done.88 = f32[7,2048]{1,0:T(8,128)S(1)} collective-permute-done((f32[7,2048]{1,0:T(8,128)S(1)}, f32[7,2048]{1,0:T(8,128)S(1)}, u32[]{:S(2)}, u32[]{:S(2)}) %collective-permute-start.88) | collective-permute-done | bytes 57376 | tf_op jit(solution)/shard_map/ppermute | solution.py:256
  806.4 14.6 %collective-permute-done.94 = f32[7,2048]{1,0:T(8,128)S(1)} collective-permute-done((f32[7,2048]{1,0:T(8,128)S(1)}, f32[7,2048]{1,0:T(8,128)S(1)}, u32[]{:S(2)}, u32[]{:S(2)}) %collective-permute-start.94) | collective-permute-done | bytes 57376 | tf_op jit(solution)/shard_map/ppermute | solution.py:256
  (665 shorter events, 485.9 us)
Async XLA Ops:
  2.6 32.8 %collective-permute-start.4 = (bf16[256,2048]{1,0:T(8,128)(2,1)}, bf16[256,2048]{1,0:T(8,128)(2,1)S(1)}, u32[]{:S(2)}, u32[]{:S(2)}) collective-permute-start(bf16[256,2048]{1,0:T(8,128)(2,1)} %param.17), channel_id=1, source_target_pairs={{0,1},{1,0},{2,3},{3,2},{4,5},{5,4},{6,7},{7,6},{8,9},{9,8},{10,11... | collective-permute-start | bytes 3145736 | tf_op jit(solution)/shard_map/ppermute | solution.py:63
  15.7 60.9 %collective-permute-start.9 = (bf16[256,2048]{1,0:T(8,128)(2,1)S(1)}, bf16[256,2048]{1,0:T(8,128)(2,1)}, u32[]{:S(2)}, u32[]{:S(2)}) collective-permute-start(bf16[256,2048]{1,0:T(8,128)(2,1)S(1)} %copy-done.44), channel_id=1, source_target_pairs={{0,2},{2,0},{1,3},{3,1},{4,6},{6,4},{5,7},{7,5},{8,10},{10,8},{9,1... | collective-permute-start | bytes 3145736 | tf_op jit(solution)/shard_map/ppermute | solution.py:67
  17.6 79.7 %collective-permute-start.12 = (bf16[256,2048]{1,0:T(8,128)(2,1)}, bf16[256,2048]{1,0:T(8,128)(2,1)}, u32[]{:S(2)}, u32[]{:S(2)}) collective-permute-start(bf16[256,2048]{1,0:T(8,128)(2,1)} %param.29), channel_id=1, source_target_pairs={{0,8},{8,16},{16,24},{24,28},{28,20},{20,12},{12,4},{4,0},{1,9},{9... | collective-permute-start | bytes 3145736 | tf_op jit(solution)/shard_map/ppermute | solution.py:85
  33.3 65.5 %collective-permute-start.13 = (bf16[256,2048]{1,0:T(8,128)(2,1)}, bf16[256,2048]{1,0:T(8,128)(2,1)}, u32[]{:S(2)}, u32[]{:S(2)}) collective-permute-start(bf16[256,2048]{1,0:T(8,128)(2,1)} %param.29), channel_id=1, source_target_pairs={{8,0},{16,8},{24,16},{28,24},{20,28},{12,20},{4,12},{0,4},{9,1},{1... | collective-permute-start | bytes 3145736 | tf_op jit(solution)/shard_map/ppermute | solution.py:88
  35.4 34.8 %collective-permute-start.5 = (bf16[736,512]{1,0:T(8,128)(2,1)S(1)}, bf16[736,512]{1,0:T(8,128)(2,1)}, u32[]{:S(2)}, u32[]{:S(2)}) collective-permute-start(bf16[736,512]{1,0:T(8,128)(2,1)S(1)} %collective-permute-done.2), channel_id=1, source_target_pairs={{0,8},{8,16},{16,24},{24,28},{28,20},{20,12},{12,4},{4,0},{1,9},{9... | collective-permute-start | bytes 2261000 | tf_op jit(solution)/shard_map/ppermute | solution.py:85
  35.5 36.2 %collective-permute-start.6 = (bf16[736,512]{1,0:T(8,128)(2,1)S(1)}, bf16[736,512]{1,0:T(8,128)(2,1)}, u32[]{:S(2)}, u32[]{:S(2)}) collective-permute-start(bf16[736,512]{1,0:T(8,128)(2,1)S(1)} %collective-permute-done.3), channel_id=1, source_target_pairs={{8,0},{16,8},{24,16},{28,24},{20,28},{12,20},{4,12},{0,4},{9,1},{1... | collective-permute-start | bytes 2261000 | tf_op jit(solution)/shard_map/ppermute | solution.py:88
  164.8 31.7 %collective-permute-start.29 = (bf16[8,2,1,64,640]{4,3,0,2,1:T(8,128)(2,1)}, bf16[8,2,1,64,640]{4,3,0,2,1:T(8,128)(2,1)}, u32[]{:S(2)}, u32[]{:S(2)}) collective-permute-start(bf16[8,2,1,64,640]{4,3,0,2,1:T(8,128)(2,1)} %maximum_select_fusion.2), channel_id=1, source_target_pairs={{0,1},{1,0},{2,3},{3,2},{4,5},{5,4},{6,7},{7,6},{8,9},{9,8},{10,11... | collective-permute-start | bytes 3932168 | tf_op jit(solution)/shard_map/ppermute | solution.py:63
  201.4 41.1 %collective-permute-start.34 = (bf16[256,2048]{1,0:T(8,128)(2,1)}, bf16[256,2048]{1,0:T(8,128)(2,1)S(1)}, u32[]{:S(2)}, u32[]{:S(2)}) collective-permute-start(bf16[256,2048]{1,0:T(8,128)(2,1)} %collective-permute-done.24), channel_id=1, source_target_pairs={{0,8},{8,16},{16,24},{24,28},{28,20},{20,12},{12,4},{4,0},{1,9},{9... | collective-permute-start | bytes 3145736 | tf_op jit(solution)/shard_map/ppermute | solution.py:85
  203.1 40.8 %collective-permute-start.35 = (bf16[256,2048]{1,0:T(8,128)(2,1)}, bf16[256,2048]{1,0:T(8,128)(2,1)S(1)}, u32[]{:S(2)}, u32[]{:S(2)}) collective-permute-start(bf16[256,2048]{1,0:T(8,128)(2,1)} %collective-permute-done.25), channel_id=1, source_target_pairs={{8,0},{16,8},{24,16},{28,24},{20,28},{12,20},{4,12},{0,4},{9,1},{1... | collective-permute-start | bytes 3145736 | tf_op jit(solution)/shard_map/ppermute | solution.py:88
  265.2 33.4 %collective-permute-start.30 = (bf16[256,2048]{1,0:T(8,128)(2,1)S(1)}, bf16[256,2048]{1,0:T(8,128)(2,1)}, u32[]{:S(2)}, u32[]{:S(2)}) collective-permute-start(bf16[256,2048]{1,0:T(8,128)(2,1)S(1)} %bitcast.142), channel_id=1, source_target_pairs={{0,8},{8,16},{16,24},{24,28},{28,20},{20,12},{12,4},{4,0},{1,9},{9... | collective-permute-start | bytes 3145736 | tf_op jit(solution)/shard_map/ppermute | solution.py:85
  265.6 33.2 %collective-permute-start.31 = (bf16[256,2048]{1,0:T(8,128)(2,1)S(1)}, bf16[256,2048]{1,0:T(8,128)(2,1)}, u32[]{:S(2)}, u32[]{:S(2)}) collective-permute-start(bf16[256,2048]{1,0:T(8,128)(2,1)S(1)} %bitcast.143), channel_id=1, source_target_pairs={{8,0},{16,8},{24,16},{28,24},{20,28},{12,20},{4,12},{0,4},{9,1},{1... | collective-permute-start | bytes 3145736 | tf_op jit(solution)/shard_map/ppermute | solution.py:88
  515.2 36.5 %collective-permute-start.64 = (bf16[256,2048]{1,0:T(8,128)(2,1)S(1)}, bf16[256,2048]{1,0:T(8,128)(2,1)S(1)}, u32[]{:S(2)}, u32[]{:S(2)}) collective-permute-start(bf16[256,2048]{1,0:T(8,128)(2,1)S(1)} %get-tuple-element.301), channel_id=1, source_target_pairs={{0,8},{8,16},{16,24},{24,28},{28,20},{20,12},{12,4},{4,0},{1,9},{9... | collective-permute-start | bytes 3145736 | tf_op jit(solution)/shard_map/ppermute | solution.py:85
  516.7 35.0 %collective-permute-start.65 = (bf16[256,2048]{1,0:T(8,128)(2,1)S(1)}, bf16[256,2048]{1,0:T(8,128)(2,1)}, u32[]{:S(2)}, u32[]{:S(2)}) collective-permute-start(bf16[256,2048]{1,0:T(8,128)(2,1)S(1)} %get-tuple-element.302), channel_id=1, source_target_pairs={{8,0},{16,8},{24,16},{28,24},{20,28},{12,20},{4,12},{0,4},{9,1},{1... | collective-permute-start | bytes 3145736 | tf_op jit(solution)/shard_map/ppermute | solution.py:88
  556.4 30.7 %collective-permute-start.69 = (bf16[256,2048]{1,0:T(8,128)(2,1)}, bf16[256,2048]{1,0:T(8,128)(2,1)S(1)}, u32[]{:S(2)}, u32[]{:S(2)}) collective-permute-start(bf16[256,2048]{1,0:T(8,128)(2,1)} %get-tuple-element.458), channel_id=1, source_target_pairs={{0,8},{8,16},{16,24},{24,28},{28,20},{20,12},{12,4},{4,0},{1,9},{9... | collective-permute-start | bytes 3145736 | tf_op jit(solution)/shard_map/ppermute | solution.py:85
  599.1 48.1 %collective-permute-start.72 = (bf16[512,2048]{1,0:T(8,128)(2,1)S(1)}, bf16[512,2048]{1,0:T(8,128)(2,1)S(1)}, u32[]{:S(2)}, u32[]{:S(2)}) collective-permute-start(bf16[512,2048]{1,0:T(8,128)(2,1)S(1)} %get-tuple-element.322), channel_id=1, source_target_pairs={{0,8},{8,16},{16,24},{24,28},{28,20},{20,12},{12,4},{4,0},{1,9},{9... | collective-permute-start | bytes 6291464 | tf_op jit(solution)/shard_map/ppermute | solution.py:85
  600.5 48.0 %collective-permute-start.73 = (bf16[512,2048]{1,0:T(8,128)(2,1)}, bf16[512,2048]{1,0:T(8,128)(2,1)S(1)}, u32[]{:S(2)}, u32[]{:S(2)}) collective-permute-start(bf16[512,2048]{1,0:T(8,128)(2,1)} %get-tuple-element.323), channel_id=1, source_target_pairs={{8,0},{16,8},{24,16},{28,24},{20,28},{12,20},{4,12},{0,4},{9,1},{1... | collective-permute-start | bytes 6291464 | tf_op jit(solution)/shard_map/ppermute | solution.py:88
  666.4 48.3 %collective-permute-start.77 = (bf16[512,2048]{1,0:T(8,128)(2,1)}, bf16[512,2048]{1,0:T(8,128)(2,1)}, u32[]{:S(2)}, u32[]{:S(2)}) collective-permute-start(bf16[512,2048]{1,0:T(8,128)(2,1)} %get-tuple-element.334), channel_id=1, source_target_pairs={{0,8},{8,16},{16,24},{24,28},{28,20},{20,12},{12,4},{4,0},{1,9},{9... | collective-permute-start | bytes 6291464 | tf_op jit(solution)/shard_map/ppermute | solution.py:85
  668.0 48.1 %collective-permute-start.78 = (bf16[512,2048]{1,0:T(8,128)(2,1)}, bf16[512,2048]{1,0:T(8,128)(2,1)}, u32[]{:S(2)}, u32[]{:S(2)}) collective-permute-start(bf16[512,2048]{1,0:T(8,128)(2,1)} %get-tuple-element.335), channel_id=1, source_target_pairs={{8,0},{16,8},{24,16},{28,24},{20,28},{12,20},{4,12},{0,4},{9,1},{1... | collective-permute-start | bytes 6291464 | tf_op jit(solution)/shard_map/ppermute | solution.py:88
  675.2 49.0 %collective-permute-start.85 = (bf16[256,2048]{1,0:T(8,128)(2,1)}, bf16[256,2048]{1,0:T(8,128)(2,1)}, u32[]{:S(2)}, u32[]{:S(2)}) collective-permute-start(bf16[256,2048]{1,0:T(8,128)(2,1)} %slice.395), channel_id=1, source_target_pairs={{0,1},{1,0},{2,3},{3,2},{4,5},{5,4},{6,7},{7,6},{8,9},{9,8},{10,11... | collective-permute-start | bytes 3145736 | tf_op jit(solution)/shard_map/ppermute | solution.py:63
  722.1 56.4 %collective-permute-start.81 = (bf16[512,2048]{1,0:T(8,128)(2,1)}, bf16[512,2048]{1,0:T(8,128)(2,1)}, u32[]{:S(2)}, u32[]{:S(2)}) collective-permute-start(bf16[512,2048]{1,0:T(8,128)(2,1)} %get-tuple-element.347), channel_id=1, source_target_pairs={{0,8},{8,16},{16,24},{24,28},{28,20},{20,12},{12,4},{4,0},{1,9},{9... | collective-permute-start | bytes 6291464 | tf_op jit(solution)/shard_map/ppermute | solution.py:85
  723.6 54.9 %collective-permute-start.82 = (bf16[512,2048]{1,0:T(8,128)(2,1)}, bf16[512,2048]{1,0:T(8,128)(2,1)}, u32[]{:S(2)}, u32[]{:S(2)}) collective-permute-start(bf16[512,2048]{1,0:T(8,128)(2,1)} %get-tuple-element.348), channel_id=1, source_target_pairs={{8,0},{16,8},{24,16},{28,24},{20,28},{12,20},{4,12},{0,4},{9,1},{1... | collective-permute-start | bytes 6291464 | tf_op jit(solution)/shard_map/ppermute | solution.py:88
  732.1 46.4 %collective-permute-start.84 = (bf16[368,512]{1,0:T(8,128)(2,1)S(1)}, bf16[368,512]{1,0:T(8,128)(2,1)S(1)}, u32[]{:S(2)}, u32[]{:S(2)}) collective-permute-start(bf16[368,512]{1,0:T(8,128)(2,1)S(1)} %constant_dynamic-slice_fusion.11), channel_id=1, source_target_pairs={{8,0},{16,8},{24,16},{28,24},{20,28},{12,20},{4,12},{0,4},{9,1},{1... | collective-permute-start | bytes 1130504 | tf_op jit(solution)/shard_map/ppermute | solution.py:88
  732.5 45.8 %collective-permute-start.83 = (bf16[352,512]{1,0:T(8,128)(2,1)S(1)}, bf16[352,512]{1,0:T(8,128)(2,1)S(1)}, u32[]{:S(2)}, u32[]{:S(2)}) collective-permute-start(bf16[352,512]{1,0:T(8,128)(2,1)S(1)} %constant_dynamic-slice_fusion), channel_id=1, source_target_pairs={{0,8},{8,16},{16,24},{24,28},{28,20},{20,12},{12,4},{4,0},{1,9},{9... | collective-permute-start | bytes 1081352 | tf_op jit(solution)/shard_map/ppermute | solution.py:85
  738.7 39.7 %collective-permute-start.88 = (f32[7,2048]{1,0:T(8,128)S(1)}, f32[7,2048]{1,0:T(8,128)S(1)}, u32[]{:S(2)}, u32[]{:S(2)}) collective-permute-start(f32[7,2048]{1,0:T(8,128)S(1)} %add.784), channel_id=1, source_target_pairs={{0,4},{4,0},{8,12},{12,8},{16,20},{20,16},{24,28},{28,24},{1,5},{5... | collective-permute-start | bytes 172040 | tf_op jit(solution)/shard_map/ppermute | solution.py:256
  (192 other events, 2560.8 us)

commit v3 on v2

--- a/solution.py
+++ b/solution.py
@@ -90,15 +90,16 @@
     def gather(self, block):
         return Gather(self, block)
 
-    def reduce(self, whole=None, far=None):
-        return Reduce(self, whole, far)
+    def reduce(self, whole):
+        whole = sync(whole)
+        return Reduce(self, slices, (whole,), lambda: whole)
 
 
 class Gather:
     def __init__(self, ring, block):
         self.ring, self.size, self.hop = ring, block.shape[0], 0
         self.left = self.right = block
-        self.came = [(block,)]
+        self.came, self.source = [(block,)], ()
         self.hops = ring.count // 2 if ring.unrolled else 1
         if ring.unrolled:
             whole = jnp.zeros((self.size * ring.count, block.shape[1]), block.dtype)
@@ -147,25 +148,23 @@
         down_ref[:rest] = behind_ref[:rest]
 
 
+def slices(ring, whole, offsets):
+    size = whole.shape[0] // ring.count
+    return tuple(
+        lax.dynamic_slice_in_dim(whole, ring.member(o) * size, size, 0) for o in offsets
+    )
+
+
 class Reduce:
-    def __init__(self, ring, whole=None, far=None):
-        self.ring, self.next, self.far = ring, (), far
+    def __init__(self, ring, share, source, whole=None, far=None):
+        self.ring, self.share, self.source = ring, share, source
         self.hop = self.hops = ring.count // 2 if ring.unrolled else 1
-        if whole is not None:
-            self.give(sync(whole))
-
-    def give(self, whole):
-        self.whole, self.size = whole, whole.shape[0] // self.ring.count
-        if not self.ring.unrolled:
-            return
-        if self.far is None:
-            self.far = self.share(self.hops)
-        elif self.hop < self.hops:
-            self.next = (self.share(self.hop), self.share(-self.hop))
-
-    def share(self, offset):
-        at = self.ring.member(offset) * self.size
-        return lax.dynamic_slice_in_dim(self.whole, at, self.size, 0)
+        if not ring.unrolled:
+            self.whole, self.far = whole(), ()
+        elif far is None:
+            (self.far,) = share(ring, *source, (self.hops,))
+        else:
+            self.far = far
 
     def ended(self):
         return self.hop == 0
@@ -177,22 +176,24 @@
             half = self.far.shape[0] // 32 * 16
             left, right = self.far[:half], self.far[half:]
         else:
-            block = jax.ShapeDtypeStruct(self.next[0].shape, bf16)
+            size, width = self.next[0].shape
+            step = math.gcd(width, 512)
+            inputs = (*self.next, self.left, self.right)
             left, right = tiled_call(
                 hop_kernel,
-                [block] * 2,
-                (*self.next, self.left, self.right),
-                [pl.BlockSpec(p.shape, lambda i: (0, 0)) for p in (*self.next, self.left, self.right)],
-                [pl.BlockSpec(block.shape, lambda i: (0, 0))] * 2,
-                1,
+                [jax.ShapeDtypeStruct((size, width), bf16)] * 2,
+                inputs,
+                [pl.BlockSpec((p.shape[0], step), lambda i: (0, i)) for p in inputs],
+                [pl.BlockSpec((size, step), lambda i: (0, i))] * 2,
+                width // step,
             )
         return self.ring.up(left), self.ring.down(right)
 
     def upcoming(self):
-        if not self.ring.unrolled or self.hop - 1 < 0 or not hasattr(self, "whole"):
+        if not self.ring.unrolled:
             return ()
         later = self.hop - 1
-        return tuple(self.share(o) for o in ((later, -later) if later else (0,)))
+        return self.share(self.ring, *self.source, (later, -later) if later else (0,))
 
     def accept(self, pieces, later=()):
         self.hop -= 1
@@ -213,9 +214,12 @@
 
 def phase(rings, *values):
     rings = [r for r in rings if not r.ended()]
-    pieces, later, values = sync(([r.step() for r in rings], [r.upcoming() for r in rings], values))
-    for r, p, n in zip(rings, pieces, later):
+    pieces, later, sources, values = sync(
+        ([r.step() for r in rings], [r.upcoming() for r in rings], [r.source for r in rings], values)
+    )
+    for r, p, n, source in zip(rings, pieces, later, sources):
         r.accept(p, n)
+        r.source = source
     return values[0] if len(values) == 1 else values
 
 
@@ -461,8 +465,9 @@
 
 
 def feed_forward_kernel(x_ref, gate_ref, up_ref, gate_pre_ref, up_pre_ref, hidden_ref):
-    gate_pre = dot(x_ref[...], gate_ref[...], (1, 0))
-    up_pre = dot(x_ref[...], up_ref[...], (1, 0))
+    x = x_ref[...]
+    gate_pre = dot(x, gate_ref[...].reshape(-1, TILE), (1, 0))
+    up_pre = dot(x, up_ref[...].reshape(-1, TILE), (1, 0))
     gate_pre_ref[...] = gate_pre
     up_pre_ref[...] = up_pre
     bend = jnp.tanh(gelu_scale * (gate_pre + 0.044715 * gate_pre**3))
@@ -479,9 +484,10 @@
     grad_gate_ref[...] = (grad * up_ref[...] * slope).astype(bf16)
 
 
-def grad_in_kernel(grad_gate_ref, grad_up_ref, gate_ref, up_ref, out_ref):
-    out_ref[...] = dot(grad_gate_ref[...], gate_ref[...], (1, 1)) + dot(
-        grad_up_ref[...], up_ref[...], (1, 1)
+def grad_in_kernel(grad_gate_ref, grad_up_ref, pair_ref, out_ref):
+    rows = pair_ref.shape[0] // 2
+    out_ref[...] = dot(grad_gate_ref[...], pair_ref[:rows], (1, 1)) + dot(
+        grad_up_ref[...], pair_ref[rows:], (1, 1)
     )
 
 
@@ -501,11 +507,18 @@
     return pl.BlockSpec((rows, TILE), lambda i: (0, i))
 
 
-def feed_forward(x, gate, up, part, before=()):
+def feed_forward(x, pair, part, before=()):
     tokens, width = x.shape
-    units = gate.shape[1]
+    units = pair.shape[1]
     steps = units // TILE // 2
+    size = width // lax.axis_size("dp")
+    pair = pair.reshape(-1, 2, size, units)
     wide = jax.ShapeDtypeStruct((tokens, units), f32)
+
+    def weight(which):
+        return pl.BlockSpec(
+            (width // size, None, size, TILE), lambda i: (0, which, 0, i + part * steps)
+        )
 
     def tile(rows):
         return pl.BlockSpec((rows, TILE), lambda i: (0, i + part * steps))
@@ -519,15 +532,15 @@
         grid=(steps,),
         in_specs=[
             pl.BlockSpec((tokens, width), lambda i: (0, 0)),
-            tile(width),
-            tile(width),
+            weight(0),
+            weight(1),
             *[pl.BlockSpec(memory_space=pl.ANY)] * len(before),
         ],
         out_specs=[tile(tokens)] * 3,
         input_output_aliases={3 + i: i for i in range(len(before))},
         compiler_params=pltpu.CompilerParams(vmem_limit_bytes=48 * 2**20),
         cost_estimate=light,
-    )(x, gate, up, *before)
+    )(x, pair, pair, *before)
 
 
 def pair_grad_kernel(left_ref, gate_ref, up_ref, out_ref):
@@ -557,6 +570,48 @@
     return out.transpose(0, 2, 1, 3, 4).reshape(2 * width, units)
 
 
+def pair_share_kernel(members_ref, *refs):
+    number = (len(refs) - 2) // 2
+    gate_ref, up_ref = refs[number : number + 2]
+    for left_ref, out_ref in zip(refs[:number], refs[number + 2 :]):
+        left = left_ref[...]
+        rows = left.shape[1]
+        out_ref[:rows] = dot(left, gate_ref[...], (0, 0)).astype(bf16)
+        out_ref[rows:] = dot(left, up_ref[...], (0, 0)).astype(bf16)
+
+
+def pair_share(ring, left, grad_gate, grad_up, offsets):
+    tokens, width = left.shape
+    units = grad_gate.shape[1]
+    size = width // ring.count
+    step = units // 2
+
+    def own(k):
+        return pl.BlockSpec((tokens, size), lambda j, at: (0, at[k]))
+
+    grads = pl.BlockSpec((tokens, step), lambda j, at: (0, j))
+    number = len(offsets)
+    return tuple(
+        pl.pallas_call(
+            pair_share_kernel,
+            out_shape=[jax.ShapeDtypeStruct((2 * size, units), bf16)] * number,
+            grid_spec=pltpu.PrefetchScalarGridSpec(
+                num_scalar_prefetch=1,
+                grid=(2,),
+                in_specs=[*map(own, range(number)), grads, grads],
+                out_specs=[pl.BlockSpec((2 * size, step), lambda j, at: (0, j))] * number,
+            ),
+            compiler_params=pltpu.CompilerParams(vmem_limit_bytes=40 * 2**20),
+            cost_estimate=light,
+        )(
+            jnp.stack([ring.member(o) for o in offsets]).astype(jnp.int32),
+            *[left] * number,
+            grad_gate,
+            grad_up,
+        )
+    )
+
+
 def feed_forward_back(grad, down_t, gate_pre, up_pre, far, before=()):
     half, width = grad.shape
     units = down_t.shape[1]
@@ -581,18 +636,22 @@
     )(grad, down_t, gate_pre, up_pre, *before)
 
 
-def grad_in(grad_gate, grad_up, gate, up, far):
+def grad_in(grad_gate, grad_up, pair, far):
     tokens, units = grad_gate.shape
-    half, width = tokens // 2, gate.shape[0]
+    half, width = tokens // 2, pair.shape[0] // 2
+    size = width // lax.axis_size("dp")
+    tile = max(size, 128)
+    if tile > size:
+        pair = pair.reshape(width // tile, tile // size, 2, size, units)
+        pair = pair.transpose(0, 2, 1, 3, 4).reshape(2 * width, units)
     rows = pl.BlockSpec((half, units), lambda i: (far, 0))
-    weights = pl.BlockSpec((TILE, units), lambda i: (i, 0))
     return tiled_call(
         grad_in_kernel,
         [jax.ShapeDtypeStruct((half, width), f32)],
-        (grad_gate, grad_up, gate, up),
-        [rows, rows, weights, weights],
-        [column_tile(half)],
-        width // TILE,
+        (grad_gate, grad_up, pair),
+        [rows, rows, pl.BlockSpec((2 * tile, units), lambda i: (i, 0))],
+        [pl.BlockSpec((half, tile), lambda i: (0, i))],
+        width // tile,
     )[0]
 
 
@@ -675,14 +734,15 @@
         jnp.pad(extra, ((0, 16 - gain_rows), (0, 0))),
     ]
     first = ring.gather(jnp.concatenate(parts))
-    gate, up, last = (ring.gather(w) for w in (w_gate, w_up, w_down.T))
+    pair_block, down_block = stack(w_gate, w_up), w_down.T
     inputs = tokens.astype(f32)
     vectors = layer_vectors.astype(f32)
     tokens_near = phase([first], core_swap(tokens))
     tables = phase([first], *rotary_tables(segment_ids))
     cosine, sine = tables
-    tokens_far = phase([first], chip_swap(tokens))
-    tokens_last = phase([first, gate], core_swap(tokens_far))
+    tokens_far, pair_block, down_block = phase([first], chip_swap(tokens), pair_block, down_block)
+    tokens_last, pair_block = phase([first], core_swap(tokens_far), pair_block)
+    both = ring.gather(pair_block)
 
     whole = first.whole.reshape(count, -1, line)
     starts = [sum(p.shape[0] for p in parts[:i]) for i in range(len(parts) + 1)]
@@ -720,7 +780,7 @@
             for t in (tokens_near, tokens_far, tokens_last)
         ),
     )
-    normed_all, kv_weight = phase([up], normed_all, chip_swap(kv_of(1 - chip)))
+    kv_weight, small_part = sync((chip_swap(kv_of(1 - chip)), small_part))
     qkv_weight = jnp.concatenate(
         [query_weight.reshape(-1, line), interleave(kv_of(chip), kv_weight)], axis=1
     )
@@ -731,12 +791,12 @@
     )
     half = length // 2
     attn_far = product_right(attended_low[half:], out_t)
-    attn_far, attended_low, small_part, normed_low, small_all = phase(
-        [gate], attn_far, attended_low, small_part, normed_low, chip_swap(small_part)
-    )
+    attn_far, attended_low, normed_low, small_all, down_block = phase(
+        [both], attn_far, attended_low, normed_low, chip_swap(small_part), down_block
+    )
+    attn_far, attended_low = sync((add_core(attn_far).astype(bf16), attended_low))
     attn_near = product_right(attended_low[:half], out_t)
-    attn_far, attn_near = phase([up], cross(attn_far), attn_near)
-    attn = add_core(attn_near) + attn_far
+    attn = add_core(attn_near) + chip_swap(attn_far)
     small_all = interleave(small_part, small_all)
     layer_gate_weight, layer_proj_weight, left_weight, right_weight = jnp.split(
         small_all, [layer_dim, 2 * layer_dim, 2 * layer_dim + rank], axis=1
@@ -746,17 +806,17 @@
     after_attn = inputs + rms_norm(attn, gains[1])
     mixed = (after_attn + normed + rms_norm(laurel_pre, gains[2])) * root_half
     ff_in_low = rms_norm(mixed, gains[3]).astype(bf16)
-    ff_in_low, mixed, attn, laurel_pre = phase([gate], ff_in_low, mixed, attn, laurel_pre)
-    ff_in_near, ff_in_far = phase([up], core_swap(ff_in_low), chip_swap(ff_in_low))
+    ff_in_low, mixed, attn, laurel_pre, down_block = phase(
+        [both], ff_in_low, mixed, attn, laurel_pre, down_block
+    )
+    ff_in_near, ff_in_low, mixed = sync((core_swap(ff_in_low), ff_in_low, mixed))
+    ff_in_far, down_block = phase([both], chip_swap(ff_in_low), down_block)
     ff_in_all = stack(ff_in_low, ff_in_near, ff_in_far, core_swap(ff_in_far))
-    ff_in_all = phase([gate, up], ff_in_all)
-    gate_weight, up_weight = gate.whole, up.whole
-    forward, ff_in_all = phase(
-        [last], feed_forward(ff_in_all, gate_weight, up_weight, 0), ff_in_all
-    )
-    forward, ff_in_all = phase(
-        [last], feed_forward(ff_in_all, gate_weight, up_weight, 1, forward), ff_in_all
-    )
+    ff_in_all, down_block = phase([both], ff_in_all, down_block)
+    pair = both.whole
+    last = ring.gather(down_block)
+    forward, ff_in_all = phase([last], feed_forward(ff_in_all, pair, 0), ff_in_all)
+    forward, ff_in_all = phase([last], feed_forward(ff_in_all, pair, 1, forward), ff_in_all)
     gate_pre, up_pre, hidden_low = forward
     hidden_near, hidden_far = hidden_low[:half], hidden_low[half:]
 
@@ -813,54 +873,26 @@
     far_grad, grad_ff_all = sync(
         (product_left(far_columns, hidden_low).astype(bf16), grad_ff_all)
     )
-    down_back = ring.reduce(far=far_grad)
     down_grad = product_left(grad_ff_all, hidden_low).astype(bf16)
-    if ring.unrolled:
-        down_grad, grad_ff_all = phase([down_back], down_grad, grad_ff_all)
-    down_back.give(down_grad)
+    down_back = Reduce(ring, slices, (down_grad,), lambda: down_grad, far_grad)
+    grad_ff_all = phase([down_back], grad_ff_all)
     grads_low = feed_forward_back(grad_ff_all[half:], down_t, gate_pre, up_pre, 1, grads_low)
-    ff_in_far, *grads_low = phase([down_back], grad_in(*grads_low, gate_weight, up_weight, 1), *grads_low)
-    ff_in_far, ff_in_near, *grads_low = phase(
-        [down_back], cross(ff_in_far), grad_in(*grads_low, gate_weight, up_weight, 0), *grads_low
+    ff_in_far, *grads_low = phase([down_back], grad_in(*grads_low, pair, 1), *grads_low)
+    both_back = Reduce(
+        ring, pair_share, (ff_in_all, *grads_low), lambda: pair_grad(ff_in_all, *grads_low)
+    )
+    ff_in_far, ff_in_near, both_back.far, both_back.source = phase(
+        [down_back],
+        cross(ff_in_far),
+        grad_in(*grads_low, pair, 0),
+        both_back.far,
+        both_back.source,
     )
     grad_ff_in = add_core(ff_in_near) + ff_in_far
     grad_mixed_norm, grad_gain_three = norm_back(mixed, gains[3], grad_ff_in)
     grad_branch = (grad_after_ff + grad_mixed_norm) * root_half
     grad_attn, grad_gain_one = norm_back(attn, gains[1], grad_branch)
     grad_attn_low, grad_branch = sync((grad_attn.astype(bf16), grad_branch))
-    grad_attn_far, grad_attn_near, grad_attn_low, grad_branch, both_grad = phase(
-        [down_back],
-        chip_swap(grad_attn_low),
-        core_swap(grad_attn_low),
-        grad_attn_low,
-        grad_branch,
-        pair_grad(ff_in_all, *grads_low),
-    )
-    both_back = ring.reduce(both_grad)
-    grad_attn_all = stack(grad_attn_low, grad_attn_near, grad_attn_far, core_swap(grad_attn_far))
-    grad_attended_low = product(grad_attn_all, out_t).astype(bf16)
-    grad_qkv_low, head_grads = attention_back(
-        here, qkv_raw, qkv_low, grad_attended_low, cosine, sine, segment_ids, head_scales
-    )
-    normed_far = product_right(grad_qkv_low[half:], qkv_weight)
-    normed_far, grad_qkv_low, grad_attn_all, grad_branch = phase(
-        [both_back], normed_far, grad_qkv_low, grad_attn_all, grad_branch
-    )
-
-    normed_far, grad_qkv_low = sync((add_core(normed_far).astype(bf16), grad_qkv_low))
-    normed_far = chip_swap(normed_far)
-    qkv_grad = product_left(normed_all, grad_qkv_low).astype(bf16)
-    out_grad = product_left(grad_attn_all, attended_low).astype(bf16)
-    normed_near = product_right(grad_qkv_low[:half], qkv_weight)
-    normed_far, normed_near, qkv_grad, out_grad, kv_grad, grad_branch = phase(
-        [both_back],
-        normed_far,
-        normed_near,
-        qkv_grad,
-        out_grad,
-        small_core(qkv_grad[:, line:]),
-        grad_branch,
-    )
     grad_laurel, grad_gain_two = norm_back(laurel_pre, gains[2], grad_branch)
     grad_laurel_low = grad_laurel.astype(bf16)
     grad_right = product_left(grad_laurel_low, left_low)
@@ -869,7 +901,35 @@
     small_grad = jnp.concatenate(
         [grad_layer_gate, grad_layer_proj, grad_left, grad_right], axis=1
     ).astype(bf16)
-    small_grad = small_chip(small_core(small_grad))
+    grad_attn_far, grad_attn_near, grad_attn_low, grad_branch, small_grad, grad_left_low = phase(
+        [down_back, both_back],
+        chip_swap(grad_attn_low),
+        core_swap(grad_attn_low),
+        grad_attn_low,
+        grad_branch,
+        small_grad,
+        grad_left_low,
+    )
+    grad_attn_all = stack(grad_attn_low, grad_attn_near, grad_attn_far, core_swap(grad_attn_far))
+    grad_attended_low = product(grad_attn_all, out_t).astype(bf16)
+    grad_qkv_low, head_grads = attention_back(
+        here, qkv_raw, qkv_low, grad_attended_low, cosine, sine, segment_ids, head_scales
+    )
+    normed_far = product_right(grad_qkv_low[half:], qkv_weight)
+    normed_far, grad_qkv_low, grad_attn_all, grad_branch, small_grad = phase(
+        [both_back],
+        normed_far,
+        grad_qkv_low,
+        grad_attn_all,
+        grad_branch,
+        small_core(small_grad),
+    )
+
+    normed_far, grad_qkv_low = sync((add_core(normed_far).astype(bf16), grad_qkv_low))
+    qkv_grad = product_left(normed_all, grad_qkv_low).astype(bf16)
+    out_grad = product_left(grad_attn_all, attended_low).astype(bf16)
+    kv_grad = small_core(qkv_grad[:, line:])
+    small_grad = small_chip(small_grad)
     second = jnp.concatenate(
         [
             qkv_grad[:, :line].reshape(count, -1, line),
@@ -880,7 +940,11 @@
         ],
         axis=1,
     )
-    second, grad_left_low = phase([both_back], second, grad_left_low)
+    normed_far, second, grad_qkv_low, grad_branch = phase(
+        [both_back], normed_far, second, grad_qkv_low, grad_branch
+    )
+    normed_far = chip_swap(normed_far)
+    normed_near = product_right(grad_qkv_low[:half], qkv_weight)
     second = ring.reduce(second.reshape(-1, line))
     grad_normed_heads = add_core(normed_near) + normed_far
     grad_normed = grad_branch + product_right(grad_left_low, left_weight) + grad_normed_heads

time: 852 us -> 833 us (0.978)
  waiting for transfers between devices: 327 us -> 278 us
  local copies, waits for them, and re-layouts: 143 us -> 165 us
  Pallas kernels: 150 us -> 165 us
  starting transfers between devices: 81.5 us -> 71.6 us
    ppermute x28 -> x24, waiting for transfers between devices: 186 us -> 142 us  [up(): return lax.ppermute(value, 'dp', self.ahead)]
    pallas_call x0 -> x5, Pallas kernels: none -> 31.6 us  [pair_share(): pl.pallas_call(pair_share_kernel, out_shape=[jax.ShapeDtypeStruct((2 * si...]
    ppermute x3, waiting for transfers between devices: 58.4 us -> 27.7 us  [sum_step(): lax.ppermute(value, 'dp', [(i, i ^ step) for i in range(count)])]
    ppermute x15, waiting for transfers between devices: 52.7 us -> 78.5 us  [chip_swap(): return lax.ppermute(value, 'mp', [(0, 2), (2, 0), (1, 3), (3, 1)])]
    pallas_call x12 -> x11, Pallas kernels: 74.4 us -> 54.8 us  [tiled_call(): pl.pallas_call(kernel, out_shape=outs, grid=(steps,), in_specs=specs, out...]
    unnamed x250 -> x268, local copies, waits for them, and re-layouts: 52.1 us -> 61.6 us
    ppermute x28 -> x24, starting transfers between devices: 28.3 us -> 20.7 us  [down(): return lax.ppermute(value, 'dp', self.behind)]
    dynamic_update_slice x36 -> x27, local copies, waits for them, and re-layouts: 34.8 us -> 39 us  [put(): return lax.dynamic_update_slice(whole, piece, (start, 0))]
  transfers between devices with their start and end apart: 98 -> 90, of which waited for: 56 -> 53; matrix products, arithmetic and copies ran while one was open for 25% -> 28% of each run, Pallas kernels for 17% -> 19%
where the time goes in v3:
time: 833 us; the launch traced here: 823 us
  waiting for transfers between devices  278 us (33%)
  local copies, waits for them, and re-layouts  165 us (20%)
  Pallas kernels  165 us (20%)
  other arithmetic  72.2 us (9%)
  starting transfers between devices  71.6 us (9%)
  matrix products  68.2 us (8%)
    ppermute x24, waiting for transfers between devices, up(): return lax.ppermute(value, 'dp', self.ahead)  142 us
    ppermute x15, waiting for transfers between devices, chip_swap(): return lax.ppermute(value, 'mp', [(0, 2), (2, 0), (1, 3), (3, 1)])  78.5 us
    unnamed x268, local copies, waits for them, and re-layouts  61.6 us
    pallas_call x11, Pallas kernels, tiled_call(): pl.pallas_call(kernel, out_shape=outs, grid=(steps,), in_specs=specs, out...  54.8 us
    dynamic_update_slice x27, local copies, waits for them, and re-layouts, put(): return lax.dynamic_update_slice(whole, piece, (start, 0))  39 us
    dot_general x12, matrix products, product_right(): lax.dot_general(left, right, (((1,), (1,)), ((), ())), preferred_element_...  33.9 us
    pallas_call x5, Pallas kernels, pair_share(): pl.pallas_call(pair_share_kernel, out_shape=[jax.ShapeDtypeStruct((2 * si...  31.6 us
    ppermute x24, starting transfers between devices, up(): return lax.ppermute(value, 'dp', self.ahead)  29.6 us
  transfers between devices with their start and end apart: 90, of which 53 were waited for; matrix products, arithmetic and copies ran while one was open for 28% of the time, Pallas kernels for 19%

profile of v3, /device:TPU:0, one launch (start us, length us, event | category | flops | bytes accessed | tf_op | source)
XLA Modules:
  0.0 823.3 jit_solution(4308257243555077709)
XLA Ops:
  17.6 14.0 %collective-permute-done.2 = bf16[736,512]{1,0:T(8,128)(2,1)} collective-permute-done((bf16[736,512]{1,0:T(8,128)(2,1)S(1)}, bf16[736,512]{1,0:T(8,128)(2,1)}, u32[]{:S(2)}, u32[]{:S(2)}) %collective-permute-start.2) | collective-permute-done | bytes 753696 | tf_op jit(solution)/shard_map/ppermute | solution.py:85
  152.8 19.1 %collective-permute-done.22 = bf16[256,2048]{1,0:T(8,128)(2,1)S(1)} collective-permute-done((bf16[256,2048]{1,0:T(8,128)(2,1)S(1)}, bf16[256,2048]{1,0:T(8,128)(2,1)S(1)}, u32[]{:S(2)}, u32[]{:S(2)}) %collective-permute-start.22) | collective-permute-done | bytes 1048608 | tf_op jit(solution)/shard_map/ppermute | solution.py:67
  177.4 18.5 %collective-permute-done.18 = bf16[512,2048]{1,0:T(8,128)(2,1)} collective-permute-done((bf16[512,2048]{1,0:T(8,128)(2,1)}, bf16[512,2048]{1,0:T(8,128)(2,1)}, u32[]{:S(2)}, u32[]{:S(2)}) %collective-permute-start.18) | collective-permute-done | bytes 2097184 | tf_op jit(solution)/shard_map/ppermute | solution.py:85
  202.8 22.4 %collective-permute-done.27.refs_2_ = bf16[256,2048]{1,0:T(8,128)(2,1)} collective-permute-done((bf16[256,2048]{1,0:T(8,128)(2,1)S(1)}, bf16[256,2048]{1,0:T(8,128)(2,1)}, u32[]{:S(2)}, u32[]{:S(2)}) %collective-permute-start.27) | collective-permute-done | bytes 1048608 | tf_op jit(solution)/shard_map/ppermute | solution.py:67
  225.2 19.4 %collective-permute-done.25 = bf16[512,2048]{1,0:T(8,128)(2,1)} collective-permute-done((bf16[512,2048]{1,0:T(8,128)(2,1)}, bf16[512,2048]{1,0:T(8,128)(2,1)}, u32[]{:S(2)}, u32[]{:S(2)}) %collective-permute-start.25) | collective-permute-done | bytes 2097184 | tf_op jit(solution)/shard_map/ppermute | solution.py:85
  259.9 11.8 %collective-permute-done.28 = bf16[256,2048]{1,0:T(8,128)(2,1)S(1)} collective-permute-done((bf16[256,2048]{1,0:T(8,128)(2,1)S(1)}, bf16[256,2048]{1,0:T(8,128)(2,1)S(1)}, u32[]{:S(2)}, u32[]{:S(2)}) %collective-permute-start.28) | collective-permute-done | bytes 1048608 | tf_op jit(solution)/shard_map/ppermute | solution.py:85
  285.1 14.2 %shard_map.292 = (f32[1024,2048]{1,0:T(8,128)}, f32[1024,2048]{1,0:T(8,128)}, bf16[1024,2048]{1,0:T(8,128)(2,1)S(1)}) custom-call(bf16[1024,2048]{1,0:T(8,128)(2,1)} %copy-done, bf16[8,2,256,2048]{3,2,1,0:T(8,128)(2,1)} %bitcast.118, bf16[8,2,256,2048]{3,2,1,0:T(8,128)(2,1)} %bitcast.119), custom_call_target="tpu_custom_call" | custom-call | flops 1 | bytes 1 | tf_op jit(solution)/shard_map/pallas_call | solution.py:529
  305.7 14.2 %shard_map.293 = (f32[1024,2048]{1,0:T(8,128)}, f32[1024,2048]{1,0:T(8,128)}, bf16[1024,2048]{1,0:T(8,128)(2,1)S(1)}) custom-call(bf16[1024,2048]{1,0:T(8,128)(2,1)} %copy-done, bf16[8,2,256,2048]{3,2,1,0:T(8,128)(2,1)} %bitcast.120, bf16[8,2,256,2048]{3,2,1,0:T(8,128)(2,1)} %bitcast.121, ...), custom_call_target="tpu_custom_call", output_to_operand_aliasing={{0}: (3, {}), {1}: (4, {}), {2}: (5, {})} | custom-call | flops 1 | bytes 1 | tf_op jit(solution)/shard_map/pallas_call | solution.py:529
  333.4 10.1 %fusion.34 = f32[512,1280]{1,0:T(8,128)} fusion(bf16[1280,2048]{1,0:T(8,128)(2,1)} %get-tuple-element.531, bf16[1024,2048]{1,0:T(8,128)(2,1)S(1)} %get-tuple-element.280), kind=kOutput, calls=%fused_computation.103 | convolution fusion | flops 2684354560 | bytes 9961472 | tf_op jit(solution)/shard_map/dot_general | solution.py:45
  358.3 9.2 %collective-permute-done.37 = bf16[128,2048]{1,0:T(8,128)(2,1)S(1)} collective-permute-done((bf16[128,2048]{1,0:T(8,128)(2,1)S(1)}, bf16[128,2048]{1,0:T(8,128)(2,1)S(1)}, u32[]{:S(2)}, u32[]{:S(2)}) %collective-permute-start.37) | collective-permute-done | bytes 524320 | tf_op jit(solution)/shard_map/ppermute | solution.py:85
  406.9 12.7 %shard_map.296 = (bf16[1024,2048]{1,0:T(8,128)(2,1)}, bf16[1024,2048]{1,0:T(8,128)(2,1)}) custom-call(bf16[512,2048]{1,0:T(8,128)(2,1)S(1)} %shard_map.295.refs_0_, bf16[2048,2048]{1,0:T(8,128)(2,1)} %get-tuple-element.542.refs_1_, f32[1024,2048]{1,0:T(8,128)} %get-tuple-element.292.refs_2_, f32[1024,2048]{1,0:T(8,128)} %get-tuple-element.293.refs_3_), custom_call_target="tpu_custom_call" | custom-call | flops 1 | bytes 1 | tf_op jit(solution)/shard_map/pallas_call | solution.py:622
  419.6 9.3 %collective-permute-done.45.refs_2_ = bf16[256,2048]{1,0:T(8,128)(2,1)S(1)} collective-permute-done((bf16[256,2048]{1,0:T(8,128)(2,1)S(1)}, bf16[256,2048]{1,0:T(8,128)(2,1)S(1)}, u32[]{:S(2)}, u32[]{:S(2)}) %collective-permute-start.45) | collective-permute-done | bytes 1048608 | tf_op jit(solution)/shard_map/ppermute | solution.py:67
  437.8 9.6 %convolution_convert_fusion = bf16[2048,2048]{1,0:T(8,128)(2,1)S(1)} fusion(bf16[1024,2048]{1,0:T(8,128)(2,1)S(1)} %shard_map.297, bf16[1024,2048]{1,0:T(8,128)(2,1)S(1)} %copy-done.25), kind=kOutput, calls=%fused_computation | convolution fusion | flops 8594128896 | bytes 16777216 | tf_op jit(solution)/shard_map/dot_general | solution.py:41
  454.1 12.7 %shard_map.299 = (bf16[1024,2048]{1,0:T(8,128)(2,1)}, bf16[1024,2048]{1,0:T(8,128)(2,1)}) custom-call(bf16[512,2048]{1,0:T(8,128)(2,1)S(1)} %slice.273.refs_0_, bf16[2048,2048]{1,0:T(8,128)(2,1)} %get-tuple-element.542.refs_1_, f32[1024,2048]{1,0:T(8,128)} %get-tuple-element.292.refs_2_, ...), custom_call_target="tpu_custom_call", output_to_operand_aliasing={{0}: (4, {}), {1}: (5, {})} | custom-call | flops 1 | bytes 1 | tf_op jit(solution)/shard_map/pallas_call | solution.py:622
  466.8 14.4 %shard_map.300 = f32[512,2048]{1,0:T(8,128)S(1)} custom-call(bf16[1024,2048]{1,0:T(8,128)(2,1)} %get-tuple-element.388.grad_gate_ref.refs_1_.refs_2_, bf16[1024,2048]{1,0:T(8,128)(2,1)} %get-tuple-element.389.grad_up_ref.refs_2_.refs_3_, bf16[4096,2048]{1,0:T(8,128)(2,1)} %copy-done.46), custom_call_target="tpu_custom_call" | custom-call | flops 1 | bytes 1 | tf_op jit(solution)/shard_map/pallas_call | solution.py:495
  493.9 15.1 %shard_map.302 = f32[512,2048]{1,0:T(8,128)S(1)} custom-call(bf16[1024,2048]{1,0:T(8,128)(2,1)} %get-tuple-element.388.grad_gate_ref.refs_1_.refs_2_, bf16[1024,2048]{1,0:T(8,128)(2,1)} %get-tuple-element.389.grad_up_ref.refs_2_.refs_3_, bf16[4096,2048]{1,0:T(8,128)(2,1)} %copy-done.46), custom_call_target="tpu_custom_call" | custom-call | flops 1 | bytes 1 | tf_op jit(solution)/shard_map/pallas_call | solution.py:495
  531.0 7.7 shard_map.305
  556.0 17.6 %collective-permute-done.58.left_ref = bf16[256,2048]{1,0:T(8,128)(2,1)S(1)} collective-permute-done((bf16[256,2048]{1,0:T(8,128)(2,1)}, bf16[256,2048]{1,0:T(8,128)(2,1)S(1)}, u32[]{:S(2)}, u32[]{:S(2)}) %collective-permute-start.58) | collective-permute-done | bytes 1048608 | tf_op jit(solution)/shard_map/ppermute | solution.py:85
  609.3 8.1 shard_map.309
  679.2 7.7 collective-permute-done.67.left_ref
  710.9 8.5 %collective-permute-done.77 = bf16[256,2048]{1,0:T(8,128)(2,1)} collective-permute-done((bf16[256,2048]{1,0:T(8,128)(2,1)}, bf16[256,2048]{1,0:T(8,128)(2,1)}, u32[]{:S(2)}, u32[]{:S(2)}) %collective-permute-start.77) | collective-permute-done | bytes 1048608 | tf_op jit(solution)/shard_map/ppermute | solution.py:67
  742.8 14.2 %collective-permute-done.80 = f32[7,2048]{1,0:T(8,128)S(1)} collective-permute-done((f32[7,2048]{1,0:T(8,128)S(1)}, f32[7,2048]{1,0:T(8,128)S(1)}, u32[]{:S(2)}, u32[]{:S(2)}) %collective-permute-start.80) | collective-permute-done | bytes 57376 | tf_op jit(solution)/shard_map/ppermute | solution.py:260
  766.7 8.4 %collective-permute-done.81.left_ref = bf16[720,512]{1,0:T(8,128)(2,1)S(1)} collective-permute-done((bf16[720,512]{1,0:T(8,128)(2,1)S(1)}, bf16[720,512]{1,0:T(8,128)(2,1)S(1)}, u32[]{:S(2)}, u32[]{:S(2)}) %collective-permute-start.81) | collective-permute-done | bytes 737312 | tf_op jit(solution)/shard_map/ppermute | solution.py:85
  785.2 13.5 %collective-permute-done.86 = f32[7,2048]{1,0:T(8,128)S(1)} collective-permute-done((f32[7,2048]{1,0:T(8,128)S(1)}, f32[7,2048]{1,0:T(8,128)S(1)}, u32[]{:S(2)}, u32[]{:S(2)}) %collective-permute-start.86) | collective-permute-done | bytes 57376 | tf_op jit(solution)/shard_map/ppermute | solution.py:260
  (660 shorter events, 507.7 us)
Async XLA Ops:
  2.5 30.6 %collective-permute-start.4 = (bf16[256,2048]{1,0:T(8,128)(2,1)}, bf16[256,2048]{1,0:T(8,128)(2,1)S(1)}, u32[]{:S(2)}, u32[]{:S(2)}) collective-permute-start(bf16[256,2048]{1,0:T(8,128)(2,1)} %param.17), channel_id=1, source_target_pairs={{0,1},{1,0},{2,3},{3,2},{4,5},{5,4},{6,7},{7,6},{8,9},{9,8},{10,11... | collective-permute-start | bytes 3145736 | tf_op jit(solution)/shard_map/ppermute | solution.py:63
  15.6 46.0 %collective-permute-start.9 = (bf16[256,2048]{1,0:T(8,128)(2,1)}, bf16[256,2048]{1,0:T(8,128)(2,1)}, u32[]{:S(2)}, u32[]{:S(2)}) collective-permute-start(bf16[256,2048]{1,0:T(8,128)(2,1)} %param.17), channel_id=1, source_target_pairs={{0,2},{2,0},{1,3},{3,1},{4,6},{6,4},{5,7},{7,5},{8,10},{10,8},{9,1... | collective-permute-start | bytes 3145736 | tf_op jit(solution)/shard_map/ppermute | solution.py:67
  93.3 47.0 %collective-permute-start.13 = (bf16[512,2048]{1,0:T(8,128)(2,1)S(1)}, bf16[512,2048]{1,0:T(8,128)(2,1)}, u32[]{:S(2)}, u32[]{:S(2)}) collective-permute-start(bf16[512,2048]{1,0:T(8,128)(2,1)S(1)} %shard_map.288), channel_id=1, source_target_pairs={{0,8},{8,16},{16,24},{24,28},{28,20},{20,12},{12,4},{4,0},{1,9},{9... | collective-permute-start | bytes 6291464 | tf_op jit(solution)/shard_map/ppermute | solution.py:85
  94.9 46.8 %collective-permute-start.14 = (bf16[512,2048]{1,0:T(8,128)(2,1)S(1)}, bf16[512,2048]{1,0:T(8,128)(2,1)}, u32[]{:S(2)}, u32[]{:S(2)}) collective-permute-start(bf16[512,2048]{1,0:T(8,128)(2,1)S(1)} %shard_map.288), channel_id=1, source_target_pairs={{8,0},{16,8},{24,16},{28,24},{20,28},{12,20},{4,12},{0,4},{9,1},{1... | collective-permute-start | bytes 6291464 | tf_op jit(solution)/shard_map/ppermute | solution.py:88
  147.9 47.9 %collective-permute-start.18 = (bf16[512,2048]{1,0:T(8,128)(2,1)}, bf16[512,2048]{1,0:T(8,128)(2,1)}, u32[]{:S(2)}, u32[]{:S(2)}) collective-permute-start(bf16[512,2048]{1,0:T(8,128)(2,1)} %collective-permute-done.13), channel_id=1, source_target_pairs={{0,8},{8,16},{16,24},{24,28},{28,20},{20,12},{12,4},{4,0},{1,9},{9... | collective-permute-start | bytes 6291464 | tf_op jit(solution)/shard_map/ppermute | solution.py:85
  148.6 47.6 %collective-permute-start.19 = (bf16[512,2048]{1,0:T(8,128)(2,1)}, bf16[512,2048]{1,0:T(8,128)(2,1)}, u32[]{:S(2)}, u32[]{:S(2)}) collective-permute-start(bf16[512,2048]{1,0:T(8,128)(2,1)} %collective-permute-done.14), channel_id=1, source_target_pairs={{8,0},{16,8},{24,16},{28,24},{20,28},{12,20},{4,12},{0,4},{9,1},{1... | collective-permute-start | bytes 6291464 | tf_op jit(solution)/shard_map/ppermute | solution.py:88
  196.3 48.4 %collective-permute-start.25 = (bf16[512,2048]{1,0:T(8,128)(2,1)}, bf16[512,2048]{1,0:T(8,128)(2,1)}, u32[]{:S(2)}, u32[]{:S(2)}) collective-permute-start(bf16[512,2048]{1,0:T(8,128)(2,1)} %collective-permute-done.18), channel_id=1, source_target_pairs={{0,8},{8,16},{16,24},{24,28},{28,20},{20,12},{12,4},{4,0},{1,9},{9... | collective-permute-start | bytes 6291464 | tf_op jit(solution)/shard_map/ppermute | solution.py:85
  196.7 48.1 %collective-permute-start.26 = (bf16[512,2048]{1,0:T(8,128)(2,1)}, bf16[512,2048]{1,0:T(8,128)(2,1)}, u32[]{:S(2)}, u32[]{:S(2)}) collective-permute-start(bf16[512,2048]{1,0:T(8,128)(2,1)} %collective-permute-done.19), channel_id=1, source_target_pairs={{8,0},{16,8},{24,16},{28,24},{20,28},{12,20},{4,12},{0,4},{9,1},{1... | collective-permute-start | bytes 6291464 | tf_op jit(solution)/shard_map/ppermute | solution.py:88
  451.8 31.2 %collective-permute-start.50 = (bf16[256,2048]{1,0:T(8,128)(2,1)S(1)}, bf16[256,2048]{1,0:T(8,128)(2,1)S(1)}, u32[]{:S(2)}, u32[]{:S(2)}) collective-permute-start(bf16[256,2048]{1,0:T(8,128)(2,1)S(1)} %get-tuple-element.304), channel_id=1, source_target_pairs={{0,8},{8,16},{16,24},{24,28},{28,20},{20,12},{12,4},{4,0},{1,9},{9... | collective-permute-start | bytes 3145736 | tf_op jit(solution)/shard_map/ppermute | solution.py:85
  453.4 29.7 %collective-permute-start.51 = (bf16[256,2048]{1,0:T(8,128)(2,1)S(1)}, bf16[256,2048]{1,0:T(8,128)(2,1)S(1)}, u32[]{:S(2)}, u32[]{:S(2)}) collective-permute-start(bf16[256,2048]{1,0:T(8,128)(2,1)S(1)} %get-tuple-element.305), channel_id=1, source_target_pairs={{8,0},{16,8},{24,16},{28,24},{20,28},{12,20},{4,12},{0,4},{9,1},{1... | collective-permute-start | bytes 3145736 | tf_op jit(solution)/shard_map/ppermute | solution.py:88
  487.9 29.3 %collective-permute-start.52 = (bf16[256,2048]{1,0:T(8,128)(2,1)S(1)}, bf16[256,2048]{1,0:T(8,128)(2,1)S(1)}, u32[]{:S(2)}, u32[]{:S(2)}) collective-permute-start(bf16[256,2048]{1,0:T(8,128)(2,1)S(1)} %get-tuple-element.316), channel_id=1, source_target_pairs={{0,8},{8,16},{16,24},{24,28},{28,20},{20,12},{12,4},{4,0},{1,9},{9... | collective-permute-start | bytes 3145736 | tf_op jit(solution)/shard_map/ppermute | solution.py:85
  526.9 29.1 %collective-permute-start.57 = (bf16[256,2048]{1,0:T(8,128)(2,1)}, bf16[256,2048]{1,0:T(8,128)(2,1)}, u32[]{:S(2)}, u32[]{:S(2)}) collective-permute-start(bf16[256,2048]{1,0:T(8,128)(2,1)} %get-tuple-element.328), channel_id=1, source_target_pairs={{8,0},{16,8},{24,16},{28,24},{20,28},{12,20},{4,12},{0,4},{9,1},{1... | collective-permute-start | bytes 3145736 | tf_op jit(solution)/shard_map/ppermute | solution.py:88
  528.9 44.7 %collective-permute-start.58 = (bf16[256,2048]{1,0:T(8,128)(2,1)}, bf16[256,2048]{1,0:T(8,128)(2,1)S(1)}, u32[]{:S(2)}, u32[]{:S(2)}) collective-permute-start(bf16[256,2048]{1,0:T(8,128)(2,1)} %get-tuple-element.519), channel_id=1, source_target_pairs={{0,8},{8,16},{16,24},{24,28},{28,20},{20,12},{12,4},{4,0},{1,9},{9... | collective-permute-start | bytes 3145736 | tf_op jit(solution)/shard_map/ppermute | solution.py:85
  530.4 44.4 %collective-permute-start.59 = (bf16[256,2048]{1,0:T(8,128)(2,1)}, bf16[256,2048]{1,0:T(8,128)(2,1)S(1)}, u32[]{:S(2)}, u32[]{:S(2)}) collective-permute-start(bf16[256,2048]{1,0:T(8,128)(2,1)} %get-tuple-element.518), channel_id=1, source_target_pairs={{8,0},{16,8},{24,16},{28,24},{20,28},{12,20},{4,12},{0,4},{9,1},{1... | collective-permute-start | bytes 3145736 | tf_op jit(solution)/shard_map/ppermute | solution.py:88
  579.7 48.3 %collective-permute-start.63 = (bf16[512,2048]{1,0:T(8,128)(2,1)}, bf16[512,2048]{1,0:T(8,128)(2,1)}, u32[]{:S(2)}, u32[]{:S(2)}) collective-permute-start(bf16[512,2048]{1,0:T(8,128)(2,1)} %get-tuple-element.348), channel_id=1, source_target_pairs={{0,8},{8,16},{16,24},{24,28},{28,20},{20,12},{12,4},{4,0},{1,9},{9... | collective-permute-start | bytes 6291464 | tf_op jit(solution)/shard_map/ppermute | solution.py:85
  581.2 48.1 %collective-permute-start.64 = (bf16[512,2048]{1,0:T(8,128)(2,1)}, bf16[512,2048]{1,0:T(8,128)(2,1)}, u32[]{:S(2)}, u32[]{:S(2)}) collective-permute-start(bf16[512,2048]{1,0:T(8,128)(2,1)} %get-tuple-element.349), channel_id=1, source_target_pairs={{8,0},{16,8},{24,16},{28,24},{20,28},{12,20},{4,12},{0,4},{9,1},{1... | collective-permute-start | bytes 6291464 | tf_op jit(solution)/shard_map/ppermute | solution.py:88
  588.7 31.1 %collective-permute-start.66 = (bf16[8,2,64,640]{3,2,1,0:T(8,128)(2,1)}, bf16[8,2,64,640]{3,2,1,0:T(8,128)(2,1)}, u32[]{:S(2)}, u32[]{:S(2)}) collective-permute-start(bf16[8,2,64,640]{3,2,1,0:T(8,128)(2,1)} %dynamic-slice_bitcast_fusion), channel_id=1, source_target_pairs={{0,1},{1,0},{2,3},{3,2},{4,5},{5,4},{6,7},{7,6},{8,9},{9,8},{10,11... | collective-permute-start | bytes 3932168 | tf_op jit(solution)/shard_map/ppermute | solution.py:63
  631.3 36.5 %collective-permute-start.71 = (bf16[8,64,640]{2,1,0:T(8,128)(2,1)}, bf16[8,64,640]{2,1,0:T(8,128)(2,1)}, u32[]{:S(2)}, u32[]{:S(2)}) collective-permute-start(bf16[8,64,640]{2,1,0:T(8,128)(2,1)} %dynamic-slice_bitcast_fusion.2), channel_id=1, source_target_pairs={{0,2},{2,0},{1,3},{3,1},{4,6},{6,4},{5,7},{7,5},{8,10},{10,8},{9,1... | collective-permute-start | bytes 1966088 | tf_op jit(solution)/shard_map/ppermute | solution.py:67
  638.5 48.5 %collective-permute-start.67 = (bf16[512,2048]{1,0:T(8,128)(2,1)}, bf16[512,2048]{1,0:T(8,128)(2,1)}, u32[]{:S(2)}, u32[]{:S(2)}) collective-permute-start(bf16[512,2048]{1,0:T(8,128)(2,1)} %get-tuple-element.366), channel_id=1, source_target_pairs={{0,8},{8,16},{16,24},{24,28},{28,20},{20,12},{12,4},{4,0},{1,9},{9... | collective-permute-start | bytes 6291464 | tf_op jit(solution)/shard_map/ppermute | solution.py:85
  639.9 48.0 %collective-permute-start.68 = (bf16[512,2048]{1,0:T(8,128)(2,1)}, bf16[512,2048]{1,0:T(8,128)(2,1)}, u32[]{:S(2)}, u32[]{:S(2)}) collective-permute-start(bf16[512,2048]{1,0:T(8,128)(2,1)} %get-tuple-element.367), channel_id=1, source_target_pairs={{8,0},{16,8},{24,16},{28,24},{20,28},{12,20},{4,12},{0,4},{9,1},{1... | collective-permute-start | bytes 6291464 | tf_op jit(solution)/shard_map/ppermute | solution.py:88
  699.8 57.1 %collective-permute-start.72 = (bf16[512,2048]{1,0:T(8,128)(2,1)}, bf16[512,2048]{1,0:T(8,128)(2,1)}, u32[]{:S(2)}, u32[]{:S(2)}) collective-permute-start(bf16[512,2048]{1,0:T(8,128)(2,1)} %get-tuple-element.384), channel_id=1, source_target_pairs={{0,8},{8,16},{16,24},{24,28},{28,20},{20,12},{12,4},{4,0},{1,9},{9... | collective-permute-start | bytes 6291464 | tf_op jit(solution)/shard_map/ppermute | solution.py:85
  701.1 55.9 %collective-permute-start.73 = (bf16[512,2048]{1,0:T(8,128)(2,1)S(1)}, bf16[512,2048]{1,0:T(8,128)(2,1)}, u32[]{:S(2)}, u32[]{:S(2)}) collective-permute-start(bf16[512,2048]{1,0:T(8,128)(2,1)S(1)} %get-tuple-element.385), channel_id=1, source_target_pairs={{8,0},{16,8},{24,16},{28,24},{20,28},{12,20},{4,12},{0,4},{9,1},{1... | collective-permute-start | bytes 6291464 | tf_op jit(solution)/shard_map/ppermute | solution.py:88
  706.8 50.2 %collective-permute-start.75 = (bf16[368,512]{1,0:T(8,128)(2,1)S(1)}, bf16[368,512]{1,0:T(8,128)(2,1)S(1)}, u32[]{:S(2)}, u32[]{:S(2)}) collective-permute-start(bf16[368,512]{1,0:T(8,128)(2,1)S(1)} %constant_dynamic-slice_fusion.9), channel_id=1, source_target_pairs={{8,0},{16,8},{24,16},{28,24},{20,28},{12,20},{4,12},{0,4},{9,1},{1... | collective-permute-start | bytes 1130504 | tf_op jit(solution)/shard_map/ppermute | solution.py:88
  709.3 47.7 %collective-permute-start.74 = (bf16[352,512]{1,0:T(8,128)(2,1)}, bf16[352,512]{1,0:T(8,128)(2,1)S(1)}, u32[]{:S(2)}, u32[]{:S(2)}) collective-permute-start(bf16[352,512]{1,0:T(8,128)(2,1)} %constant_dynamic-slice_fusion), channel_id=1, source_target_pairs={{0,8},{8,16},{16,24},{24,28},{28,20},{20,12},{12,4},{4,0},{1,9},{9... | collective-permute-start | bytes 1081352 | tf_op jit(solution)/shard_map/ppermute | solution.py:85
  (192 other events, 2241.8 us)

commit v4 on v3

--- a/solution.py
+++ b/solution.py
@@ -177,7 +177,7 @@
             left, right = self.far[:half], self.far[half:]
         else:
             size, width = self.next[0].shape
-            step = math.gcd(width, 512)
+            step = math.gcd(width, 1024)
             inputs = (*self.next, self.left, self.right)
             left, right = tiled_call(
                 hop_kernel,
@@ -269,11 +269,11 @@
 
 def stack(*pieces):
     rows, width = pieces[0].shape
-    step = width // 4
+    step = width // 2
     return pl.pallas_call(
         stack_kernel,
         out_shape=jax.ShapeDtypeStruct((rows * len(pieces), width), pieces[0].dtype),
-        grid=(4,),
+        grid=(2,),
         in_specs=[pl.BlockSpec((rows, step), lambda i: (0, i))] * len(pieces),
         out_specs=pl.BlockSpec((rows * len(pieces), step), lambda i: (0, i)),
         compiler_params=pltpu.CompilerParams(vmem_limit_bytes=24 * 2**20),
@@ -812,9 +812,9 @@
     ff_in_near, ff_in_low, mixed = sync((core_swap(ff_in_low), ff_in_low, mixed))
     ff_in_far, down_block = phase([both], chip_swap(ff_in_low), down_block)
     ff_in_all = stack(ff_in_low, ff_in_near, ff_in_far, core_swap(ff_in_far))
-    ff_in_all, down_block = phase([both], ff_in_all, down_block)
+    last = ring.gather(down_block)
+    ff_in_all = phase([both], ff_in_all)
     pair = both.whole
-    last = ring.gather(down_block)
     forward, ff_in_all = phase([last], feed_forward(ff_in_all, pair, 0), ff_in_all)
     forward, ff_in_all = phase([last], feed_forward(ff_in_all, pair, 1, forward), ff_in_all)
     gate_pre, up_pre, hidden_low = forward
@@ -892,7 +892,9 @@
     grad_mixed_norm, grad_gain_three = norm_back(mixed, gains[3], grad_ff_in)
     grad_branch = (grad_after_ff + grad_mixed_norm) * root_half
     grad_attn, grad_gain_one = norm_back(attn, gains[1], grad_branch)
-    grad_attn_low, grad_branch = sync((grad_attn.astype(bf16), grad_branch))
+    grad_attn_low, grad_branch, both_back.source = sync(
+        (grad_attn.astype(bf16), grad_branch, both_back.source)
+    )
     grad_laurel, grad_gain_two = norm_back(laurel_pre, gains[2], grad_branch)
     grad_laurel_low = grad_laurel.astype(bf16)
     grad_right = product_left(grad_laurel_low, left_low)
@@ -940,11 +942,11 @@
         ],
         axis=1,
     )
-    normed_far, second, grad_qkv_low, grad_branch = phase(
-        [both_back], normed_far, second, grad_qkv_low, grad_branch
+    normed_near = product_right(grad_qkv_low[:half], qkv_weight)
+    normed_far, normed_near, second, grad_branch = phase(
+        [both_back], normed_far, normed_near, second, grad_branch
     )
     normed_far = chip_swap(normed_far)
-    normed_near = product_right(grad_qkv_low[:half], qkv_weight)
     second = ring.reduce(second.reshape(-1, line))
     grad_normed_heads = add_core(normed_near) + normed_far
     grad_normed = grad_branch + product_right(grad_left_low, left_weight) + grad_normed_heads

time: 833 us -> 818 us (0.982)
    unnamed x268 -> x272, local copies, waits for them, and re-layouts: 61.6 us -> 60.7 us
where the time goes in v4:
time: 818 us; the launch traced here: 809 us
  waiting for transfers between devices  274 us (33%)
  local copies, waits for them, and re-layouts  163 us (20%)
  Pallas kernels  158 us (19%)
  other arithmetic  72.1 us (9%)
  starting transfers between devices  71.9 us (9%)
  matrix products  67.9 us (8%)
    ppermute x24, waiting for transfers between devices, up(): return lax.ppermute(value, 'dp', self.ahead)  142 us
    ppermute x15, waiting for transfers between devices, chip_swap(): return lax.ppermute(value, 'mp', [(0, 2), (2, 0), (1, 3), (3, 1)])  75.2 us
    unnamed x272, local copies, waits for them, and re-layouts  60.7 us
    pallas_call x11, Pallas kernels, tiled_call(): pl.pallas_call(kernel, out_shape=outs, grid=(steps,), in_specs=specs, out...  50.6 us
    dynamic_update_slice x27, local copies, waits for them, and re-layouts, put(): return lax.dynamic_update_slice(whole, piece, (start, 0))  39.3 us
    dot_general x12, matrix products, product_right(): lax.dot_general(left, right, (((1,), (1,)), ((), ())), preferred_element_...  33.9 us
    pallas_call x5, Pallas kernels, pair_share(): pl.pallas_call(pair_share_kernel, out_shape=[jax.ShapeDtypeStruct((2 * si...  31.1 us
    ppermute x24, starting transfers between devices, up(): return lax.ppermute(value, 'dp', self.ahead)  29.1 us
  transfers between devices with their start and end apart: 90, of which 53 were waited for; matrix products, arithmetic and copies ran while one was open for 28% of the time, Pallas kernels for 19%

profile of v4, /device:TPU:0, one launch (start us, length us, event | category | flops | bytes accessed | tf_op | source)
XLA Modules:
  0.0 808.9 jit_solution(12904016457552260244)
XLA Ops:
  17.6 14.0 %collective-permute-done.2 = bf16[736,512]{1,0:T(8,128)(2,1)} collective-permute-done((bf16[736,512]{1,0:T(8,128)(2,1)S(1)}, bf16[736,512]{1,0:T(8,128)(2,1)}, u32[]{:S(2)}, u32[]{:S(2)}) %collective-permute-start.2) | collective-permute-done | bytes 753696 | tf_op jit(solution)/shard_map/ppermute | solution.py:85
  152.8 19.0 %collective-permute-done.22 = bf16[256,2048]{1,0:T(8,128)(2,1)S(1)} collective-permute-done((bf16[256,2048]{1,0:T(8,128)(2,1)S(1)}, bf16[256,2048]{1,0:T(8,128)(2,1)S(1)}, u32[]{:S(2)}, u32[]{:S(2)}) %collective-permute-start.22) | collective-permute-done | bytes 1048608 | tf_op jit(solution)/shard_map/ppermute | solution.py:67
  177.4 18.5 %collective-permute-done.18 = bf16[512,2048]{1,0:T(8,128)(2,1)} collective-permute-done((bf16[512,2048]{1,0:T(8,128)(2,1)}, bf16[512,2048]{1,0:T(8,128)(2,1)}, u32[]{:S(2)}, u32[]{:S(2)}) %collective-permute-start.18) | collective-permute-done | bytes 2097184 | tf_op jit(solution)/shard_map/ppermute | solution.py:85
  206.5 18.7 %collective-permute-done.27.refs_2_ = bf16[256,2048]{1,0:T(8,128)(2,1)} collective-permute-done((bf16[256,2048]{1,0:T(8,128)(2,1)S(1)}, bf16[256,2048]{1,0:T(8,128)(2,1)}, u32[]{:S(2)}, u32[]{:S(2)}) %collective-permute-start.27) | collective-permute-done | bytes 1048608 | tf_op jit(solution)/shard_map/ppermute | solution.py:67
  225.2 19.4 %collective-permute-done.25 = bf16[512,2048]{1,0:T(8,128)(2,1)} collective-permute-done((bf16[512,2048]{1,0:T(8,128)(2,1)}, bf16[512,2048]{1,0:T(8,128)(2,1)}, u32[]{:S(2)}, u32[]{:S(2)}) %collective-permute-start.25) | collective-permute-done | bytes 2097184 | tf_op jit(solution)/shard_map/ppermute | solution.py:85
  261.2 11.0 %collective-permute-done.30 = bf16[256,2048]{1,0:T(8,128)(2,1)S(1)} collective-permute-done((bf16[256,2048]{1,0:T(8,128)(2,1)S(1)}, bf16[256,2048]{1,0:T(8,128)(2,1)S(1)}, u32[]{:S(2)}, u32[]{:S(2)}) %collective-permute-start.30) | collective-permute-done | bytes 1048608 | tf_op jit(solution)/shard_map/ppermute | solution.py:85
  280.0 14.2 %shard_map.292 = (f32[1024,2048]{1,0:T(8,128)}, f32[1024,2048]{1,0:T(8,128)}, bf16[1024,2048]{1,0:T(8,128)(2,1)S(1)}) custom-call(bf16[1024,2048]{1,0:T(8,128)(2,1)} %copy-done, bf16[8,2,256,2048]{3,2,1,0:T(8,128)(2,1)} %bitcast.118, bf16[8,2,256,2048]{3,2,1,0:T(8,128)(2,1)} %bitcast.119), custom_call_target="tpu_custom_call" | custom-call | flops 1 | bytes 1 | tf_op jit(solution)/shard_map/pallas_call | solution.py:529
  300.6 14.3 %shard_map.293 = (f32[1024,2048]{1,0:T(8,128)}, f32[1024,2048]{1,0:T(8,128)}, bf16[1024,2048]{1,0:T(8,128)(2,1)S(1)}) custom-call(bf16[1024,2048]{1,0:T(8,128)(2,1)} %copy-done, bf16[8,2,256,2048]{3,2,1,0:T(8,128)(2,1)} %bitcast.120, bf16[8,2,256,2048]{3,2,1,0:T(8,128)(2,1)} %bitcast.121, ...), custom_call_target="tpu_custom_call", output_to_operand_aliasing={{0}: (3, {}), {1}: (4, {}), {2}: (5, {})} | custom-call | flops 1 | bytes 1 | tf_op jit(solution)/shard_map/pallas_call | solution.py:529
  327.8 10.0 %fusion.33 = f32[512,1280]{1,0:T(8,128)} fusion(bf16[1280,2048]{1,0:T(8,128)(2,1)} %get-tuple-element.535, bf16[1024,2048]{1,0:T(8,128)(2,1)S(1)} %get-tuple-element.281), kind=kOutput, calls=%fused_computation.101 | convolution fusion | flops 2684354560 | bytes 9961472 | tf_op jit(solution)/shard_map/dot_general | solution.py:45
  354.4 9.3 %collective-permute-done.37 = bf16[128,2048]{1,0:T(8,128)(2,1)S(1)} collective-permute-done((bf16[128,2048]{1,0:T(8,128)(2,1)S(1)}, bf16[128,2048]{1,0:T(8,128)(2,1)S(1)}, u32[]{:S(2)}, u32[]{:S(2)}) %collective-permute-start.37) | collective-permute-done | bytes 524320 | tf_op jit(solution)/shard_map/ppermute | solution.py:85
  402.8 12.7 %shard_map.296 = (bf16[1024,2048]{1,0:T(8,128)(2,1)}, bf16[1024,2048]{1,0:T(8,128)(2,1)}) custom-call(bf16[512,2048]{1,0:T(8,128)(2,1)S(1)} %shard_map.295.refs_0_, bf16[2048,2048]{1,0:T(8,128)(2,1)} %get-tuple-element.546.refs_1_, f32[1024,2048]{1,0:T(8,128)} %get-tuple-element.293.refs_2_, f32[1024,2048]{1,0:T(8,128)} %get-tuple-element.294.refs_3_), custom_call_target="tpu_custom_call" | custom-call | flops 1 | bytes 1 | tf_op jit(solution)/shard_map/pallas_call | solution.py:622
  415.5 9.5 %collective-permute-done.45.refs_2_ = bf16[256,2048]{1,0:T(8,128)(2,1)S(1)} collective-permute-done((bf16[256,2048]{1,0:T(8,128)(2,1)S(1)}, bf16[256,2048]{1,0:T(8,128)(2,1)S(1)}, u32[]{:S(2)}, u32[]{:S(2)}) %collective-permute-start.45) | collective-permute-done | bytes 1048608 | tf_op jit(solution)/shard_map/ppermute | solution.py:67
  433.0 9.6 %convolution_convert_fusion = bf16[2048,2048]{1,0:T(8,128)(2,1)S(1)} fusion(bf16[1024,2048]{1,0:T(8,128)(2,1)S(1)} %shard_map.297, bf16[1024,2048]{1,0:T(8,128)(2,1)S(1)} %copy-done.25), kind=kOutput, calls=%fused_computation | convolution fusion | flops 8594128896 | bytes 16777216 | tf_op jit(solution)/shard_map/dot_general | solution.py:41
  449.3 12.7 %shard_map.299 = (bf16[1024,2048]{1,0:T(8,128)(2,1)}, bf16[1024,2048]{1,0:T(8,128)(2,1)}) custom-call(bf16[512,2048]{1,0:T(8,128)(2,1)S(1)} %slice.273.refs_0_, bf16[2048,2048]{1,0:T(8,128)(2,1)} %get-tuple-element.546.refs_1_, f32[1024,2048]{1,0:T(8,128)} %get-tuple-element.293.refs_2_, ...), custom_call_target="tpu_custom_call", output_to_operand_aliasing={{0}: (4, {}), {1}: (5, {})} | custom-call | flops 1 | bytes 1 | tf_op jit(solution)/shard_map/pallas_call | solution.py:622
  462.0 14.4 %shard_map.300 = f32[512,2048]{1,0:T(8,128)S(1)} custom-call(bf16[1024,2048]{1,0:T(8,128)(2,1)} %get-tuple-element.392.grad_gate_ref.refs_1_.refs_2_, bf16[1024,2048]{1,0:T(8,128)(2,1)} %get-tuple-element.393.grad_up_ref.refs_2_.refs_3_, bf16[4096,2048]{1,0:T(8,128)(2,1)} %copy-done.46), custom_call_target="tpu_custom_call" | custom-call | flops 1 | bytes 1 | tf_op jit(solution)/shard_map/pallas_call | solution.py:495
  488.3 15.1 %shard_map.302 = f32[512,2048]{1,0:T(8,128)S(1)} custom-call(bf16[1024,2048]{1,0:T(8,128)(2,1)} %get-tuple-element.392.grad_gate_ref.refs_1_.refs_2_, bf16[1024,2048]{1,0:T(8,128)(2,1)} %get-tuple-element.393.grad_up_ref.refs_2_.refs_3_, bf16[4096,2048]{1,0:T(8,128)(2,1)} %copy-done.46), custom_call_target="tpu_custom_call" | custom-call | flops 1 | bytes 1 | tf_op jit(solution)/shard_map/pallas_call | solution.py:495
  534.5 7.5 shard_map.305
  549.1 17.8 %collective-permute-done.58.left_ref = bf16[256,2048]{1,0:T(8,128)(2,1)S(1)} collective-permute-done((bf16[256,2048]{1,0:T(8,128)(2,1)}, bf16[256,2048]{1,0:T(8,128)(2,1)S(1)}, u32[]{:S(2)}, u32[]{:S(2)}) %collective-permute-start.58) | collective-permute-done | bytes 1048608 | tf_op jit(solution)/shard_map/ppermute | solution.py:85
  585.3 7.3 shard_map.307
  600.9 8.1 shard_map.309
  696.6 8.9 %collective-permute-done.77 = bf16[256,2048]{1,0:T(8,128)(2,1)} collective-permute-done((bf16[256,2048]{1,0:T(8,128)(2,1)}, bf16[256,2048]{1,0:T(8,128)(2,1)}, u32[]{:S(2)}, u32[]{:S(2)}) %collective-permute-start.77) | collective-permute-done | bytes 1048608 | tf_op jit(solution)/shard_map/ppermute | solution.py:67
  728.9 13.7 %collective-permute-done.80 = f32[7,2048]{1,0:T(8,128)S(1)} collective-permute-done((f32[7,2048]{1,0:T(8,128)S(1)}, f32[7,2048]{1,0:T(8,128)S(1)}, u32[]{:S(2)}, u32[]{:S(2)}) %collective-permute-start.80) | collective-permute-done | bytes 57376 | tf_op jit(solution)/shard_map/ppermute | solution.py:260
  752.4 8.4 %collective-permute-done.81.left_ref = bf16[720,512]{1,0:T(8,128)(2,1)S(1)} collective-permute-done((bf16[720,512]{1,0:T(8,128)(2,1)S(1)}, bf16[720,512]{1,0:T(8,128)(2,1)S(1)}, u32[]{:S(2)}, u32[]{:S(2)}) %collective-permute-start.81) | collective-permute-done | bytes 737312 | tf_op jit(solution)/shard_map/ppermute | solution.py:85
  770.9 13.5 %collective-permute-done.86 = f32[7,2048]{1,0:T(8,128)S(1)} collective-permute-done((f32[7,2048]{1,0:T(8,128)S(1)}, f32[7,2048]{1,0:T(8,128)S(1)}, u32[]{:S(2)}, u32[]{:S(2)}) %collective-permute-start.86) | collective-permute-done | bytes 57376 | tf_op jit(solution)/shard_map/ppermute | solution.py:260
  (664 shorter events, 498.5 us)
Async XLA Ops:
  2.5 30.6 %collective-permute-start.4 = (bf16[256,2048]{1,0:T(8,128)(2,1)}, bf16[256,2048]{1,0:T(8,128)(2,1)S(1)}, u32[]{:S(2)}, u32[]{:S(2)}) collective-permute-start(bf16[256,2048]{1,0:T(8,128)(2,1)} %param.17), channel_id=1, source_target_pairs={{0,1},{1,0},{2,3},{3,2},{4,5},{5,4},{6,7},{7,6},{8,9},{9,8},{10,11... | collective-permute-start | bytes 3145736 | tf_op jit(solution)/shard_map/ppermute | solution.py:63
  15.6 46.0 %collective-permute-start.9 = (bf16[256,2048]{1,0:T(8,128)(2,1)}, bf16[256,2048]{1,0:T(8,128)(2,1)}, u32[]{:S(2)}, u32[]{:S(2)}) collective-permute-start(bf16[256,2048]{1,0:T(8,128)(2,1)} %param.17), channel_id=1, source_target_pairs={{0,2},{2,0},{1,3},{3,1},{4,6},{6,4},{5,7},{7,5},{8,10},{10,8},{9,1... | collective-permute-start | bytes 3145736 | tf_op jit(solution)/shard_map/ppermute | solution.py:67
  93.3 47.0 %collective-permute-start.13 = (bf16[512,2048]{1,0:T(8,128)(2,1)S(1)}, bf16[512,2048]{1,0:T(8,128)(2,1)}, u32[]{:S(2)}, u32[]{:S(2)}) collective-permute-start(bf16[512,2048]{1,0:T(8,128)(2,1)S(1)} %shard_map.288), channel_id=1, source_target_pairs={{0,8},{8,16},{16,24},{24,28},{28,20},{20,12},{12,4},{4,0},{1,9},{9... | collective-permute-start | bytes 6291464 | tf_op jit(solution)/shard_map/ppermute | solution.py:85
  94.9 46.8 %collective-permute-start.14 = (bf16[512,2048]{1,0:T(8,128)(2,1)S(1)}, bf16[512,2048]{1,0:T(8,128)(2,1)}, u32[]{:S(2)}, u32[]{:S(2)}) collective-permute-start(bf16[512,2048]{1,0:T(8,128)(2,1)S(1)} %shard_map.288), channel_id=1, source_target_pairs={{8,0},{16,8},{24,16},{28,24},{20,28},{12,20},{4,12},{0,4},{9,1},{1... | collective-permute-start | bytes 6291464 | tf_op jit(solution)/shard_map/ppermute | solution.py:88
  147.9 47.9 %collective-permute-start.18 = (bf16[512,2048]{1,0:T(8,128)(2,1)}, bf16[512,2048]{1,0:T(8,128)(2,1)}, u32[]{:S(2)}, u32[]{:S(2)}) collective-permute-start(bf16[512,2048]{1,0:T(8,128)(2,1)} %collective-permute-done.13), channel_id=1, source_target_pairs={{0,8},{8,16},{16,24},{24,28},{28,20},{20,12},{12,4},{4,0},{1,9},{9... | collective-permute-start | bytes 6291464 | tf_op jit(solution)/shard_map/ppermute | solution.py:85
  148.6 47.7 %collective-permute-start.19 = (bf16[512,2048]{1,0:T(8,128)(2,1)}, bf16[512,2048]{1,0:T(8,128)(2,1)}, u32[]{:S(2)}, u32[]{:S(2)}) collective-permute-start(bf16[512,2048]{1,0:T(8,128)(2,1)} %collective-permute-done.14), channel_id=1, source_target_pairs={{8,0},{16,8},{24,16},{28,24},{20,28},{12,20},{4,12},{0,4},{9,1},{1... | collective-permute-start | bytes 6291464 | tf_op jit(solution)/shard_map/ppermute | solution.py:88
  196.3 48.4 %collective-permute-start.25 = (bf16[512,2048]{1,0:T(8,128)(2,1)}, bf16[512,2048]{1,0:T(8,128)(2,1)}, u32[]{:S(2)}, u32[]{:S(2)}) collective-permute-start(bf16[512,2048]{1,0:T(8,128)(2,1)} %collective-permute-done.18), channel_id=1, source_target_pairs={{0,8},{8,16},{16,24},{24,28},{28,20},{20,12},{12,4},{4,0},{1,9},{9... | collective-permute-start | bytes 6291464 | tf_op jit(solution)/shard_map/ppermute | solution.py:85
  196.8 48.1 %collective-permute-start.26 = (bf16[512,2048]{1,0:T(8,128)(2,1)}, bf16[512,2048]{1,0:T(8,128)(2,1)}, u32[]{:S(2)}, u32[]{:S(2)}) collective-permute-start(bf16[512,2048]{1,0:T(8,128)(2,1)} %collective-permute-done.19), channel_id=1, source_target_pairs={{8,0},{16,8},{24,16},{28,24},{20,28},{12,20},{4,12},{0,4},{9,1},{1... | collective-permute-start | bytes 6291464 | tf_op jit(solution)/shard_map/ppermute | solution.py:88
  253.5 42.7 %collective-permute-start.28 = (bf16[256,2048]{1,0:T(8,128)(2,1)S(1)}, bf16[256,2048]{1,0:T(8,128)(2,1)}, u32[]{:S(2)}, u32[]{:S(2)}) collective-permute-start(bf16[256,2048]{1,0:T(8,128)(2,1)S(1)} %bitcast.138), channel_id=1, source_target_pairs={{0,8},{8,16},{16,24},{24,28},{28,20},{20,12},{12,4},{4,0},{1,9},{9... | collective-permute-start | bytes 3145736 | tf_op jit(solution)/shard_map/ppermute | solution.py:85
  254.0 42.3 %collective-permute-start.29 = (bf16[256,2048]{1,0:T(8,128)(2,1)S(1)}, bf16[256,2048]{1,0:T(8,128)(2,1)}, u32[]{:S(2)}, u32[]{:S(2)}) collective-permute-start(bf16[256,2048]{1,0:T(8,128)(2,1)S(1)} %bitcast.139), channel_id=1, source_target_pairs={{8,0},{16,8},{24,16},{28,24},{20,28},{12,20},{4,12},{0,4},{9,1},{1... | collective-permute-start | bytes 3145736 | tf_op jit(solution)/shard_map/ppermute | solution.py:88
  447.0 31.2 %collective-permute-start.50 = (bf16[256,2048]{1,0:T(8,128)(2,1)S(1)}, bf16[256,2048]{1,0:T(8,128)(2,1)S(1)}, u32[]{:S(2)}, u32[]{:S(2)}) collective-permute-start(bf16[256,2048]{1,0:T(8,128)(2,1)S(1)} %get-tuple-element.305), channel_id=1, source_target_pairs={{0,8},{8,16},{16,24},{24,28},{28,20},{20,12},{12,4},{4,0},{1,9},{9... | collective-permute-start | bytes 3145736 | tf_op jit(solution)/shard_map/ppermute | solution.py:85
  522.3 44.6 %collective-permute-start.58 = (bf16[256,2048]{1,0:T(8,128)(2,1)}, bf16[256,2048]{1,0:T(8,128)(2,1)S(1)}, u32[]{:S(2)}, u32[]{:S(2)}) collective-permute-start(bf16[256,2048]{1,0:T(8,128)(2,1)} %get-tuple-element.523), channel_id=1, source_target_pairs={{0,8},{8,16},{16,24},{24,28},{28,20},{20,12},{12,4},{4,0},{1,9},{9... | collective-permute-start | bytes 3145736 | tf_op jit(solution)/shard_map/ppermute | solution.py:85
  523.8 44.3 %collective-permute-start.59 = (bf16[256,2048]{1,0:T(8,128)(2,1)}, bf16[256,2048]{1,0:T(8,128)(2,1)S(1)}, u32[]{:S(2)}, u32[]{:S(2)}) collective-permute-start(bf16[256,2048]{1,0:T(8,128)(2,1)} %get-tuple-element.522), channel_id=1, source_target_pairs={{8,0},{16,8},{24,16},{28,24},{20,28},{12,20},{4,12},{0,4},{9,1},{1... | collective-permute-start | bytes 3145736 | tf_op jit(solution)/shard_map/ppermute | solution.py:88
  533.3 34.7 %collective-permute-start.61 = (bf16[256,2048]{1,0:T(8,128)(2,1)S(1)}, bf16[256,2048]{1,0:T(8,128)(2,1)S(1)}, u32[]{:S(2)}, u32[]{:S(2)}) collective-permute-start(bf16[256,2048]{1,0:T(8,128)(2,1)S(1)} %fusion.24.refs_0_), channel_id=1, source_target_pairs={{0,2},{2,0},{1,3},{3,1},{4,6},{6,4},{5,7},{7,5},{8,10},{10,8},{9,1... | collective-permute-start | bytes 3145736 | tf_op jit(solution)/shard_map/ppermute | solution.py:67
  571.8 48.3 %collective-permute-start.63 = (bf16[512,2048]{1,0:T(8,128)(2,1)}, bf16[512,2048]{1,0:T(8,128)(2,1)}, u32[]{:S(2)}, u32[]{:S(2)}) collective-permute-start(bf16[512,2048]{1,0:T(8,128)(2,1)} %get-tuple-element.352), channel_id=1, source_target_pairs={{0,8},{8,16},{16,24},{24,28},{28,20},{20,12},{12,4},{4,0},{1,9},{9... | collective-permute-start | bytes 6291464 | tf_op jit(solution)/shard_map/ppermute | solution.py:85
  573.4 48.1 %collective-permute-start.64 = (bf16[512,2048]{1,0:T(8,128)(2,1)}, bf16[512,2048]{1,0:T(8,128)(2,1)}, u32[]{:S(2)}, u32[]{:S(2)}) collective-permute-start(bf16[512,2048]{1,0:T(8,128)(2,1)} %get-tuple-element.353), channel_id=1, source_target_pairs={{8,0},{16,8},{24,16},{28,24},{20,28},{12,20},{4,12},{0,4},{9,1},{1... | collective-permute-start | bytes 6291464 | tf_op jit(solution)/shard_map/ppermute | solution.py:88
  580.9 30.5 %collective-permute-start.66 = (bf16[8,2,64,640]{3,2,1,0:T(8,128)(2,1)}, bf16[8,2,64,640]{3,2,1,0:T(8,128)(2,1)}, u32[]{:S(2)}, u32[]{:S(2)}) collective-permute-start(bf16[8,2,64,640]{3,2,1,0:T(8,128)(2,1)} %dynamic-slice_bitcast_fusion), channel_id=1, source_target_pairs={{0,1},{1,0},{2,3},{3,2},{4,5},{5,4},{6,7},{7,6},{8,9},{9,8},{10,11... | collective-permute-start | bytes 3932168 | tf_op jit(solution)/shard_map/ppermute | solution.py:63
  622.7 34.7 %collective-permute-start.71 = (bf16[8,64,640]{2,1,0:T(8,128)(2,1)S(1)}, bf16[8,64,640]{2,1,0:T(8,128)(2,1)S(1)}, u32[]{:S(2)}, u32[]{:S(2)}) collective-permute-start(bf16[8,64,640]{2,1,0:T(8,128)(2,1)S(1)} %dynamic-slice_bitcast_fusion.2), channel_id=1, source_target_pairs={{0,2},{2,0},{1,3},{3,1},{4,6},{6,4},{5,7},{7,5},{8,10},{10,8},{9,1... | collective-permute-start | bytes 1966088 | tf_op jit(solution)/shard_map/ppermute | solution.py:67
  629.4 48.1 %collective-permute-start.67 = (bf16[512,2048]{1,0:T(8,128)(2,1)}, bf16[512,2048]{1,0:T(8,128)(2,1)}, u32[]{:S(2)}, u32[]{:S(2)}) collective-permute-start(bf16[512,2048]{1,0:T(8,128)(2,1)} %get-tuple-element.370), channel_id=1, source_target_pairs={{0,8},{8,16},{16,24},{24,28},{28,20},{20,12},{12,4},{4,0},{1,9},{9... | collective-permute-start | bytes 6291464 | tf_op jit(solution)/shard_map/ppermute | solution.py:85
  630.7 47.8 %collective-permute-start.68 = (bf16[512,2048]{1,0:T(8,128)(2,1)}, bf16[512,2048]{1,0:T(8,128)(2,1)}, u32[]{:S(2)}, u32[]{:S(2)}) collective-permute-start(bf16[512,2048]{1,0:T(8,128)(2,1)} %get-tuple-element.371), channel_id=1, source_target_pairs={{8,0},{16,8},{24,16},{28,24},{20,28},{12,20},{4,12},{0,4},{9,1},{1... | collective-permute-start | bytes 6291464 | tf_op jit(solution)/shard_map/ppermute | solution.py:88
  685.5 57.1 %collective-permute-start.72 = (bf16[512,2048]{1,0:T(8,128)(2,1)}, bf16[512,2048]{1,0:T(8,128)(2,1)}, u32[]{:S(2)}, u32[]{:S(2)}) collective-permute-start(bf16[512,2048]{1,0:T(8,128)(2,1)} %get-tuple-element.388), channel_id=1, source_target_pairs={{0,8},{8,16},{16,24},{24,28},{28,20},{20,12},{12,4},{4,0},{1,9},{9... | collective-permute-start | bytes 6291464 | tf_op jit(solution)/shard_map/ppermute | solution.py:85
  686.7 56.0 %collective-permute-start.73 = (bf16[512,2048]{1,0:T(8,128)(2,1)S(1)}, bf16[512,2048]{1,0:T(8,128)(2,1)}, u32[]{:S(2)}, u32[]{:S(2)}) collective-permute-start(bf16[512,2048]{1,0:T(8,128)(2,1)S(1)} %get-tuple-element.389), channel_id=1, source_target_pairs={{8,0},{16,8},{24,16},{28,24},{20,28},{12,20},{4,12},{0,4},{9,1},{1... | collective-permute-start | bytes 6291464 | tf_op jit(solution)/shard_map/ppermute | solution.py:88
  692.7 49.9 %collective-permute-start.75 = (bf16[368,512]{1,0:T(8,128)(2,1)S(1)}, bf16[368,512]{1,0:T(8,128)(2,1)S(1)}, u32[]{:S(2)}, u32[]{:S(2)}) collective-permute-start(bf16[368,512]{1,0:T(8,128)(2,1)S(1)} %constant_dynamic-slice_fusion.9), channel_id=1, source_target_pairs={{8,0},{16,8},{24,16},{28,24},{20,28},{12,20},{4,12},{0,4},{9,1},{1... | collective-permute-start | bytes 1130504 | tf_op jit(solution)/shard_map/ppermute | solution.py:88
  695.2 47.4 %collective-permute-start.74 = (bf16[352,512]{1,0:T(8,128)(2,1)}, bf16[352,512]{1,0:T(8,128)(2,1)S(1)}, u32[]{:S(2)}, u32[]{:S(2)}) collective-permute-start(bf16[352,512]{1,0:T(8,128)(2,1)} %constant_dynamic-slice_fusion), channel_id=1, source_target_pairs={{0,8},{8,16},{16,24},{24,28},{28,20},{20,12},{12,4},{4,0},{1,9},{9... | collective-permute-start | bytes 1081352 | tf_op jit(solution)/shard_map/ppermute | solution.py:85
  (194 other events, 2223.3 us)

commit v5 on v4

--- a/solution.py
+++ b/solution.py
@@ -878,15 +878,11 @@
     grad_ff_all = phase([down_back], grad_ff_all)
     grads_low = feed_forward_back(grad_ff_all[half:], down_t, gate_pre, up_pre, 1, grads_low)
     ff_in_far, *grads_low = phase([down_back], grad_in(*grads_low, pair, 1), *grads_low)
+    ff_in_far, ff_in_near, *grads_low = phase(
+        [down_back], cross(ff_in_far), grad_in(*grads_low, pair, 0), *grads_low
+    )
     both_back = Reduce(
         ring, pair_share, (ff_in_all, *grads_low), lambda: pair_grad(ff_in_all, *grads_low)
-    )
-    ff_in_far, ff_in_near, both_back.far, both_back.source = phase(
-        [down_back],
-        cross(ff_in_far),
-        grad_in(*grads_low, pair, 0),
-        both_back.far,
-        both_back.source,
     )
     grad_ff_in = add_core(ff_in_near) + ff_in_far
     grad_mixed_norm, grad_gain_three = norm_back(mixed, gains[3], grad_ff_in)

time: 818 us -> 819 us (level)
    unnamed x272 -> x274, local copies, waits for them, and re-layouts: 60.7 us -> 60 us
  transfers between devices with their start and end apart: 90 -> 90, of which waited for: 53 -> 53; matrix products, arithmetic and copies ran while one was open for 28% -> 29% of each run, Pallas kernels for 19% -> 19%
where the time goes in v5:
time: 819 us; the launch traced here: 810 us
  waiting for transfers between devices  274 us (33%)
  local copies, waits for them, and re-layouts  162 us (20%)
  Pallas kernels  158 us (19%)
  other arithmetic  72.6 us (9%)
  starting transfers between devices  71.1 us (9%)
  matrix products  69.7 us (9%)
    ppermute x24, waiting for transfers between devices, up(): return lax.ppermute(value, 'dp', self.ahead)  139 us
    ppermute x15, waiting for transfers between devices, chip_swap(): return lax.ppermute(value, 'mp', [(0, 2), (2, 0), (1, 3), (3, 1)])  76.9 us
    unnamed x274, local copies, waits for them, and re-layouts  60 us
    pallas_call x11, Pallas kernels, tiled_call(): pl.pallas_call(kernel, out_shape=outs, grid=(steps,), in_specs=specs, out...  50.5 us
    dynamic_update_slice x27, local copies, waits for them, and re-layouts, put(): return lax.dynamic_update_slice(whole, piece, (start, 0))  39.2 us
    dot_general x12, matrix products, product_right(): lax.dot_general(left, right, (((1,), (1,)), ((), ())), preferred_element_...  33.9 us
    pallas_call x5, Pallas kernels, pair_share(): pl.pallas_call(pair_share_kernel, out_shape=[jax.ShapeDtypeStruct((2 * si...  31.2 us
    ppermute x24, starting transfers between devices, up(): return lax.ppermute(value, 'dp', self.ahead)  29.5 us
  transfers between devices with their start and end apart: 90, of which 53 were waited for; matrix products, arithmetic and copies ran while one was open for 29% of the time, Pallas kernels for 19%

profile of v5, /device:TPU:0, one launch (start us, length us, event | category | flops | bytes accessed | tf_op | source)
XLA Modules:
  0.0 809.7 jit_solution(7108916260756990577)
XLA Ops:
  17.6 14.0 %collective-permute-done.2 = bf16[736,512]{1,0:T(8,128)(2,1)} collective-permute-done((bf16[736,512]{1,0:T(8,128)(2,1)S(1)}, bf16[736,512]{1,0:T(8,128)(2,1)}, u32[]{:S(2)}, u32[]{:S(2)}) %collective-permute-start.2) | collective-permute-done | bytes 753696 | tf_op jit(solution)/shard_map/ppermute | solution.py:85
  152.9 19.0 %collective-permute-done.22 = bf16[256,2048]{1,0:T(8,128)(2,1)S(1)} collective-permute-done((bf16[256,2048]{1,0:T(8,128)(2,1)S(1)}, bf16[256,2048]{1,0:T(8,128)(2,1)S(1)}, u32[]{:S(2)}, u32[]{:S(2)}) %collective-permute-start.22) | collective-permute-done | bytes 1048608 | tf_op jit(solution)/shard_map/ppermute | solution.py:67
  177.4 18.5 %collective-permute-done.18 = bf16[512,2048]{1,0:T(8,128)(2,1)} collective-permute-done((bf16[512,2048]{1,0:T(8,128)(2,1)}, bf16[512,2048]{1,0:T(8,128)(2,1)}, u32[]{:S(2)}, u32[]{:S(2)}) %collective-permute-start.18) | collective-permute-done | bytes 2097184 | tf_op jit(solution)/shard_map/ppermute | solution.py:85
  206.5 18.7 %collective-permute-done.27.refs_2_ = bf16[256,2048]{1,0:T(8,128)(2,1)} collective-permute-done((bf16[256,2048]{1,0:T(8,128)(2,1)S(1)}, bf16[256,2048]{1,0:T(8,128)(2,1)}, u32[]{:S(2)}, u32[]{:S(2)}) %collective-permute-start.27) | collective-permute-done | bytes 1048608 | tf_op jit(solution)/shard_map/ppermute | solution.py:67
  225.2 19.4 %collective-permute-done.25 = bf16[512,2048]{1,0:T(8,128)(2,1)} collective-permute-done((bf16[512,2048]{1,0:T(8,128)(2,1)}, bf16[512,2048]{1,0:T(8,128)(2,1)}, u32[]{:S(2)}, u32[]{:S(2)}) %collective-permute-start.25) | collective-permute-done | bytes 2097184 | tf_op jit(solution)/shard_map/ppermute | solution.py:85
  261.2 11.0 %collective-permute-done.30 = bf16[256,2048]{1,0:T(8,128)(2,1)S(1)} collective-permute-done((bf16[256,2048]{1,0:T(8,128)(2,1)S(1)}, bf16[256,2048]{1,0:T(8,128)(2,1)S(1)}, u32[]{:S(2)}, u32[]{:S(2)}) %collective-permute-start.30) | collective-permute-done | bytes 1048608 | tf_op jit(solution)/shard_map/ppermute | solution.py:85
  280.0 14.3 %shard_map.292 = (f32[1024,2048]{1,0:T(8,128)}, f32[1024,2048]{1,0:T(8,128)}, bf16[1024,2048]{1,0:T(8,128)(2,1)S(1)}) custom-call(bf16[1024,2048]{1,0:T(8,128)(2,1)} %copy-done, bf16[8,2,256,2048]{3,2,1,0:T(8,128)(2,1)} %bitcast.118, bf16[8,2,256,2048]{3,2,1,0:T(8,128)(2,1)} %bitcast.119), custom_call_target="tpu_custom_call" | custom-call | flops 1 | bytes 1 | tf_op jit(solution)/shard_map/pallas_call | solution.py:529
  300.6 14.3 %shard_map.293 = (f32[1024,2048]{1,0:T(8,128)}, f32[1024,2048]{1,0:T(8,128)}, bf16[1024,2048]{1,0:T(8,128)(2,1)S(1)}) custom-call(bf16[1024,2048]{1,0:T(8,128)(2,1)} %copy-done, bf16[8,2,256,2048]{3,2,1,0:T(8,128)(2,1)} %bitcast.120, bf16[8,2,256,2048]{3,2,1,0:T(8,128)(2,1)} %bitcast.121, ...), custom_call_target="tpu_custom_call", output_to_operand_aliasing={{0}: (3, {}), {1}: (4, {}), {2}: (5, {})} | custom-call | flops 1 | bytes 1 | tf_op jit(solution)/shard_map/pallas_call | solution.py:529
  327.8 10.0 %fusion.33 = f32[512,1280]{1,0:T(8,128)} fusion(bf16[1280,2048]{1,0:T(8,128)(2,1)} %get-tuple-element.531, bf16[1024,2048]{1,0:T(8,128)(2,1)S(1)} %get-tuple-element.279), kind=kOutput, calls=%fused_computation.101 | convolution fusion | flops 2684354560 | bytes 9961472 | tf_op jit(solution)/shard_map/dot_general | solution.py:45
  354.3 9.3 %collective-permute-done.37 = bf16[128,2048]{1,0:T(8,128)(2,1)S(1)} collective-permute-done((bf16[128,2048]{1,0:T(8,128)(2,1)S(1)}, bf16[128,2048]{1,0:T(8,128)(2,1)S(1)}, u32[]{:S(2)}, u32[]{:S(2)}) %collective-permute-start.37) | collective-permute-done | bytes 524320 | tf_op jit(solution)/shard_map/ppermute | solution.py:85
  402.7 12.7 %shard_map.296 = (bf16[1024,2048]{1,0:T(8,128)(2,1)}, bf16[1024,2048]{1,0:T(8,128)(2,1)}) custom-call(bf16[512,2048]{1,0:T(8,128)(2,1)S(1)} %shard_map.295.refs_0_, bf16[2048,2048]{1,0:T(8,128)(2,1)} %get-tuple-element.542.refs_1_, f32[1024,2048]{1,0:T(8,128)} %get-tuple-element.291.refs_2_, f32[1024,2048]{1,0:T(8,128)} %get-tuple-element.292.refs_3_), custom_call_target="tpu_custom_call" | custom-call | flops 1 | bytes 1 | tf_op jit(solution)/shard_map/pallas_call | solution.py:622
  415.4 9.5 %collective-permute-done.45.refs_2_ = bf16[256,2048]{1,0:T(8,128)(2,1)S(1)} collective-permute-done((bf16[256,2048]{1,0:T(8,128)(2,1)S(1)}, bf16[256,2048]{1,0:T(8,128)(2,1)S(1)}, u32[]{:S(2)}, u32[]{:S(2)}) %collective-permute-start.45) | collective-permute-done | bytes 1048608 | tf_op jit(solution)/shard_map/ppermute | solution.py:67
  433.0 9.6 %convolution_convert_fusion = bf16[2048,2048]{1,0:T(8,128)(2,1)S(1)} fusion(bf16[1024,2048]{1,0:T(8,128)(2,1)S(1)} %shard_map.297, bf16[1024,2048]{1,0:T(8,128)(2,1)S(1)} %copy-done.25), kind=kOutput, calls=%fused_computation | convolution fusion | flops 8594128896 | bytes 16777216 | tf_op jit(solution)/shard_map/dot_general | solution.py:41
  449.2 12.7 %shard_map.299 = (bf16[1024,2048]{1,0:T(8,128)(2,1)}, bf16[1024,2048]{1,0:T(8,128)(2,1)}) custom-call(bf16[512,2048]{1,0:T(8,128)(2,1)S(1)} %slice.273.refs_0_, bf16[2048,2048]{1,0:T(8,128)(2,1)} %get-tuple-element.542.refs_1_, f32[1024,2048]{1,0:T(8,128)} %get-tuple-element.291.refs_2_, ...), custom_call_target="tpu_custom_call", output_to_operand_aliasing={{0}: (4, {}), {1}: (5, {})} | custom-call | flops 1 | bytes 1 | tf_op jit(solution)/shard_map/pallas_call | solution.py:622
  462.0 14.4 %shard_map.300 = f32[512,2048]{1,0:T(8,128)S(1)} custom-call(bf16[1024,2048]{1,0:T(8,128)(2,1)} %get-tuple-element.388.grad_gate_ref.refs_1_.refs_2_, bf16[1024,2048]{1,0:T(8,128)(2,1)} %get-tuple-element.389.grad_up_ref.refs_2_.refs_3_, bf16[4096,2048]{1,0:T(8,128)(2,1)} %copy-done.48), custom_call_target="tpu_custom_call" | custom-call | flops 1 | bytes 1 | tf_op jit(solution)/shard_map/pallas_call | solution.py:495
  488.3 14.8 %shard_map.302 = f32[512,2048]{1,0:T(8,128)S(1)} custom-call(bf16[1024,2048]{1,0:T(8,128)(2,1)} %get-tuple-element.388.grad_gate_ref.refs_1_.refs_2_, bf16[1024,2048]{1,0:T(8,128)(2,1)} %get-tuple-element.389.grad_up_ref.refs_2_.refs_3_, bf16[4096,2048]{1,0:T(8,128)(2,1)} %copy-done.48), custom_call_target="tpu_custom_call" | custom-call | flops 1 | bytes 1 | tf_op jit(solution)/shard_map/pallas_call | solution.py:495
  537.5 7.5 shard_map.305
  552.2 15.4 %collective-permute-done.56 = bf16[256,2048]{1,0:T(8,128)(2,1)} collective-permute-done((bf16[256,2048]{1,0:T(8,128)(2,1)S(1)}, bf16[256,2048]{1,0:T(8,128)(2,1)}, u32[]{:S(2)}, u32[]{:S(2)}) %collective-permute-start.56) | collective-permute-done | bytes 1048608 | tf_op jit(solution)/shard_map/ppermute | solution.py:85
  601.5 8.1 shard_map.309
  647.8 7.3 shard_map.311
  697.3 8.8 %collective-permute-done.77 = bf16[256,2048]{1,0:T(8,128)(2,1)} collective-permute-done((bf16[256,2048]{1,0:T(8,128)(2,1)}, bf16[256,2048]{1,0:T(8,128)(2,1)}, u32[]{:S(2)}, u32[]{:S(2)}) %collective-permute-start.77) | collective-permute-done | bytes 1048608 | tf_op jit(solution)/shard_map/ppermute | solution.py:67
  729.4 14.0 %collective-permute-done.80 = f32[7,2048]{1,0:T(8,128)S(1)} collective-permute-done((f32[7,2048]{1,0:T(8,128)S(1)}, f32[7,2048]{1,0:T(8,128)S(1)}, u32[]{:S(2)}, u32[]{:S(2)}) %collective-permute-start.80) | collective-permute-done | bytes 57376 | tf_op jit(solution)/shard_map/ppermute | solution.py:260
  753.3 8.3 %collective-permute-done.81.left_ref = bf16[720,512]{1,0:T(8,128)(2,1)S(1)} collective-permute-done((bf16[720,512]{1,0:T(8,128)(2,1)S(1)}, bf16[720,512]{1,0:T(8,128)(2,1)S(1)}, u32[]{:S(2)}, u32[]{:S(2)}) %collective-permute-start.81) | collective-permute-done | bytes 737312 | tf_op jit(solution)/shard_map/ppermute | solution.py:85
  771.8 13.4 %collective-permute-done.86 = f32[7,2048]{1,0:T(8,128)S(1)} collective-permute-done((f32[7,2048]{1,0:T(8,128)S(1)}, f32[7,2048]{1,0:T(8,128)S(1)}, u32[]{:S(2)}, u32[]{:S(2)}) %collective-permute-start.86) | collective-permute-done | bytes 57376 | tf_op jit(solution)/shard_map/ppermute | solution.py:260
  (666 shorter events, 501.7 us)
Async XLA Ops:
  2.5 30.6 %collective-permute-start.4 = (bf16[256,2048]{1,0:T(8,128)(2,1)}, bf16[256,2048]{1,0:T(8,128)(2,1)S(1)}, u32[]{:S(2)}, u32[]{:S(2)}) collective-permute-start(bf16[256,2048]{1,0:T(8,128)(2,1)} %param.17), channel_id=1, source_target_pairs={{0,1},{1,0},{2,3},{3,2},{4,5},{5,4},{6,7},{7,6},{8,9},{9,8},{10,11... | collective-permute-start | bytes 3145736 | tf_op jit(solution)/shard_map/ppermute | solution.py:63
  15.6 46.0 %collective-permute-start.9 = (bf16[256,2048]{1,0:T(8,128)(2,1)}, bf16[256,2048]{1,0:T(8,128)(2,1)}, u32[]{:S(2)}, u32[]{:S(2)}) collective-permute-start(bf16[256,2048]{1,0:T(8,128)(2,1)} %param.17), channel_id=1, source_target_pairs={{0,2},{2,0},{1,3},{3,1},{4,6},{6,4},{5,7},{7,5},{8,10},{10,8},{9,1... | collective-permute-start | bytes 3145736 | tf_op jit(solution)/shard_map/ppermute | solution.py:67
  93.3 47.0 %collective-permute-start.13 = (bf16[512,2048]{1,0:T(8,128)(2,1)S(1)}, bf16[512,2048]{1,0:T(8,128)(2,1)}, u32[]{:S(2)}, u32[]{:S(2)}) collective-permute-start(bf16[512,2048]{1,0:T(8,128)(2,1)S(1)} %shard_map.288), channel_id=1, source_target_pairs={{0,8},{8,16},{16,24},{24,28},{28,20},{20,12},{12,4},{4,0},{1,9},{9... | collective-permute-start | bytes 6291464 | tf_op jit(solution)/shard_map/ppermute | solution.py:85
  94.9 46.8 %collective-permute-start.14 = (bf16[512,2048]{1,0:T(8,128)(2,1)S(1)}, bf16[512,2048]{1,0:T(8,128)(2,1)}, u32[]{:S(2)}, u32[]{:S(2)}) collective-permute-start(bf16[512,2048]{1,0:T(8,128)(2,1)S(1)} %shard_map.288), channel_id=1, source_target_pairs={{8,0},{16,8},{24,16},{28,24},{20,28},{12,20},{4,12},{0,4},{9,1},{1... | collective-permute-start | bytes 6291464 | tf_op jit(solution)/shard_map/ppermute | solution.py:88
  148.0 47.9 %collective-permute-start.18 = (bf16[512,2048]{1,0:T(8,128)(2,1)}, bf16[512,2048]{1,0:T(8,128)(2,1)}, u32[]{:S(2)}, u32[]{:S(2)}) collective-permute-start(bf16[512,2048]{1,0:T(8,128)(2,1)} %collective-permute-done.13), channel_id=1, source_target_pairs={{0,8},{8,16},{16,24},{24,28},{28,20},{20,12},{12,4},{4,0},{1,9},{9... | collective-permute-start | bytes 6291464 | tf_op jit(solution)/shard_map/ppermute | solution.py:85
  148.6 47.6 %collective-permute-start.19 = (bf16[512,2048]{1,0:T(8,128)(2,1)}, bf16[512,2048]{1,0:T(8,128)(2,1)}, u32[]{:S(2)}, u32[]{:S(2)}) collective-permute-start(bf16[512,2048]{1,0:T(8,128)(2,1)} %collective-permute-done.14), channel_id=1, source_target_pairs={{8,0},{16,8},{24,16},{28,24},{20,28},{12,20},{4,12},{0,4},{9,1},{1... | collective-permute-start | bytes 6291464 | tf_op jit(solution)/shard_map/ppermute | solution.py:88
  196.3 48.4 %collective-permute-start.25 = (bf16[512,2048]{1,0:T(8,128)(2,1)}, bf16[512,2048]{1,0:T(8,128)(2,1)}, u32[]{:S(2)}, u32[]{:S(2)}) collective-permute-start(bf16[512,2048]{1,0:T(8,128)(2,1)} %collective-permute-done.18), channel_id=1, source_target_pairs={{0,8},{8,16},{16,24},{24,28},{28,20},{20,12},{12,4},{4,0},{1,9},{9... | collective-permute-start | bytes 6291464 | tf_op jit(solution)/shard_map/ppermute | solution.py:85
  196.8 48.1 %collective-permute-start.26 = (bf16[512,2048]{1,0:T(8,128)(2,1)}, bf16[512,2048]{1,0:T(8,128)(2,1)}, u32[]{:S(2)}, u32[]{:S(2)}) collective-permute-start(bf16[512,2048]{1,0:T(8,128)(2,1)} %collective-permute-done.19), channel_id=1, source_target_pairs={{8,0},{16,8},{24,16},{28,24},{20,28},{12,20},{4,12},{0,4},{9,1},{1... | collective-permute-start | bytes 6291464 | tf_op jit(solution)/shard_map/ppermute | solution.py:88
  253.5 42.7 %collective-permute-start.28 = (bf16[256,2048]{1,0:T(8,128)(2,1)S(1)}, bf16[256,2048]{1,0:T(8,128)(2,1)}, u32[]{:S(2)}, u32[]{:S(2)}) collective-permute-start(bf16[256,2048]{1,0:T(8,128)(2,1)S(1)} %bitcast.138), channel_id=1, source_target_pairs={{0,8},{8,16},{16,24},{24,28},{28,20},{20,12},{12,4},{4,0},{1,9},{9... | collective-permute-start | bytes 3145736 | tf_op jit(solution)/shard_map/ppermute | solution.py:85
  253.9 42.3 %collective-permute-start.29 = (bf16[256,2048]{1,0:T(8,128)(2,1)S(1)}, bf16[256,2048]{1,0:T(8,128)(2,1)}, u32[]{:S(2)}, u32[]{:S(2)}) collective-permute-start(bf16[256,2048]{1,0:T(8,128)(2,1)S(1)} %bitcast.139), channel_id=1, source_target_pairs={{8,0},{16,8},{24,16},{28,24},{20,28},{12,20},{4,12},{0,4},{9,1},{1... | collective-permute-start | bytes 3145736 | tf_op jit(solution)/shard_map/ppermute | solution.py:88
  446.9 31.3 %collective-permute-start.50 = (bf16[256,2048]{1,0:T(8,128)(2,1)S(1)}, bf16[256,2048]{1,0:T(8,128)(2,1)S(1)}, u32[]{:S(2)}, u32[]{:S(2)}) collective-permute-start(bf16[256,2048]{1,0:T(8,128)(2,1)S(1)} %get-tuple-element.303), channel_id=1, source_target_pairs={{0,8},{8,16},{16,24},{24,28},{28,20},{20,12},{12,4},{4,0},{1,9},{9... | collective-permute-start | bytes 3145736 | tf_op jit(solution)/shard_map/ppermute | solution.py:85
  521.2 31.0 %collective-permute-start.59 = (bf16[256,2048]{1,0:T(8,128)(2,1)}, bf16[256,2048]{1,0:T(8,128)(2,1)S(1)}, u32[]{:S(2)}, u32[]{:S(2)}) collective-permute-start(bf16[256,2048]{1,0:T(8,128)(2,1)} %get-tuple-element.518), channel_id=1, source_target_pairs={{8,0},{16,8},{24,16},{28,24},{20,28},{12,20},{4,12},{0,4},{9,1},{1... | collective-permute-start | bytes 3145736 | tf_op jit(solution)/shard_map/ppermute | solution.py:88
  524.3 43.3 %collective-permute-start.56 = (bf16[256,2048]{1,0:T(8,128)(2,1)S(1)}, bf16[256,2048]{1,0:T(8,128)(2,1)}, u32[]{:S(2)}, u32[]{:S(2)}) collective-permute-start(bf16[256,2048]{1,0:T(8,128)(2,1)S(1)} %get-tuple-element.325), channel_id=1, source_target_pairs={{0,8},{8,16},{16,24},{24,28},{28,20},{20,12},{12,4},{4,0},{1,9},{9... | collective-permute-start | bytes 3145736 | tf_op jit(solution)/shard_map/ppermute | solution.py:85
  525.8 43.0 %collective-permute-start.57 = (bf16[256,2048]{1,0:T(8,128)(2,1)}, bf16[256,2048]{1,0:T(8,128)(2,1)}, u32[]{:S(2)}, u32[]{:S(2)}) collective-permute-start(bf16[256,2048]{1,0:T(8,128)(2,1)} %get-tuple-element.326), channel_id=1, source_target_pairs={{8,0},{16,8},{24,16},{28,24},{20,28},{12,20},{4,12},{0,4},{9,1},{1... | collective-permute-start | bytes 3145736 | tf_op jit(solution)/shard_map/ppermute | solution.py:88
  536.9 31.8 %collective-permute-start.61 = (bf16[256,2048]{1,0:T(8,128)(2,1)S(1)}, bf16[256,2048]{1,0:T(8,128)(2,1)S(1)}, u32[]{:S(2)}, u32[]{:S(2)}) collective-permute-start(bf16[256,2048]{1,0:T(8,128)(2,1)S(1)} %fusion.24.refs_0_), channel_id=1, source_target_pairs={{0,2},{2,0},{1,3},{3,1},{4,6},{6,4},{5,7},{7,5},{8,10},{10,8},{9,1... | collective-permute-start | bytes 3145736 | tf_op jit(solution)/shard_map/ppermute | solution.py:67
  572.5 48.3 %collective-permute-start.63 = (bf16[512,2048]{1,0:T(8,128)(2,1)}, bf16[512,2048]{1,0:T(8,128)(2,1)}, u32[]{:S(2)}, u32[]{:S(2)}) collective-permute-start(bf16[512,2048]{1,0:T(8,128)(2,1)} %get-tuple-element.348), channel_id=1, source_target_pairs={{0,8},{8,16},{16,24},{24,28},{28,20},{20,12},{12,4},{4,0},{1,9},{9... | collective-permute-start | bytes 6291464 | tf_op jit(solution)/shard_map/ppermute | solution.py:85
  574.1 48.1 %collective-permute-start.64 = (bf16[512,2048]{1,0:T(8,128)(2,1)}, bf16[512,2048]{1,0:T(8,128)(2,1)}, u32[]{:S(2)}, u32[]{:S(2)}) collective-permute-start(bf16[512,2048]{1,0:T(8,128)(2,1)} %get-tuple-element.349), channel_id=1, source_target_pairs={{8,0},{16,8},{24,16},{28,24},{20,28},{12,20},{4,12},{0,4},{9,1},{1... | collective-permute-start | bytes 6291464 | tf_op jit(solution)/shard_map/ppermute | solution.py:88
  623.4 34.4 %collective-permute-start.71 = (bf16[8,64,640]{2,1,0:T(8,128)(2,1)S(1)}, bf16[8,64,640]{2,1,0:T(8,128)(2,1)S(1)}, u32[]{:S(2)}, u32[]{:S(2)}) collective-permute-start(bf16[8,64,640]{2,1,0:T(8,128)(2,1)S(1)} %dynamic-slice_bitcast_fusion.2), channel_id=1, source_target_pairs={{0,2},{2,0},{1,3},{3,1},{4,6},{6,4},{5,7},{7,5},{8,10},{10,8},{9,1... | collective-permute-start | bytes 1966088 | tf_op jit(solution)/shard_map/ppermute | solution.py:67
  629.8 48.2 %collective-permute-start.67 = (bf16[512,2048]{1,0:T(8,128)(2,1)}, bf16[512,2048]{1,0:T(8,128)(2,1)}, u32[]{:S(2)}, u32[]{:S(2)}) collective-permute-start(bf16[512,2048]{1,0:T(8,128)(2,1)} %get-tuple-element.366), channel_id=1, source_target_pairs={{0,8},{8,16},{16,24},{24,28},{28,20},{20,12},{12,4},{4,0},{1,9},{9... | collective-permute-start | bytes 6291464 | tf_op jit(solution)/shard_map/ppermute | solution.py:85
  631.2 47.9 %collective-permute-start.68 = (bf16[512,2048]{1,0:T(8,128)(2,1)}, bf16[512,2048]{1,0:T(8,128)(2,1)}, u32[]{:S(2)}, u32[]{:S(2)}) collective-permute-start(bf16[512,2048]{1,0:T(8,128)(2,1)} %get-tuple-element.367), channel_id=1, source_target_pairs={{8,0},{16,8},{24,16},{28,24},{20,28},{12,20},{4,12},{0,4},{9,1},{1... | collective-permute-start | bytes 6291464 | tf_op jit(solution)/shard_map/ppermute | solution.py:88
  686.2 57.1 %collective-permute-start.72 = (bf16[512,2048]{1,0:T(8,128)(2,1)}, bf16[512,2048]{1,0:T(8,128)(2,1)}, u32[]{:S(2)}, u32[]{:S(2)}) collective-permute-start(bf16[512,2048]{1,0:T(8,128)(2,1)} %get-tuple-element.384), channel_id=1, source_target_pairs={{0,8},{8,16},{16,24},{24,28},{28,20},{20,12},{12,4},{4,0},{1,9},{9... | collective-permute-start | bytes 6291464 | tf_op jit(solution)/shard_map/ppermute | solution.py:85
  687.6 55.8 %collective-permute-start.73 = (bf16[512,2048]{1,0:T(8,128)(2,1)S(1)}, bf16[512,2048]{1,0:T(8,128)(2,1)}, u32[]{:S(2)}, u32[]{:S(2)}) collective-permute-start(bf16[512,2048]{1,0:T(8,128)(2,1)S(1)} %get-tuple-element.385), channel_id=1, source_target_pairs={{8,0},{16,8},{24,16},{28,24},{20,28},{12,20},{4,12},{0,4},{9,1},{1... | collective-permute-start | bytes 6291464 | tf_op jit(solution)/shard_map/ppermute | solution.py:88
  693.4 50.0 %collective-permute-start.75 = (bf16[368,512]{1,0:T(8,128)(2,1)S(1)}, bf16[368,512]{1,0:T(8,128)(2,1)S(1)}, u32[]{:S(2)}, u32[]{:S(2)}) collective-permute-start(bf16[368,512]{1,0:T(8,128)(2,1)S(1)} %constant_dynamic-slice_fusion.9), channel_id=1, source_target_pairs={{8,0},{16,8},{24,16},{28,24},{20,28},{12,20},{4,12},{0,4},{9,1},{1... | collective-permute-start | bytes 1130504 | tf_op jit(solution)/shard_map/ppermute | solution.py:88
  695.8 47.6 %collective-permute-start.74 = (bf16[352,512]{1,0:T(8,128)(2,1)}, bf16[352,512]{1,0:T(8,128)(2,1)S(1)}, u32[]{:S(2)}, u32[]{:S(2)}) collective-permute-start(bf16[352,512]{1,0:T(8,128)(2,1)} %constant_dynamic-slice_fusion), channel_id=1, source_target_pairs={{0,8},{8,16},{16,24},{24,28},{28,20},{20,12},{12,4},{4,0},{1,9},{9... | collective-permute-start | bytes 1081352 | tf_op jit(solution)/shard_map/ppermute | solution.py:85
  (195 other events, 2203.7 us)
